TPU v7x, 32 devices: a whole 2x2x4 slice. The times are simulated.
32 devices in a mesh: dp: 4 (over y, x), fsdp: 8 (over z, core).
Axes of the slice: x: 2, y: 2, z: 4, core: 2. Of those that a mesh axis runs over, the one named last changes fastest.
Arguments:
- spectra: bfloat16 [32, 80, 128], P(('dp', 'fsdp')), may hold values from -6 to 6
- gaussian: bfloat16 [32, 80, 128], P(('dp', 'fsdp')), may hold values from -6 to 6
- flow_times: float32 [32], P(('dp', 'fsdp')), may hold values from 0 to 1
- lengths: int32 [32], P(('dp', 'fsdp')), may hold values from 32 to 128, as said below
- span_flags: int32 [32, 128], P(('dp', 'fsdp')), may hold values from 0 to 1, as said below
- phone_ids: int32 [32, 128], P(('dp', 'fsdp')), may hold values from 0 to 95
- input_master: float32 [256, 1024], P(None, ('dp', 'fsdp')), may hold values from -0.625 to 0.625
- input_moment: float32 [256, 1024], P(None, ('dp', 'fsdp')), may hold values from -2.2888184e-05 to 2.2888184e-05
- input_square: float32 [256, 1024], P(None, ('dp', 'fsdp')), may hold values from 3.542059e-11 to 5.6672944e-10
- kernel_master: float32 [31, 1024, 64], P(None, ('dp', 'fsdp')), may hold values from -0.125 to 0.125
- kernel_moment: float32 [31, 1024, 64], P(None, ('dp', 'fsdp')), may hold values from -2.2888184e-05 to 2.2888184e-05
- kernel_square: float32 [31, 1024, 64], P(None, ('dp', 'fsdp')), may hold values from 3.542059e-11 to 5.6672944e-10
- joint_master: float32 [2, 1024, 3072], P(None, ('dp', 'fsdp')), may hold values from -0.1875 to 0.1875
- joint_moment: float32 [2, 1024, 3072], P(None, ('dp', 'fsdp')), may hold values from -2.2888184e-05 to 2.2888184e-05
- joint_square: float32 [2, 1024, 3072], P(None, ('dp', 'fsdp')), may hold values from 3.542059e-11 to 5.6672944e-10
- output_master: float32 [2, 1024, 1024], P(None, ('dp', 'fsdp')), may hold values from -0.5 to 0.5
- output_moment: float32 [2, 1024, 1024], P(None, ('dp', 'fsdp')), may hold values from -2.2888184e-05 to 2.2888184e-05
- output_square: float32 [2, 1024, 1024], P(None, ('dp', 'fsdp')), may hold values from 3.542059e-11 to 5.6672944e-10
- expand_master: float32 [2, 1024, 4096], P(None, ('dp', 'fsdp')), may hold values from -0.1875 to 0.1875
- expand_moment: float32 [2, 1024, 4096], P(None, ('dp', 'fsdp')), may hold values from -2.2888184e-05 to 2.2888184e-05
- expand_square: float32 [2, 1024, 4096], P(None, ('dp', 'fsdp')), may hold values from 3.542059e-11 to 5.6672944e-10
- reduce_master: float32 [2, 4096, 1024], P(None, ('dp', 'fsdp')), may hold values from -0.09375 to 0.09375
- reduce_moment: float32 [2, 4096, 1024], P(None, ('dp', 'fsdp')), may hold values from -2.2888184e-05 to 2.2888184e-05
- reduce_square: float32 [2, 4096, 1024], P(None, ('dp', 'fsdp')), may hold values from 3.542059e-11 to 5.6672944e-10
- bridge_master: float32 [2048, 1024], P(('dp', 'fsdp')), may hold values from -0.125 to 0.125
- bridge_moment: float32 [2048, 1024], P(('dp', 'fsdp')), may hold values from -2.2888184e-05 to 2.2888184e-05
- bridge_square: float32 [2048, 1024], P(('dp', 'fsdp')), may hold values from 3.542059e-11 to 5.6672944e-10
- readout_master: float32 [1024, 80], P(('dp', 'fsdp')), may hold values from -0.1875 to 0.1875
- readout_moment: float32 [1024, 80], P(('dp', 'fsdp')), may hold values from -2.2888184e-05 to 2.2888184e-05
- readout_square: float32 [1024, 80], P(('dp', 'fsdp')), may hold values from 3.542059e-11 to 5.6672944e-10
- gains_master: float32 [5, 1024], P(None, ('dp', 'fsdp')), may hold values from 0.3 to 2.5
- gains_moment: float32 [5, 1024], P(None, ('dp', 'fsdp')), may hold values from -0.00048828125 to 0.00048828125
- gains_square: float32 [5, 1024], P(None, ('dp', 'fsdp')), may hold values from 3.3733893e-09 to 2.0240336e-08
Outputs:
- loss_sum: float32 [], replicated
- frame_total: float32 [], replicated
- grad_norm: float32 [], replicated
- input_first: float32 [256, 1024], P(None, ('dp', 'fsdp'))
- input_second: float32 [256, 1024], P(None, ('dp', 'fsdp'))
- input_updated: float32 [256, 1024], P(None, ('dp', 'fsdp'))
- kernel_first: float32 [31, 1024, 64], P(None, ('dp', 'fsdp'))
- kernel_second: float32 [31, 1024, 64], P(None, ('dp', 'fsdp'))
- kernel_updated: float32 [31, 1024, 64], P(None, ('dp', 'fsdp'))
- joint_first: float32 [2, 1024, 3072], P(None, ('dp', 'fsdp'))
- joint_second: float32 [2, 1024, 3072], P(None, ('dp', 'fsdp'))
- joint_updated: float32 [2, 1024, 3072], P(None, ('dp', 'fsdp'))
- output_first: float32 [2, 1024, 1024], P(None, ('dp', 'fsdp'))
- output_second: float32 [2, 1024, 1024], P(None, ('dp', 'fsdp'))
- output_updated: float32 [2, 1024, 1024], P(None, ('dp', 'fsdp'))
- expand_first: float32 [2, 1024, 4096], P(None, ('dp', 'fsdp'))
- expand_second: float32 [2, 1024, 4096], P(None, ('dp', 'fsdp'))
- expand_updated: float32 [2, 1024, 4096], P(None, ('dp', 'fsdp'))
- reduce_first: float32 [2, 4096, 1024], P(None, ('dp', 'fsdp'))
- reduce_second: float32 [2, 4096, 1024], P(None, ('dp', 'fsdp'))
- reduce_updated: float32 [2, 4096, 1024], P(None, ('dp', 'fsdp'))
- bridge_first: float32 [2048, 1024], P(('dp', 'fsdp'))
- bridge_second: float32 [2048, 1024], P(('dp', 'fsdp'))
- bridge_updated: float32 [2048, 1024], P(('dp', 'fsdp'))
- readout_first: float32 [1024, 80], P(('dp', 'fsdp'))
- readout_second: float32 [1024, 80], P(('dp', 'fsdp'))
- readout_updated: float32 [1024, 80], P(('dp', 'fsdp'))
- gains_first: float32 [5, 1024], P(None, ('dp', 'fsdp'))
- gains_second: float32 [5, 1024], P(None, ('dp', 'fsdp'))
- gains_updated: float32 [5, 1024], P(None, ('dp', 'fsdp'))
Inputs may be any that keep to these rules, and one draw needn't show every extreme that they name: `lengths`: frames of each utterance; some utterance is 128 frames long. `span_flags`: within each utterance one run of frames inside its length, covering at least seven tenths of it, rounded down, is 1; everything else is 0.
All inputs are finite; a program needn't handle non-finite values.
Results may differ from a plain program's by a relative error of at most 0.017.
Values may be sent and summed in bfloat16 or wider, within the bound.
No kernel may reach another device: no remote copies, remote signals or barrier semaphores. Data moves between devices by JAX's collectives and lax.ppermute only.
A program may use at most 448 MiB of HBM per device.

v0:
```python
import jax
import jax.numpy as jnp
from jax import lax
from jax.sharding import PartitionSpec as P

D = 1024
HEADS = 16
FF = 4096
MEL = 80
VOCAB = 96
KS = 31
GROUPS = 16
STEP = 10


SIGMA_MIN = 1e-05
NORM_EPS = 1e-05
MASKED = -1e30
BETA_ONE = 0.9
BETA_TWO = 0.95
ADAM_EPS = 1e-08
DECAY_RATE = 0.01
CLIP_LIMIT = 0.2
RATE_SCALE = 0.5
GAIN_RATE = 0.25


def layer_norm(values, gain_row):
    center = values - jnp.mean(values, -1, keepdims=True)
    spread = jnp.mean(center * center, -1, keepdims=True)
    return center * lax.rsqrt(spread + NORM_EPS) * gain_row


def alibi_bias(frames):
    slopes = 2.0 ** (-8.0 * (jnp.arange(HEADS, dtype=jnp.float32) + 1.0) / HEADS)
    places = jnp.arange(frames, dtype=jnp.float32)
    return -slopes[:, None, None] * jnp.abs(places[:, None] - places[None, :])


def conv_mix(hidden, kernel):
    tap_count = kernel.shape[0]
    margin = tap_count // 2
    seq_count, frame_count, model_width = hidden.shape
    per_group = model_width // GROUPS
    padded = jnp.pad(hidden, ((0, 0), (margin, margin), (0, 0)))
    stacked = jnp.stack([padded[:, tap : tap + frame_count] for tap in range(tap_count)], 1)
    stacked = stacked.reshape(seq_count, tap_count, frame_count, GROUPS, per_group)
    weights = kernel.reshape(tap_count, GROUPS, per_group, per_group)
    mixed = jnp.einsum("bklgc,kgoc->blgo", stacked, weights)
    return mixed.reshape(seq_count, frame_count, model_width)


def score_block(query, keyed, valid, alibi):
    scale = query.shape[-1] ** (-0.5)
    scores = (
        jnp.einsum("sqhd,skhd->shqk", query, keyed, preferred_element_type=jnp.float32) * scale
        + alibi[None]
    )
    return jnp.where(valid[:, None, None, :], scores, MASKED)


def layer_forward(stream, mats, gain_one, gain_two, valid, alibi):
    joint_w, output_w, expand_w, reduce_w = mats
    seq_count, frame_count, model_width = stream.shape
    row_count = seq_count * frame_count
    normed = layer_norm(stream, gain_one).astype(jnp.bfloat16).reshape(row_count, model_width)
    joint = jnp.dot(normed, joint_w, preferred_element_type=jnp.float32).astype(jnp.bfloat16)
    joint = joint.reshape(seq_count, frame_count, 3, HEADS, model_width // HEADS)
    scores = score_block(joint[:, :, 0], joint[:, :, 1], valid, alibi)
    highest = jnp.max(scores, -1, keepdims=True)
    raised = jnp.exp(scores - highest)
    totals = jnp.sum(raised, -1, keepdims=True)
    probs = raised / totals
    log_total = highest + jnp.log(totals)
    context = jnp.einsum(
        "shqk,skhd->sqhd",
        probs.astype(jnp.bfloat16),
        joint[:, :, 2],
        preferred_element_type=jnp.float32,
    )
    context = context.astype(jnp.bfloat16).reshape(row_count, model_width)
    middle = stream + jnp.dot(context, output_w, preferred_element_type=jnp.float32).reshape(
        stream.shape
    )
    normed_two = layer_norm(middle, gain_two).astype(jnp.bfloat16).reshape(row_count, model_width)
    upper = jnp.dot(normed_two, expand_w, preferred_element_type=jnp.float32)
    hidden = jax.nn.gelu(upper).astype(jnp.bfloat16)
    result = middle + jnp.dot(hidden, reduce_w, preferred_element_type=jnp.float32).reshape(
        stream.shape
    )
    return (result, (stream, normed, joint, log_total, context, middle, normed_two, upper, hidden))


def layer_backward(incoming, kept, mats, gain_one, gain_two, valid, alibi):
    stream, normed, joint, log_total, context, middle, normed_two, upper, hidden = kept
    joint_w, output_w, expand_w, reduce_w = mats
    seq_count, frame_count, model_width = stream.shape
    row_count = seq_count * frame_count
    incoming_low = incoming.reshape(row_count, model_width).astype(jnp.bfloat16)
    d_reduce = jnp.dot(hidden.T, incoming_low, preferred_element_type=jnp.float32)
    d_hidden = jnp.dot(incoming_low, reduce_w.T, preferred_element_type=jnp.float32)
    gelu_pull = jax.vjp(jax.nn.gelu, upper)[1]
    d_upper = gelu_pull(d_hidden)[0].astype(jnp.bfloat16)
    d_expand = jnp.dot(normed_two.T, d_upper, preferred_element_type=jnp.float32)
    d_normed = jnp.dot(d_upper, expand_w.T, preferred_element_type=jnp.float32).reshape(
        stream.shape
    )
    norm_pull = jax.vjp(layer_norm, middle, gain_two)[1]
    d_middle, d_gain_two = norm_pull(d_normed)
    d_middle = d_middle + incoming
    d_middle_low = d_middle.reshape(row_count, model_width).astype(jnp.bfloat16)
    d_output = jnp.dot(context.T, d_middle_low, preferred_element_type=jnp.float32)
    d_context = jnp.dot(d_middle_low, output_w.T, preferred_element_type=jnp.float32).astype(
        jnp.bfloat16
    )
    d_context = d_context.reshape(seq_count, frame_count, HEADS, model_width // HEADS)
    query, keyed, valued = (joint[:, :, 0], joint[:, :, 1], joint[:, :, 2])
    probs = jnp.exp(score_block(query, keyed, valid, alibi) - log_total)
    d_probs = jnp.einsum("sqhd,skhd->shqk", d_context, valued, preferred_element_type=jnp.float32)
    d_valued = jnp.einsum(
        "shqk,sqhd->skhd", probs.astype(jnp.bfloat16), d_context, preferred_element_type=jnp.float32
    )
    inner = jnp.sum(probs * d_probs, -1, keepdims=True)
    d_scores = (probs * (d_probs - inner)).astype(jnp.bfloat16)
    scale = query.shape[-1] ** (-0.5)
    d_query = (
        jnp.einsum("shqk,skhd->sqhd", d_scores, keyed, preferred_element_type=jnp.float32) * scale
    )
    d_keyed = (
        jnp.einsum("shqk,sqhd->skhd", d_scores, query, preferred_element_type=jnp.float32) * scale
    )
    d_joint = (
        jnp.stack([d_query, d_keyed, d_valued], 2)
        .astype(jnp.bfloat16)
        .reshape(row_count, 3 * model_width)
    )
    d_joint_w = jnp.dot(normed.T, d_joint, preferred_element_type=jnp.float32)
    d_normed = jnp.dot(d_joint, joint_w.T, preferred_element_type=jnp.float32).reshape(stream.shape)
    norm_pull = jax.vjp(layer_norm, stream, gain_one)[1]
    d_stream, d_gain_one = norm_pull(d_normed)
    return (d_stream + d_middle, (d_joint_w, d_output, d_expand, d_reduce), d_gain_one, d_gain_two)


def adamw(master, moment, square, grad, rate, decay):
    moment = BETA_ONE * moment + (1.0 - BETA_ONE) * grad
    square = BETA_TWO * square + (1.0 - BETA_TWO) * grad * grad
    fixed_moment = moment / (1.0 - BETA_ONE**STEP)
    fixed_square = square / (1.0 - BETA_TWO**STEP)
    return (
        moment,
        square,
        master - rate * (fixed_moment / (jnp.sqrt(fixed_square) + ADAM_EPS) + decay * master),
    )


def weight_rates():
    fan_ins = (MEL, KS * (D // GROUPS), D, D // 8, D, FF, 2 * D, D)
    return [RATE_SCALE * fan_in ** (-0.5) for fan_in in fan_ins] + [GAIN_RATE]


def shards(
    spectra,
    gaussian,
    flow_times,
    lengths,
    span_flags,
    phone_ids,
    input_master,
    input_moment,
    input_square,
    kernel_master,
    kernel_moment,
    kernel_square,
    joint_master,
    joint_moment,
    joint_square,
    output_master,
    output_moment,
    output_square,
    expand_master,
    expand_moment,
    expand_square,
    reduce_master,
    reduce_moment,
    reduce_square,
    bridge_master,
    bridge_moment,
    bridge_square,
    readout_master,
    readout_moment,
    readout_square,
    gains_master,
    gains_moment,
    gains_square,
):
    low_type = jnp.bfloat16
    wide_dtype = jnp.float32
    input_wide, kernel_full, bridge_full, readout_full, gains_full = (
        lax.all_gather(input_master.astype(low_type), ("dp", "fsdp"), axis=1, tiled=True),
        lax.all_gather(kernel_master.astype(low_type), ("dp", "fsdp"), axis=1, tiled=True),
        lax.all_gather(bridge_master.astype(low_type), ("dp", "fsdp"), axis=0, tiled=True),
        lax.all_gather(readout_master.astype(low_type), ("dp", "fsdp"), axis=0, tiled=True),
        lax.all_gather(gains_master.astype(low_type), ("dp", "fsdp"), axis=1, tiled=True),
    )
    gains_full = gains_full.astype(wide_dtype)

    def fetch(layer_index):
        return (
            lax.all_gather(
                joint_master[layer_index].astype(low_type), ("dp", "fsdp"), axis=0, tiled=True
            ),
            lax.all_gather(
                output_master[layer_index].astype(low_type), ("dp", "fsdp"), axis=0, tiled=True
            ),
            lax.all_gather(
                expand_master[layer_index].astype(low_type), ("dp", "fsdp"), axis=0, tiled=True
            ),
            lax.all_gather(
                reduce_master[layer_index].astype(low_type), ("dp", "fsdp"), axis=0, tiled=True
            ),
        )

    def share(grads):
        return (
            lax.psum_scatter(grads[0], ("dp", "fsdp"), scatter_dimension=0, tiled=True),
            lax.psum_scatter(grads[1], ("dp", "fsdp"), scatter_dimension=0, tiled=True),
            lax.psum_scatter(grads[2], ("dp", "fsdp"), scatter_dimension=0, tiled=True),
            lax.psum_scatter(grads[3], ("dp", "fsdp"), scatter_dimension=0, tiled=True),
        )

    seq_count, mel_count, frame_count = spectra.shape
    row_count = seq_count * frame_count
    valid = jnp.arange(frame_count)[None, :] < lengths[:, None]
    valid_float = valid.astype(wide_dtype)
    flags = span_flags.astype(wide_dtype)
    clean = spectra.astype(wide_dtype)
    noise_full = gaussian.astype(wide_dtype)
    scaled = flow_times[:, None, None]
    noisy = (1.0 - (1.0 - SIGMA_MIN) * scaled) * noise_full + scaled * clean
    context = clean * (1.0 - flags[:, None, :])
    onehot = (phone_ids[:, None, :] == jnp.arange(VOCAB)[None, :, None]).astype(low_type)
    feature_rows = jnp.concatenate([noisy.astype(low_type), context.astype(low_type), onehot], 1)
    initial_state = (
        jnp.einsum("nzv,zr->nvr", feature_rows, input_wide, preferred_element_type=wide_dtype)
        * valid_float[:, :, None]
    )
    conv_out, conv_pull = jax.vjp(
        conv_mix, initial_state.astype(low_type).astype(wide_dtype), kernel_full.astype(wide_dtype)
    )
    embedded = initial_state + jax.nn.gelu(conv_out)
    alibi = alibi_bias(frame_count)
    mats_zero = fetch(0)
    encoded, kept_zero = layer_forward(
        embedded, mats_zero, gains_full[0], gains_full[1], valid, alibi
    )
    model_width = encoded.shape[-1]
    joined = (
        jnp.concatenate([encoded, embedded], -1)
        .astype(low_type)
        .reshape(row_count, 2 * model_width)
    )
    bridged = jnp.dot(joined, bridge_full, preferred_element_type=wide_dtype).reshape(encoded.shape)
    mats_one = fetch(1)
    decoded, kept_one = layer_forward(bridged, mats_one, gains_full[2], gains_full[3], valid, alibi)
    final_low = layer_norm(decoded, gains_full[4]).astype(low_type).reshape(row_count, model_width)
    predict = jnp.dot(final_low, readout_full, preferred_element_type=wide_dtype)
    target = jnp.swapaxes(clean - (1.0 - SIGMA_MIN) * noise_full, 1, 2).reshape(
        row_count, mel_count
    )
    weight = (flags * valid_float).reshape(row_count, 1)
    missed = predict - target
    loss_local = jnp.sum(weight * missed * missed)
    count_local = jnp.sum(weight)
    loss_sum, frame_total = lax.psum((loss_local, count_local), ("dp", "fsdp"))
    d_predict = (2.0 * weight * missed).astype(low_type)
    d_readout = jnp.dot(final_low.T, d_predict, preferred_element_type=wide_dtype)
    d_final = jnp.dot(d_predict, readout_full.T, preferred_element_type=wide_dtype).reshape(
        decoded.shape
    )
    final_pull = jax.vjp(layer_norm, decoded, gains_full[4])[1]
    d_decoded, d_gain_last = final_pull(d_final)
    mats_back = mats_one
    d_bridged, grads_one, d_gain_two, d_gain_three = layer_backward(
        d_decoded, kept_one, mats_back, gains_full[2], gains_full[3], valid, alibi
    )
    shard_one = share(grads_one)
    d_bridged_low = d_bridged.reshape(row_count, model_width).astype(low_type)
    d_bridge = jnp.dot(joined.T, d_bridged_low, preferred_element_type=wide_dtype)
    d_joined = jnp.dot(d_bridged_low, bridge_full.T, preferred_element_type=wide_dtype).reshape(
        seq_count, frame_count, 2 * model_width
    )
    mats_back = mats_zero
    d_embedded, grads_zero, d_gain_zero, d_gain_one = layer_backward(
        d_joined[:, :, :model_width],
        kept_zero,
        mats_back,
        gains_full[0],
        gains_full[1],
        valid,
        alibi,
    )
    shard_zero = share(grads_zero)
    d_embedded = d_embedded + d_joined[:, :, model_width:]
    gelu_pull = jax.vjp(jax.nn.gelu, conv_out)[1]
    d_conv = gelu_pull(d_embedded)[0].astype(low_type).astype(wide_dtype)
    d_conv_in, d_kernel = conv_pull(d_conv)
    initial_gradient = ((d_embedded + d_conv_in) * valid_float[:, :, None]).astype(low_type)
    input_gradient = jnp.einsum(
        "fpk,fkq->pq", feature_rows, initial_gradient, preferred_element_type=wide_dtype
    )
    d_gains = jnp.stack([d_gain_zero, d_gain_one, d_gain_two, d_gain_three, d_gain_last])
    edge_input, edge_kernel, edge_bridge, edge_readout, edge_gains = (
        lax.psum_scatter(input_gradient, ("dp", "fsdp"), scatter_dimension=1, tiled=True),
        lax.psum_scatter(d_kernel, ("dp", "fsdp"), scatter_dimension=1, tiled=True),
        lax.psum_scatter(d_bridge, ("dp", "fsdp"), scatter_dimension=0, tiled=True),
        lax.psum_scatter(d_readout, ("dp", "fsdp"), scatter_dimension=0, tiled=True),
        lax.psum_scatter(d_gains, ("dp", "fsdp"), scatter_dimension=1, tiled=True),
    )
    layer_shards = [
        jnp.stack([zero_part, one_part]) for zero_part, one_part in zip(shard_zero, shard_one)
    ]
    grads = [edge_input, edge_kernel] + layer_shards + [edge_bridge, edge_readout, edge_gains]
    squares_local = sum((jnp.sum(item * item) for item in grads))
    squared = lax.psum(squares_local, ("dp", "fsdp"))
    grad_norm = jnp.sqrt(squared) / frame_total
    factor = jnp.minimum(1.0, CLIP_LIMIT / grad_norm) / frame_total
    masters = (
        input_master,
        kernel_master,
        joint_master,
        output_master,
        expand_master,
        reduce_master,
        bridge_master,
        readout_master,
        gains_master,
    )
    moments = (
        input_moment,
        kernel_moment,
        joint_moment,
        output_moment,
        expand_moment,
        reduce_moment,
        bridge_moment,
        readout_moment,
        gains_moment,
    )
    squares = (
        input_square,
        kernel_square,
        joint_square,
        output_square,
        expand_square,
        reduce_square,
        bridge_square,
        readout_square,
        gains_square,
    )
    decays = [DECAY_RATE] * 8 + [0.0]
    results = []
    for master, moment, square, grad, rate, decay in zip(
        masters, moments, squares, grads, weight_rates(), decays
    ):
        results.extend(adamw(master, moment, square, factor * grad, rate, decay))
    return (loss_sum, frame_total, grad_norm, *results)


def solution(mesh):
    in_specs = (
        P(("dp", "fsdp"), None, None),
        P(("dp", "fsdp"), None, None),
        P(("dp", "fsdp")),
        P(("dp", "fsdp")),
        P(("dp", "fsdp"), None),
        P(("dp", "fsdp"), None),
        P(None, ("dp", "fsdp")),
        P(None, ("dp", "fsdp")),
        P(None, ("dp", "fsdp")),
        P(None, ("dp", "fsdp"), None),
        P(None, ("dp", "fsdp"), None),
        P(None, ("dp", "fsdp"), None),
        P(None, ("dp", "fsdp"), None),
        P(None, ("dp", "fsdp"), None),
        P(None, ("dp", "fsdp"), None),
        P(None, ("dp", "fsdp"), None),
        P(None, ("dp", "fsdp"), None),
        P(None, ("dp", "fsdp"), None),
        P(None, ("dp", "fsdp"), None),
        P(None, ("dp", "fsdp"), None),
        P(None, ("dp", "fsdp"), None),
        P(None, ("dp", "fsdp"), None),
        P(None, ("dp", "fsdp"), None),
        P(None, ("dp", "fsdp"), None),
        P(("dp", "fsdp"), None),
        P(("dp", "fsdp"), None),
        P(("dp", "fsdp"), None),
        P(("dp", "fsdp"), None),
        P(("dp", "fsdp"), None),
        P(("dp", "fsdp"), None),
        P(None, ("dp", "fsdp")),
        P(None, ("dp", "fsdp")),
        P(None, ("dp", "fsdp")),
    )
    out_specs = (
        P(),
        P(),
        P(),
        P(None, ("dp", "fsdp")),
        P(None, ("dp", "fsdp")),
        P(None, ("dp", "fsdp")),
        P(None, ("dp", "fsdp"), None),
        P(None, ("dp", "fsdp"), None),
        P(None, ("dp", "fsdp"), None),
        P(None, ("dp", "fsdp"), None),
        P(None, ("dp", "fsdp"), None),
        P(None, ("dp", "fsdp"), None),
        P(None, ("dp", "fsdp"), None),
        P(None, ("dp", "fsdp"), None),
        P(None, ("dp", "fsdp"), None),
        P(None, ("dp", "fsdp"), None),
        P(None, ("dp", "fsdp"), None),
        P(None, ("dp", "fsdp"), None),
        P(None, ("dp", "fsdp"), None),
        P(None, ("dp", "fsdp"), None),
        P(None, ("dp", "fsdp"), None),
        P(("dp", "fsdp"), None),
        P(("dp", "fsdp"), None),
        P(("dp", "fsdp"), None),
        P(("dp", "fsdp"), None),
        P(("dp", "fsdp"), None),
        P(("dp", "fsdp"), None),
        P(None, ("dp", "fsdp")),
        P(None, ("dp", "fsdp")),
        P(None, ("dp", "fsdp")),
    )
    return jax.shard_map(shards, mesh=mesh, in_specs=in_specs, out_specs=out_specs, check_vma=False)
```

profile of v0, /device:TPU:0, one launch (start us, length us, event | category | flops | bytes accessed | tf_op | source)
XLA Modules:
  0.0 2958.4 jit_solution(989238661156456906)
XLA Ops:
  22.3 47.5 %all_gather.39 = bf16[256,1024]{0,1:T(8,128)(2,1)S(1)} all-gather(bf16[256,32]{0,1:T(8,128)(2,1)S(1)} %convert_element_type.250), channel_id=1, replica_groups=mesh['dp'=4,'fsdp'=8] {'dp','fsdp'}, dimensions={1}, use_global_device_ids=true | all-gather | bytes 540672 | tf_op jit(solution)/shard_map/all_gather | solution.py:199
  70.9 2.1 pad_slice_fusion
  114.1 37.1 %all-gather.8 = bf16[32,32,5]{1,2,0:T(8,128)(2,1)S(1)} all-gather(bf16[1,32,5]{1,2,0:T(8,128)(2,1)S(1)} %convert_bitcast_fusion), channel_id=1, replica_groups=mesh['dp'=4,'fsdp'=8] {'dp','fsdp'}, dimensions={0}, use_global_device_ids=true | all-gather | bytes 10560 | tf_op jit(solution)/shard_map/all_gather | solution.py:203
  151.3 39.8 %all_gather.51 = bf16[1024,80]{1,0:T(8,128)(2,1)S(1)} all-gather(bf16[32,80]{1,0:T(8,128)(2,1)S(1)} %convert_element_type.284), channel_id=1, replica_groups=mesh['dp'=4,'fsdp'=8] {'dp','fsdp'}, dimensions={0}, use_global_device_ids=true | all-gather | bytes 168960 | tf_op jit(solution)/shard_map/all_gather | solution.py:202
  236.1 12.1 copy.464
  248.2 8.0 fusion.2
  258.6 3.9 fusion.31
  264.8 2.2 fusion.204
  267.7 40.0 %all-gather.28.cloned.1.call-done = bf16[1,1024,4096]{2,1,0:T(8,128)(2,1)} async-done(((bf16[1,32,4096]{2,1,0:T(8,128)(2,1)}), bf16[1,1024,4096]{2,1,0:T(8,128)(2,1)}) %all-gather.28.cloned.1.call-update) | async-done | bytes 8388624 | tf_op jit(solution)/shard_map/all_gather | solution.py:215
  307.7 6.0 fusion.18
  313.7 72.7 %all-gather.30.cloned.1.call-done = bf16[1,4096,1024]{2,1,0:T(8,128)(2,1)} async-done(((bf16[1,128,1024]{2,1,0:T(8,128)(2,1)}), bf16[1,4096,1024]{2,1,0:T(8,128)(2,1)}) %all-gather.30.cloned.1.call-update) | async-done | bytes 8388624 | tf_op jit(solution)/shard_map/all_gather | solution.py:218
  386.4 5.6 fusion.77
  392.0 58.0 %all-gather.22.cloned.1.call-done = bf16[2048,1024]{1,0:T(8,128)(2,1)} async-done(((bf16[64,1024]{1,0:T(8,128)(2,1)}), bf16[2048,1024]{1,0:T(8,128)(2,1)}) %all-gather.22.cloned.1.call-update) | async-done | bytes 4194320 | tf_op jit(solution)/shard_map/all_gather | solution.py:201
  450.0 3.0 fusion.205
  453.3 67.8 %all-gather.32.cloned.1.call-done = bf16[1,1024,3072]{2,1,0:T(8,128)(2,1)} async-done(((bf16[1,32,3072]{2,1,0:T(8,128)(2,1)}), bf16[1,1024,3072]{2,1,0:T(8,128)(2,1)}) %all-gather.32.cloned.1.call-update) | async-done | bytes 6291472 | tf_op jit(solution)/shard_map/all_gather | solution.py:209
  521.0 4.7 fusion.34
  525.8 2.3 copy.448
  532.5 46.6 %all-gather.34.cloned.1.call-done = bf16[1,1024,1024]{2,1,0:T(8,128)(2,1)} async-done(((bf16[1,32,1024]{2,1,0:T(8,128)(2,1)}), bf16[1,1024,1024]{2,1,0:T(8,128)(2,1)}) %all-gather.34.cloned.1.call-update) | async-done | bytes 2097168 | tf_op jit(solution)/shard_map/all_gather | solution.py:212
  579.0 2.2 fusion.207
  582.0 76.3 %all-gather.36.cloned.1.call-done = bf16[1,1024,4096]{2,1,0:T(8,128)(2,1)} async-done(((bf16[1,32,4096]{2,1,0:T(8,128)(2,1)}), bf16[1,1024,4096]{2,1,0:T(8,128)(2,1)}) %all-gather.36.cloned.1.call-update) | async-done | bytes 8388624 | tf_op jit(solution)/shard_map/all_gather | solution.py:215
  658.3 6.2 fusion.10
  664.5 72.7 %all-gather.38.cloned.1.call-done = bf16[1,4096,1024]{2,1,0:T(8,128)(2,1)} async-done(((bf16[1,128,1024]{2,1,0:T(8,128)(2,1)}), bf16[1,4096,1024]{2,1,0:T(8,128)(2,1)}) %all-gather.38.cloned.1.call-update) | async-done | bytes 8388624 | tf_op jit(solution)/shard_map/all_gather | solution.py:218
  737.2 5.8 fusion.208
  745.5 3.6 fusion.50
  749.1 3.5 multiply_reduce_fusion.6
  763.1 6.4 multiply_reduce_fusion.7
  772.3 7.4 fusion.43
  779.8 3.5 multiply_reduce_fusion.8
  792.9 5.1 multiply_reduce_fusion.9
  800.4 2.4 fusion.109
  803.0 11.2 convolution_bitcast_fusion
  814.2 11.6 copy.465
  825.8 7.6 fusion.195
  834.7 5.5 fusion.196
  893.4 2.1 copy.549
  902.6 6.6 pad_add_fusion
  911.0 3.7 fusion.134
  914.8 3.6 fusion.142
  918.7 16.2 fusion.20
  934.9 17.4 copy.519
  953.5 6.6 fusion.174
  961.2 6.5 fusion.176
  968.8 4.6 fusion.127
  974.7 9.8 fusion.145
  985.5 9.9 fusion.173
  996.6 8.2 fusion.175
  1006.0 8.3 fusion.177
  1015.9 48.8 %reduce-scatter.38.cloned.1.call-done = f32[32,80]{1,0:T(8,128)} async-done(((f32[1024,80]{1,0:T(8,128)}), f32[32,80]{1,0:T(8,128)}) %reduce-scatter.38.cloned.1.call-update) | async-done | bytes 10256 | tf_op jit(solution)/shard_map/reduce_scatter | solution.py:316
  1066.1 132.7 %reduce-scatter.16.cloned.1.call-done = f32[256,32]{0,1:T(8,128)} async-done(((f32[256,1024]{0,1:T(8,128)}), f32[256,32]{0,1:T(8,128)}) %reduce-scatter.16.cloned.1.call-update) | async-done | bytes 32784 | tf_op jit(solution)/shard_map/reduce_scatter | solution.py:313
  1200.2 139.9 %reduce-scatter.24.cloned.1.call-done = f32[32,1024]{1,0:T(8,128)} async-done(((f32[1024,1024]{1,0:T(8,128)}), f32[32,1024]{1,0:T(8,128)}) %reduce-scatter.24.cloned.1.call-update) | async-done | bytes 131088 | tf_op jit(solution)/shard_map/reduce_scatter | solution.py:226
  1340.1 142.0 %reduce-scatter.26.cloned.1.call-done = f32[32,1024]{1,0:T(8,128)} async-done(((f32[1024,1024]{1,0:T(8,128)}), f32[32,1024]{1,0:T(8,128)}) %reduce-scatter.26.cloned.1.call-update) | async-done | bytes 131088 | tf_op jit(solution)/shard_map/reduce_scatter | solution.py:226
  1483.8 184.1 %reduce-scatter.18.cloned.1.call-done = f32[31,32,64]{2,0,1:T(8,128)} async-done(((f32[31,1024,64]{2,0,1:T(8,128)}), f32[31,32,64]{2,0,1:T(8,128)}) %reduce-scatter.18.cloned.1.call-update) | async-done | bytes 253968 | tf_op jit(solution)/shard_map/reduce_scatter | solution.py:314
  1670.9 157.0 %reduce-scatter.20.cloned.1.call-done = f32[32,3072]{1,0:T(8,128)} async-done(((f32[1024,3072]{1,0:T(8,128)}), f32[32,3072]{1,0:T(8,128)}) %reduce-scatter.20.cloned.1.call-update) | async-done | bytes 393232 | tf_op jit(solution)/shard_map/reduce_scatter | solution.py:225
  1827.9 160.3 %reduce-scatter.22.cloned.1.call-done = f32[32,3072]{1,0:T(8,128)} async-done(((f32[1024,3072]{1,0:T(8,128)}), f32[32,3072]{1,0:T(8,128)}) %reduce-scatter.22.cloned.1.call-update) | async-done | bytes 393232 | tf_op jit(solution)/shard_map/reduce_scatter | solution.py:225
  1991.4 150.2 %reduce-scatter.36.cloned.1.call-done = f32[64,1024]{1,0:T(8,128)} async-done(((f32[2048,1024]{1,0:T(8,128)}), f32[64,1024]{1,0:T(8,128)}) %reduce-scatter.36.cloned.1.call-update) | async-done | bytes 262160 | tf_op jit(solution)/shard_map/reduce_scatter | solution.py:315
  2143.2 185.2 %reduce-scatter.32.cloned.1.call-done = f32[128,1024]{1,0:T(8,128)} async-done(((f32[4096,1024]{1,0:T(8,128)}), f32[128,1024]{1,0:T(8,128)}) %reduce-scatter.32.cloned.1.call-update) | async-done | bytes 524304 | tf_op jit(solution)/shard_map/reduce_scatter | solution.py:228
  2328.4 186.8 %reduce-scatter.34.cloned.1.call-done = f32[128,1024]{1,0:T(8,128)} async-done(((f32[4096,1024]{1,0:T(8,128)}), f32[128,1024]{1,0:T(8,128)}) %reduce-scatter.34.cloned.1.call-update) | async-done | bytes 524304 | tf_op jit(solution)/shard_map/reduce_scatter | solution.py:228
  2515.2 2.1 multiply_reduce_fusion
  2517.4 184.7 %reduce-scatter.28.cloned.1.call-done = f32[32,4096]{1,0:T(8,128)} async-done(((f32[1024,4096]{1,0:T(8,128)}), f32[32,4096]{1,0:T(8,128)}) %reduce-scatter.28.cloned.1.call-update) | async-done | bytes 524304 | tf_op jit(solution)/shard_map/reduce_scatter | solution.py:227
  2702.0 186.8 %reduce-scatter.30.cloned.1.call-done = f32[32,4096]{1,0:T(8,128)} async-done(((f32[1024,4096]{1,0:T(8,128)}), f32[32,4096]{1,0:T(8,128)}) %reduce-scatter.30.cloned.1.call-update) | async-done | bytes 524304 | tf_op jit(solution)/shard_map/reduce_scatter | solution.py:227
  2894.2 37.2 %all-reduce.32 = (f32[]{:T(128)}, f32[]{:T(128)}, f32[]{:T(128)}) all-reduce(f32[]{:T(128)} %get-tuple-element.269, f32[]{:T(128)} %get-tuple-element.254, f32[]{:T(128)S(6)} %add.485), channel_id=1, replica_groups=mesh['dp'=4,'fsdp'=8] {'dp','fsdp'}, use_global_device_ids=true, to_apply=%region_15.16 | all-reduce | flops 3 | bytes 24 | tf_op jit(solution)/shard_map/psum | solution.py:274
  2934.2 2.5 multiply_subtract_fusion.3
  2940.7 2.2 multiply_subtract_fusion
  2943.1 2.2 multiply_subtract_fusion.1
  (534 shorter events, 232.7 us)
Async XLA Ops:
  7.2 9.0 copy-start.55
  7.2 13.8 copy-start.73
  7.2 13.9 copy-start.126
  7.2 15.0 copy-start.125
  7.3 15.0 copy-start.78
  7.3 15.0 copy-start.76
  7.3 228.8 %all-gather.20.cloned.1.call-start = ((), (), s32[]{:S(2)}) async-start(), calls=%async_computation.13 | async-start | bytes 8380416 | tf_op jit(solution)/shard_map/all_gather | solution.py:200
  9.2 249.4 %all-gather.24.cloned.1.call-start = ((), (), s32[]{:S(2)}) async-start(), calls=%async_computation.27 | async-start | bytes 6488064 | tf_op jit(solution)/shard_map/all_gather | solution.py:209
  11.2 253.5 %all-gather.26.cloned.1.call-start = ((), (), s32[]{:S(2)}) async-start(), calls=%async_computation.28 | async-start | bytes 2162688 | tf_op jit(solution)/shard_map/all_gather | solution.py:212
  12.9 294.8 %all-gather.28.cloned.1.call-start = ((), (), s32[]{:S(2)}) async-start(), calls=%async_computation.29 | async-start | bytes 8650752 | tf_op jit(solution)/shard_map/all_gather | solution.py:215
  15.2 371.3 %all-gather.30.cloned.1.call-start = ((), (), s32[]{:S(2)}) async-start(), calls=%async_computation.30 | async-start | bytes 8650752 | tf_op jit(solution)/shard_map/all_gather | solution.py:218
  16.1 433.9 %all-gather.22.cloned.1.call-start = ((), (), s32[]{:S(2)}) async-start(), calls=%async_computation.14 | async-start | bytes 4325376 | tf_op jit(solution)/shard_map/all_gather | solution.py:201
  16.9 504.2 %all-gather.32.cloned.1.call-start = ((), (), s32[]{:S(2)}) async-start(), calls=%async_computation.31 | async-start | bytes 6488064 | tf_op jit(solution)/shard_map/all_gather | solution.py:209
  17.6 561.4 %all-gather.34.cloned.1.call-start = ((), (), s32[]{:S(2)}) async-start(), calls=%async_computation.32 | async-start | bytes 2162688 | tf_op jit(solution)/shard_map/all_gather | solution.py:212
  18.4 639.9 %all-gather.36.cloned.1.call-start = ((), (), s32[]{:S(2)}) async-start(), calls=%async_computation.33 | async-start | bytes 8650752 | tf_op jit(solution)/shard_map/all_gather | solution.py:215
  19.1 718.0 %all-gather.38.cloned.1.call-start = ((), (), s32[]{:S(2)}) async-start(), calls=%async_computation.34 | async-start | bytes 8650752 | tf_op jit(solution)/shard_map/all_gather | solution.py:218
  19.7 994.7 %reduce-scatter.40.cloned.1.call-start = ((), (), s32[]{:S(2)}) async-start(), calls=%async_computation.35 | async-start | bytes 540672
  21.1 51.9 %copy-start.116 = (f32[128]{0:T(128)}, f32[128]{0:T(128)S(1)}, u32[]{:S(2)}) copy-start(f32[128]{0:T(128)S(1)} %fusion.170) | copy-start | bytes 1540
  75.3 28.8 copy-start.50
  86.1 27.9 copy-start.103
  87.9 63.3 %copy-start.80 = (f32[32,80]{1,0:T(8,128)S(1)}, f32[32,80]{1,0:T(8,128)}, u32[]{:S(2)}) copy-start(f32[32,80]{1,0:T(8,128)} %param.60) | copy-start | bytes 30724
  113.7 114.2 %copy-start.53 = (bf16[1,128,1024]{1,2,0:T(8,128)(2,1)S(1)}, bf16[1,128,1024]{1,2,0:T(8,128)(2,1)}, u32[]{:S(2)}) copy-start(bf16[1,128,1024]{1,2,0:T(8,128)(2,1)} %copy.397) | copy-start | bytes 786436
  113.9 114.8 %copy-start.52 = (bf16[1,128,1024]{1,2,0:T(8,128)(2,1)S(1)}, bf16[1,128,1024]{1,2,0:T(8,128)(2,1)}, u32[]{:S(2)}) copy-start(bf16[1,128,1024]{1,2,0:T(8,128)(2,1)} %copy.398) | copy-start | bytes 786436
  151.1 78.3 %copy-start.51 = (bf16[1,128,1024]{1,2,0:T(8,128)(2,1)S(1)}, bf16[1,128,1024]{1,2,0:T(8,128)(2,1)}, u32[]{:S(2)}) copy-start(bf16[1,128,1024]{1,2,0:T(8,128)(2,1)} %copy.399) | copy-start | bytes 786436
  264.7 49.0 %copy-start.49 = (bf16[16,64,128]{2,1,0:T(8,128)(2,1)}, bf16[16,64,128]{2,1,0:T(8,128)(2,1)S(1)}, u32[]{:S(2)}) copy-start(bf16[16,64,128]{2,1,0:T(8,128)(2,1)S(1)} %convolution_convert_fusion.3) | copy-start | bytes 786436
  267.7 46.0 %copy-start.89 = (f32[128]{0:T(128)}, f32[128]{0:T(128)S(1)}, u32[]{:S(2)}) copy-start(f32[128]{0:T(128)S(1)} %fusion.160) | copy-start | bytes 1540
  313.7 136.3 %copy-start.33 = (bf16[128,1024]{1,0:T(8,128)(2,1)S(1)}, bf16[128,1024]{1,0:T(8,128)(2,1)}, u32[]{:S(2)}) copy-start(bf16[128,1024]{1,0:T(8,128)(2,1)} %get-tuple-element.210) | copy-start | bytes 786436
  392.0 133.8 %copy-start.62 = (bf16[128,1024]{1,0:T(8,128)(2,1)}, bf16[128,1024]{1,0:T(8,128)(2,1)S(1)}, u32[]{:S(2)}) copy-start(bf16[128,1024]{1,0:T(8,128)(2,1)S(1)} %fusion.77) | copy-start | bytes 786436
  453.0 75.0 %copy-start.83 = (f32[128,128]{0,1:T(8,128)S(1)}, f32[128,128]{0,1:T(8,128)}, u32[]{:S(2)}) copy-start(f32[128,128]{0,1:T(8,128)} %subtract_abs_fusion) | copy-start | bytes 196612
  453.0 76.7 %copy-start.97 = (f32[128]{0:T(128)}, f32[128]{0:T(128)S(1)}, u32[]{:S(2)}) copy-start(f32[128]{0:T(128)S(1)} %broadcast_multiply_fusion.3) | copy-start | bytes 1540
  453.2 74.8 %copy-start.129 = (f32[128]{0:T(128)}, f32[128]{0:T(128)S(1)}, u32[]{:S(2)}) copy-start(f32[128]{0:T(128)S(1)} %multiply_reduce_fusion.18) | copy-start | bytes 1540
  453.3 79.2 %copy-start.109 = (f32[128]{0:T(128)}, f32[128]{0:T(128)S(1)}, u32[]{:S(2)}) copy-start(f32[128]{0:T(128)S(1)} %fusion.161) | copy-start | bytes 1540
  581.3 83.2 %copy-start.86 = (f32[128]{0:T(128)}, f32[128]{0:T(128)S(1)}, u32[]{:S(2)}) copy-start(f32[128]{0:T(128)S(1)} %broadcast_multiply_fusion.2) | copy-start | bytes 1540
  582.0 82.5 %copy-start.92 = (f32[128]{0:T(128)}, f32[128]{0:T(128)S(1)}, u32[]{:S(2)}) copy-start(f32[128]{0:T(128)S(1)} %fusion.162) | copy-start | bytes 1540
  763.1 9.1 copy-start.14
  763.1 9.1 copy-start.5
  770.7 9.0 slice-start
  772.3 11.3 copy-start.18
  791.4 8.7 copy-start.96
  799.9 264.9 %reduce-scatter.38.cloned.1.call-start = ((), (), s32[]{:S(2)}) async-start(), calls=%async_computation.26 | async-start | bytes 540672 | tf_op jit(solution)/shard_map/reduce_scatter | solution.py:316
  834.6 364.2 %reduce-scatter.16.cloned.1.call-start = ((), (), s32[]{:S(2)}) async-start(), calls=%async_computation.15 | async-start | bytes 1081344 | tf_op jit(solution)/shard_map/reduce_scatter | solution.py:313
  911.0 429.1 %reduce-scatter.24.cloned.1.call-start = ((), (), s32[]{:S(2)}) async-start(), calls=%async_computation.19 | async-start | bytes 4325376 | tf_op jit(solution)/shard_map/reduce_scatter | solution.py:226
  914.7 567.4 %reduce-scatter.26.cloned.1.call-start = ((), (), s32[]{:S(2)}) async-start(), calls=%async_computation.20 | async-start | bytes 4325376 | tf_op jit(solution)/shard_map/reduce_scatter | solution.py:226
  918.5 749.4 %reduce-scatter.18.cloned.1.call-start = ((), (), s32[]{:S(2)}) async-start(), calls=%async_computation.16 | async-start | bytes 17301504 | tf_op jit(solution)/shard_map/reduce_scatter | solution.py:314
  952.4 875.5 %reduce-scatter.20.cloned.1.call-start = ((), (), s32[]{:S(2)}) async-start(), calls=%async_computation.17 | async-start | bytes 12976128 | tf_op jit(solution)/shard_map/reduce_scatter | solution.py:225
  960.1 1028.1 %reduce-scatter.22.cloned.1.call-start = ((), (), s32[]{:S(2)}) async-start(), calls=%async_computation.18 | async-start | bytes 12976128 | tf_op jit(solution)/shard_map/reduce_scatter | solution.py:225
  967.8 1173.8 %reduce-scatter.36.cloned.1.call-start = ((), (), s32[]{:S(2)}) async-start(), calls=%async_computation.25 | async-start | bytes 8650752 | tf_op jit(solution)/shard_map/reduce_scatter | solution.py:315
  973.5 1355.0 %reduce-scatter.32.cloned.1.call-start = ((), (), s32[]{:S(2)}) async-start(), calls=%async_computation.23 | async-start | bytes 17301504 | tf_op jit(solution)/shard_map/reduce_scatter | solution.py:228
  984.5 1530.8 %reduce-scatter.34.cloned.1.call-start = ((), (), s32[]{:S(2)}) async-start(), calls=%async_computation.24 | async-start | bytes 17301504 | tf_op jit(solution)/shard_map/reduce_scatter | solution.py:228
  995.4 1706.7 %reduce-scatter.28.cloned.1.call-start = ((), (), s32[]{:S(2)}) async-start(), calls=%async_computation.21 | async-start | bytes 17301504 | tf_op jit(solution)/shard_map/reduce_scatter | solution.py:227
  1004.8 1884.1 %reduce-scatter.30.cloned.1.call-start = ((), (), s32[]{:S(2)}) async-start(), calls=%async_computation.22 | async-start | bytes 17301504 | tf_op jit(solution)/shard_map/reduce_scatter | solution.py:227
  1014.3 1919.8 %copy-start.46 = (f32[31,32,64]{2,1,0:T(8,128)S(1)}, f32[31,32,64]{2,1,0:T(8,128)}, u32[]{:S(2)}) copy-start(f32[31,32,64]{2,1,0:T(8,128)} %param.42) | copy-start | bytes 761860
  1014.3 1919.8 %copy-start.68 = (f32[31,32,64]{2,1,0:T(8,128)S(1)}, f32[31,32,64]{2,1,0:T(8,128)}, u32[]{:S(2)}) copy-start(f32[31,32,64]{2,1,0:T(8,128)} %param.44) | copy-start | bytes 761860
  1014.3 1925.6 %copy-start.104 = (f32[5,32]{1,0:T(8,128)S(1)}, f32[5,32]{1,0:T(8,128)}, u32[]{:S(2)}) copy-start(f32[5,32]{1,0:T(8,128)} %param.63) | copy-start | bytes 1924
  1014.4 1925.6 %copy-start.114 = (f32[5,32]{1,0:T(8,128)S(1)}, f32[5,32]{1,0:T(8,128)}, u32[]{:S(2)}) copy-start(f32[5,32]{1,0:T(8,128)} %param.65) | copy-start | bytes 1924
  1014.4 1925.6 %copy-start.115 = (f32[5,32]{1,0:T(8,128)S(1)}, f32[5,32]{1,0:T(8,128)}, u32[]{:S(2)}) copy-start(f32[5,32]{1,0:T(8,128)} %param.64) | copy-start | bytes 1924
  1014.4 1926.2 %copy-start.27 = (f32[2,128,1024]{2,1,0:T(8,128)S(1)}, f32[2,128,1024]{2,1,0:T(8,128)}, u32[]{:S(2)}) copy-start(f32[2,128,1024]{2,1,0:T(8,128)} %param.54) | copy-start | bytes 3145732
  2328.4 612.1 %copy-start.41 = (f32[128,1024]{1,0:T(8,128)S(1)}, f32[128,1024]{1,0:T(8,128)}, u32[]{:S(2)}) copy-start(f32[128,1024]{1,0:T(8,128)} %reduce-scatter.32.cloned.1.call-done) | copy-start | bytes 1572868
  2515.2 425.3 %copy-start.42 = (f32[128,1024]{1,0:T(8,128)S(1)}, f32[128,1024]{1,0:T(8,128)}, u32[]{:S(2)}) copy-start(f32[128,1024]{1,0:T(8,128)} %reduce-scatter.34.cloned.1.call-done) | copy-start | bytes 1572868
  2934.2 8.7 copy-start.28
  2934.2 8.7 copy-start.44
  2934.2 8.7 copy-start.45
  2934.2 8.7 copy-start.60
  2934.2 8.7 copy-start.61
  (97 other events, 450.5 us)
Sparse Core Ops, SparseCore 0:
  11.0 88.1 all-gather.19
  102.2 67.5 all-gather.23
  172.8 55.7 all-gather.25
  231.4 76.2 all-gather.27
  310.5 75.8 all-gather.29
  389.3 60.6 all-gather.21
  453.0 67.9 all-gather.31
  524.0 54.9 all-gather.33
  582.0 76.2 all-gather.35
  661.2 75.9 all-gather.37
  800.0 132.2 reduce-scatter.39
  934.5 130.2 reduce-scatter.37
  1067.6 131.1 reduce-scatter.15
  1201.0 139.0 reduce-scatter.23
  1342.3 139.7 reduce-scatter.25
  1484.4 183.4 reduce-scatter.17
  1674.7 153.0 reduce-scatter.19
  1833.8 154.3 reduce-scatter.21
  1990.6 150.9 reduce-scatter.35
  2143.8 184.5 reduce-scatter.31
  2330.8 184.3 reduce-scatter.33
  2517.6 184.3 reduce-scatter.27
  2704.4 184.3 reduce-scatter.29
where the time goes:
time: 2970 us; the launch traced here: 2960 us
  waiting for transfers between devices  2300 us (77%)
  local copies, waits for them, and re-layouts  232 us (8%)
  matrix products  190 us (6%)
  blocking collectives  162 us (5%)
  other arithmetic  51.2 us (2%)
    reduce_scatter x2, waiting for transfers between devices, share(): lax.psum_scatter(grads[3], ('dp', 'fsdp'), scatter_dimension=0, tiled=True)  372 us
    reduce_scatter x2, waiting for transfers between devices, share(): lax.psum_scatter(grads[2], ('dp', 'fsdp'), scatter_dimension=0, tiled=True)  371 us
    reduce_scatter x2, waiting for transfers between devices, share(): lax.psum_scatter(grads[0], ('dp', 'fsdp'), scatter_dimension=0, tiled=True)  317 us
    reduce_scatter x2, waiting for transfers between devices, share(): lax.psum_scatter(grads[1], ('dp', 'fsdp'), scatter_dimension=0, tiled=True)  282 us
    reduce_scatter x1, waiting for transfers between devices, shards(): lax.psum_scatter(d_kernel, ('dp', 'fsdp'), scatter_dimension=1, tiled=True)  184 us
    reduce_scatter x1, waiting for transfers between devices, shards(): lax.psum_scatter(d_bridge, ('dp', 'fsdp'), scatter_dimension=0, tiled=True)  150 us
    all_gather x2, waiting for transfers between devices, fetch(): lax.all_gather(reduce_master[layer_index].astype(low_type), ('dp', 'fsdp'...  145 us
    reduce_scatter x1, waiting for transfers between devices, shards(): lax.psum_scatter(input_gradient, ('dp', 'fsdp'), scatter_dimension=1, til...  133 us
  transfers between devices with their start and end apart: 23, of which 19 were waited for; matrix products, arithmetic and copies ran while one was open for 13% of the time, Pallas kernels for 0%

commit v1 on v0

--- a/solution.py
+++ b/solution.py
@@ -1,6 +1,8 @@
 import jax
 import jax.numpy as jnp
 from jax import lax
+from jax.experimental import pallas as pl
+from jax.experimental.pallas import tpu as pltpu
 from jax.sharding import PartitionSpec as P
 
 D = 1024
@@ -366,6 +368,975 @@
     return (loss_sum, frame_total, grad_norm, *results)
 
 
+LOW = jnp.bfloat16
+WIDE = jnp.float32
+BOTH = ("dp", "fsdp")
+VMEM_GRANT = 24 * 2**20
+GRANT = pltpu.CompilerParams(vmem_limit_bytes=VMEM_GRANT)
+TAPS_OUT = 8
+GELU_SCALE = 0.7978845608028654
+SHORT = pl.CostEstimate(flops=1000, bytes_accessed=1000, transcendentals=0)
+LANES = 512
+Z_LINES = [[half + 2 * i for i in range(4)] for half in range(2)]
+
+
+def swap_x(item):
+    return lax.ppermute(item, "dp", [(i, i ^ 1) for i in range(4)])
+
+
+def swap_y(item):
+    return lax.ppermute(item, "dp", [(i, i ^ 2) for i in range(4)])
+
+
+def swap_core(item):
+    return lax.ppermute(item, "fsdp", [(i, i ^ 1) for i in range(8)])
+
+
+def shift_z(item, hops):
+    return lax.ppermute(item, "fsdp", [(i, (i + 2 * hops) % 8) for i in range(8)])
+
+
+def pick(stacked, index):
+    return lax.dynamic_index_in_dim(stacked, index, 0, keepdims=False)
+
+
+def in_order(core, mine, other):
+    first = core == 0
+    return jnp.where(first, mine, other), jnp.where(first, other, mine)
+
+
+def side_by_side(core, mine):
+    return jnp.concatenate(in_order(core, mine, swap_core(mine)), -1)
+
+
+def z_line(own, z):
+    parts = [own] + [shift_z(own, hops) for hops in (1, 2, 3)]
+    line = jnp.zeros((4,) + own.shape, own.dtype)
+    for hops, part in enumerate(parts):
+        line = lax.dynamic_update_index_in_dim(line, part, (z - hops) % 4, 0)
+    return line
+
+
+def laid_out(weights_ref, places_ref, whole_ref, part):
+    for slot in range(16):
+        start = pl.multiple_of(places_ref[slot] * part, 16)
+        whole_ref[pl.ds(start, part), :] = weights_ref[slot]
+
+
+def piece_dot(rows, weights, base, part, count, low=False, with_gelu=False):
+    gathered, places = weights
+    row_count, depth = rows.shape
+    out_type = LOW if low else WIDE
+    width = count * LANES
+
+    def body(places_ref, rows_ref, weights_ref, *refs):
+        whole_ref = refs[-1]
+        laid_out(weights_ref, places_ref, whole_ref, part)
+        total = jnp.dot(rows_ref[...], whole_ref[...], preferred_element_type=WIDE)
+        refs[0][...] = total.astype(out_type)
+        if with_gelu:
+            refs[1][...] = jax.nn.gelu(total).astype(LOW)
+
+    out_spec = pl.BlockSpec((row_count, LANES), lambda j, s: (0, j))
+    shape = jax.ShapeDtypeStruct((row_count, width), out_type)
+    low_shape = jax.ShapeDtypeStruct((row_count, width), LOW)
+    return pl.pallas_call(
+        body,
+        grid_spec=pltpu.PrefetchScalarGridSpec(
+            num_scalar_prefetch=1,
+            grid=(count,),
+            in_specs=[
+                pl.BlockSpec((row_count, depth), lambda j, s: (0, 0)),
+                pl.BlockSpec((16, part, LANES), lambda j, s: (0, j + base // part, 0)),
+            ],
+            out_specs=[out_spec, out_spec] if with_gelu else out_spec,
+            scratch_shapes=[pltpu.VMEM((depth, LANES), LOW)],
+        ),
+        out_shape=[shape, low_shape] if with_gelu else shape,
+        compiler_params=GRANT,
+        cost_estimate=SHORT,
+    )(places, rows, gathered)
+
+
+def gelu_slope(values):
+    cubic = 0.044715 * values * values
+    bent = jnp.tanh(GELU_SCALE * values * (1.0 + cubic))
+    return 0.5 * (1.0 + bent) + 0.5 * values * (1.0 - bent * bent) * GELU_SCALE * (
+        1.0 + 3.0 * cubic
+    )
+
+
+def piece_dot_back(grads, weights, base, part, upper=None, split=False):
+    gathered, places = weights
+    row_count, width = grads.shape
+    depth, steps = 16 * part, grads.shape[1] // LANES
+    half = depth // 2
+
+    def body(places_ref, grads_ref, weights_ref, *refs):
+        total_ref, whole_ref = refs[-2:]
+        laid_out(weights_ref, places_ref, whole_ref, part)
+        product = lax.dot_general(
+            grads_ref[...],
+            whole_ref[...],
+            (((1,), (1,)), ((), ())),
+            preferred_element_type=WIDE,
+        )
+
+        @pl.when(pl.program_id(0) == 0)
+        def _():
+            total_ref[...] = product
+
+        @pl.when(pl.program_id(0) > 0)
+        def _():
+            total_ref[...] += product
+
+        @pl.when(pl.program_id(0) == steps - 1)
+        def _():
+            if upper is not None:
+                refs[1][...] = (total_ref[...] * gelu_slope(refs[0][...])).astype(LOW)
+            elif split:
+                core = places_ref[16]
+                refs[0][...] = total_ref[:, pl.ds(pl.multiple_of(core * half, 128), half)]
+                refs[1][...] = total_ref[:, pl.ds(pl.multiple_of((1 - core) * half, 128), half)]
+            else:
+                refs[0][...] = total_ref[...]
+
+    def fixed(shape):
+        return pl.BlockSpec(shape, lambda j, s: (0, 0))
+
+    if split:
+        shapes = [jax.ShapeDtypeStruct((row_count, half), WIDE)] * 2
+    else:
+        shapes = [jax.ShapeDtypeStruct((row_count, depth), WIDE if upper is None else LOW)]
+    extra = [] if upper is None else [upper]
+    out = pl.pallas_call(
+        body,
+        grid_spec=pltpu.PrefetchScalarGridSpec(
+            num_scalar_prefetch=1,
+            grid=(steps,),
+            in_specs=[
+                pl.BlockSpec((row_count, LANES), lambda j, s: (0, j)),
+                pl.BlockSpec((16, part, LANES), lambda j, s: (0, j + base // part, 0)),
+            ]
+            + [fixed(item.shape) for item in extra],
+            out_specs=[fixed(item.shape) for item in shapes],
+            scratch_shapes=[
+                pltpu.VMEM((row_count, depth), WIDE),
+                pltpu.VMEM((depth, LANES), LOW),
+            ],
+        ),
+        out_shape=shapes,
+        compiler_params=GRANT,
+        cost_estimate=SHORT,
+    )(places, grads, gathered, *extra)
+    return out if split else out[0]
+
+
+def whole_blocks(items):
+    return [pl.BlockSpec(item.shape, lambda s, n=len(item.shape): (0,) * n) for item in items]
+
+
+def one_step(body, scalars, operands, shapes, scratch=()):
+    return pl.pallas_call(
+        body,
+        grid_spec=pltpu.PrefetchScalarGridSpec(
+            num_scalar_prefetch=1,
+            grid=(),
+            in_specs=[pl.BlockSpec(memory_space=pltpu.VMEM)] * len(operands),
+            out_specs=[pl.BlockSpec(memory_space=pltpu.VMEM)] * len(shapes),
+            scratch_shapes=list(scratch),
+        ),
+        out_shape=shapes,
+        compiler_params=GRANT,
+        cost_estimate=SHORT,
+    )(scalars, *operands)
+
+
+def norm_forward(base, mine, other, gain, scalars, halves):
+    addends = [] if mine is None else [mine, other]
+    bases = [] if base is None else [base]
+    rows = (mine if base is None else base).shape[0]
+    width = gain.shape[1]
+    half = width // 2
+
+    def body(scalars_ref, *refs):
+        gain_ref, stream_ref, normed_ref = refs[-3:]
+        base_ref = None if base is None else refs[0]
+        if mine is None:
+            stream_ref[...] = base_ref[...]
+        elif halves:
+            mine_ref, other_ref = refs[len(bases) : len(bases) + 2]
+            core = scalars_ref[16]
+            for ref, side in ((mine_ref, core), (other_ref, 1 - core)):
+                lanes = pl.ds(pl.multiple_of(side * half, 128), half)
+                part = ref[...]
+                stream_ref[:, lanes] = part if base is None else base_ref[:, lanes] + part
+        else:
+            mine_ref, other_ref = refs[len(bases) : len(bases) + 2]
+            stream_ref[...] = base_ref[...] + (mine_ref[...] + other_ref[...])
+        normed_ref[...] = (norm_parts(stream_ref[...]) * gain_ref[...]).astype(LOW)
+
+    shapes = [jax.ShapeDtypeStruct((rows, width), WIDE), jax.ShapeDtypeStruct((rows, width), LOW)]
+    return one_step(body, scalars, (*bases, *addends, gain), shapes)
+
+
+def norm_backward(mine, other, values, gain, incoming, scalars):
+    rows, width = values.shape
+    half = width // 2
+
+    def body(scalars_ref, mine_ref, other_ref, values_ref, gain_ref, incoming_ref, *refs):
+        total_ref, low_ref, low_half_ref, row_ref, terms_ref = refs
+        core = scalars_ref[16]
+        back, terms = norm_back(values_ref[...], gain_ref[...], mine_ref[...] + other_ref[...])
+        total = incoming_ref[...] + back
+        total_ref[...] = total
+        low_ref[...] = total.astype(LOW)
+        low_half_ref[...] = low_ref[:, pl.ds(pl.multiple_of(core * half, 128), half)]
+        terms_ref[...] = terms
+        own = terms_ref[pl.ds(pl.multiple_of(core * (rows // 2), 8), rows // 2), :]
+        row_ref[...] = jnp.sum(own, 0, keepdims=True)
+
+    shapes = [
+        jax.ShapeDtypeStruct((rows, width), WIDE),
+        jax.ShapeDtypeStruct((rows, width), LOW),
+        jax.ShapeDtypeStruct((rows, half), LOW),
+        jax.ShapeDtypeStruct((1, width), WIDE),
+    ]
+    scratch = [pltpu.VMEM((rows, width), WIDE)]
+    return one_step(
+        body, scalars, (mine, other, values, gain, incoming), shapes, scratch
+    )
+
+
+def head_probs(joint_ref, head, size, slope, valid, distance):
+    third = joint_ref.shape[1] // 3
+    query = joint_ref[:, head * size : (head + 1) * size]
+    keyed = joint_ref[:, third + head * size : third + (head + 1) * size]
+    scores = lax.dot_general(
+        query, keyed, (((1,), (1,)), ((), ())), preferred_element_type=WIDE
+    )
+    scores = jnp.where(valid, scores * size ** (-0.5) - slope * distance, MASKED)
+    raised = jnp.exp(scores - jnp.max(scores, -1, keepdims=True))
+    return query, keyed, raised / jnp.sum(raised, -1, keepdims=True)
+
+
+def frame_distance(frames):
+    ahead = lax.broadcasted_iota(jnp.int32, (frames, frames), 0)
+    return jnp.abs(ahead - lax.broadcasted_iota(jnp.int32, (frames, frames), 1)).astype(WIDE)
+
+
+def attend(joint, slopes, valid, size):
+    rows, triple = joint.shape
+    frames, third = rows // 2, triple // 3
+
+    def body(slopes_ref, joint_ref, valid_ref, out_ref):
+        distance = frame_distance(frames)
+        mask = jnp.broadcast_to(valid_ref[0] > 0.5, (frames, frames))
+        for head in range(third // size):
+            _, _, probs = head_probs(joint_ref, head, size, slopes_ref[head], mask, distance)
+            value = joint_ref[:, 2 * third + head * size : 2 * third + (head + 1) * size]
+            mixed = jnp.dot(probs.astype(LOW), value, preferred_element_type=WIDE)
+            out_ref[:, head * size : (head + 1) * size] = mixed.astype(LOW)
+
+    return pl.pallas_call(
+        body,
+        grid_spec=pltpu.PrefetchScalarGridSpec(
+            num_scalar_prefetch=1,
+            grid=(2,),
+            in_specs=[
+                pl.BlockSpec((frames, triple), lambda u, s: (u, 0)),
+                pl.BlockSpec((1, 1, frames), lambda u, s: (u, 0, 0)),
+            ],
+            out_specs=pl.BlockSpec((frames, third), lambda u, s: (u, 0)),
+        ),
+        out_shape=jax.ShapeDtypeStruct((rows, third), LOW),
+        compiler_params=GRANT,
+        cost_estimate=SHORT,
+    )(slopes, joint, valid)
+
+
+def attend_back(joint, mine, other, slopes, valid, size):
+    rows, triple = joint.shape
+    frames, third = rows // 2, triple // 3
+
+    def body(slopes_ref, joint_ref, mine_ref, other_ref, valid_ref, out_ref):
+        distance = frame_distance(frames)
+        mask = jnp.broadcast_to(valid_ref[0] > 0.5, (frames, frames))
+        scale = size ** (-0.5)
+        for head in range(third // size):
+            cut = slice(head * size, (head + 1) * size)
+            query, keyed, probs = head_probs(
+                joint_ref, head, size, slopes_ref[head], mask, distance
+            )
+            value = joint_ref[:, 2 * third + head * size : 2 * third + (head + 1) * size]
+            grad = (mine_ref[:, cut] + other_ref[:, cut]).astype(LOW)
+            d_probs = lax.dot_general(
+                grad, value, (((1,), (1,)), ((), ())), preferred_element_type=WIDE
+            )
+            inner = jnp.sum(probs * d_probs, -1, keepdims=True)
+            d_scores = (probs * (d_probs - inner)).astype(LOW)
+            d_query = jnp.dot(d_scores, keyed, preferred_element_type=WIDE) * scale
+            d_keyed = jnp.dot(d_scores.T, query, preferred_element_type=WIDE) * scale
+            d_value = jnp.dot(probs.astype(LOW).T, grad, preferred_element_type=WIDE)
+            for spot, item in enumerate((d_query, d_keyed, d_value)):
+                start = spot * third + head * size
+                out_ref[:, start : start + size] = item.astype(LOW)
+
+    def utterance(width):
+        return pl.BlockSpec((frames, width), lambda u, s: (u, 0))
+
+    return pl.pallas_call(
+        body,
+        grid_spec=pltpu.PrefetchScalarGridSpec(
+            num_scalar_prefetch=1,
+            grid=(2,),
+            in_specs=[
+                utterance(triple),
+                utterance(third),
+                utterance(third),
+                pl.BlockSpec((1, 1, frames), lambda u, s: (u, 0, 0)),
+            ],
+            out_specs=utterance(triple),
+        ),
+        out_shape=jax.ShapeDtypeStruct((rows, triple), LOW),
+        compiler_params=GRANT,
+        cost_estimate=SHORT,
+    )(slopes, joint, mine, other, valid)
+
+
+def packed_tokens(left, right, numbers):
+    rows, depth = left.shape
+    quarter, width = depth // 4, right.shape[1]
+
+    def body(numbers_ref, left_ref, right_ref, out_ref):
+        for spot in range(2):
+            start = pl.multiple_of(numbers_ref[spot] * quarter, 128)
+            out_ref[:, spot * quarter : (spot + 1) * quarter] = left_ref[:, pl.ds(start, quarter)]
+        out_ref[:, 2 * quarter :] = right_ref[...]
+
+    shapes = [jax.ShapeDtypeStruct((rows, 2 * quarter + width), LOW)]
+    return one_step(body, numbers, (left, right), shapes)[0]
+
+
+def outer_sum(left, right, got, number, second, out_type):
+    rows, depth = left.shape
+    quarter, width = depth // 4, right.shape[1]
+
+    def body(number_ref, left_ref, right_ref, far_left_ref, far_right_ref, out_ref):
+        dims = (((0,), (0,)), ((), ()))
+        total = lax.dot_general(
+            left_ref[...], right_ref[...], dims, preferred_element_type=WIDE
+        )
+        total = total + lax.dot_general(
+            far_left_ref[...], far_right_ref[...], dims, preferred_element_type=WIDE
+        )
+        out_ref[...] = total.astype(out_type)
+
+    return pl.pallas_call(
+        body,
+        grid_spec=pltpu.PrefetchScalarGridSpec(
+            num_scalar_prefetch=1,
+            grid=(width // LANES,),
+            in_specs=[
+                pl.BlockSpec((rows, quarter), lambda j, s: (0, s[0])),
+                pl.BlockSpec((rows, LANES), lambda j, s: (0, j)),
+                pl.BlockSpec((rows, quarter), lambda j, s: (0, second)),
+                pl.BlockSpec((rows, LANES), lambda j, s: (0, j + 2 * quarter // LANES)),
+            ],
+            out_specs=pl.BlockSpec((quarter, LANES), lambda j, s: (0, j)),
+        ),
+        out_shape=jax.ShapeDtypeStruct((quarter, width), out_type),
+        compiler_params=GRANT,
+        cost_estimate=SHORT,
+    )(number, left, right, got, got)
+
+
+def banded_kernel(body, operands, blocks, out_block, shape, sums):
+    def summed(*refs):
+        if not sums:
+            refs[-1][...] = body(*refs[:-1])
+            return
+
+        @pl.when(pl.program_id(0) == 0)
+        def _():
+            refs[-1][...] = jnp.zeros_like(refs[-1])
+
+        refs[-1][...] += body(*refs[:-1])
+
+    return pl.pallas_call(
+        summed,
+        grid=(5,),
+        in_specs=blocks,
+        out_specs=out_block,
+        out_shape=jax.ShapeDtypeStruct(shape, WIDE),
+        compiler_params=GRANT,
+        cost_estimate=SHORT,
+    )(*operands)
+
+
+def banded_dot(windows, banded):
+    rows, (_, depth, width) = windows.shape[0], banded.shape
+    return banded_kernel(
+        lambda left, right: jnp.dot(left[...], right[0], preferred_element_type=WIDE),
+        (windows, banded),
+        [
+            pl.BlockSpec((rows, depth), lambda i: (0, i)),
+            pl.BlockSpec((1, depth, width), lambda i: (i, 0, 0)),
+        ],
+        pl.BlockSpec((rows, width), lambda i: (0, 0)),
+        (rows, width),
+        True,
+    )
+
+
+def banded_back(grads, banded):
+    rows, (_, depth, width) = grads.shape[0], banded.shape
+    dims = (((1,), (1,)), ((), ()))
+    return banded_kernel(
+        lambda left, right: lax.dot_general(
+            left[...], right[0], dims, preferred_element_type=WIDE
+        ),
+        (grads, banded),
+        [
+            pl.BlockSpec((rows, width), lambda i: (0, i)),
+            pl.BlockSpec((1, depth, width), lambda i: (i, 0, 0)),
+        ],
+        pl.BlockSpec((rows, depth), lambda i: (0, 0)),
+        (rows, depth),
+        True,
+    )
+
+
+def banded_outer(windows, grads):
+    rows, width = grads.shape
+    depth = windows.shape[1] // 5
+    dims = (((0,), (0,)), ((), ()))
+    return banded_kernel(
+        lambda left, right: lax.dot_general(
+            left[...], right[...], dims, preferred_element_type=WIDE
+        ),
+        (windows, grads),
+        [
+            pl.BlockSpec((rows, depth), lambda i: (0, i)),
+            pl.BlockSpec((rows, width), lambda i: (0, 0)),
+        ],
+        pl.BlockSpec((depth, width), lambda i: (i, 0)),
+        (windows.shape[1], width),
+        False,
+    )
+
+
+def norm_parts(values):
+    center = values - jnp.mean(values, -1, keepdims=True)
+    spread = jnp.mean(center * center, -1, keepdims=True)
+    return center * lax.rsqrt(spread + NORM_EPS)
+
+
+def norm_back(values, gain_row, grads):
+    center = values - jnp.mean(values, -1, keepdims=True)
+    spread = jnp.mean(center * center, -1, keepdims=True)
+    inverse = lax.rsqrt(spread + NORM_EPS)
+    unit = center * inverse
+    scaled = grads * gain_row
+    back = inverse * (
+        scaled
+        - jnp.mean(scaled, -1, keepdims=True)
+        - unit * jnp.mean(scaled * unit, -1, keepdims=True)
+    )
+    return back, grads * unit
+
+
+def tp_forward(stream, normed, mats, gain_two, slopes, valid, scalars, beside=None):
+    (joint_out, jo), (expand, ex), (reduce, re) = mats
+    width = stream.shape[1]
+    joint = piece_dot(normed, joint_out, jo, 64, 3, low=True)
+    context = attend(joint, slopes, valid, width // HEADS)
+    context = side_by_side(scalars[16], context)
+    mixed = piece_dot(context, joint_out, jo + 192, 64, 1)
+    if beside is not None:
+        mixed, _ = tie((mixed, beside))
+    middle, normed_two = norm_forward(stream, mixed, swap_core(mixed), gain_two, scalars, True)
+    upper, hidden = piece_dot(normed_two, expand, ex, 64, 4, with_gelu=True)
+    lowered = piece_dot(hidden, reduce, re, 128, 2)
+    kept = (stream, normed, joint, context, middle, normed_two, upper, hidden)
+    return middle, lowered, kept
+
+
+tie = lax.optimization_barrier
+
+
+class Share:
+    def __init__(self, left, right, spot, by_y):
+        y, x = spot
+        self.left, self.right = left, right
+        if by_y:
+            self.hops = [swap_y, swap_x]
+            passed, theirs = (y, 1 - x), ((1 - y, 1 - x), (1 - y, x))
+        else:
+            self.hops = [swap_x, swap_y]
+            passed, theirs = (1 - y, x), ((1 - y, 1 - x), (y, 1 - x))
+        numbers = [2 * row + column for row, column in (passed, (y, x), *theirs)]
+        self.passed, self.own, *theirs = [number.astype(jnp.int32) for number in numbers]
+        self.made = packed_tokens(left, right, jnp.stack(theirs))
+        self.flying = self.total = self.beside = None
+        self.turns = 0
+
+    def send(self):
+        if self.hops:
+            self.flying = self.hops.pop(0)(self.made)
+        else:
+            self.flying = None
+            self.total = lax.psum_scatter(
+                self.made, "fsdp", scatter_dimension=0, axis_index_groups=Z_LINES, tiled=True
+            )
+
+    def land(self, landed):
+        terms = (self.left, self.right, landed)
+        if self.hops:
+            self.made = outer_sum(*terms, self.passed[None], 0, LOW)
+            self.kept = outer_sum(*terms, self.own[None], 1, WIDE)
+        else:
+            self.made = (self.kept + landed.astype(WIDE)).astype(LOW)
+
+
+class Flow:
+    def __init__(self):
+        self.shares = []
+
+    def add(self, values, *terms):
+        added = [Share(*term) for term in terms]
+        values, made = tie((values, [share.made for share in added]))
+        for share, item in zip(added, made):
+            share.made = item
+            share.send()
+        self.shares += added
+        return (*values, *added)
+
+    def turn(self, *values):
+        flying = [share for share in self.shares if share.flying is not None]
+        summed = [share for share in self.shares if share.total is not None]
+        for share in summed:
+            share.turns += 1
+        summed = [share for share in summed if share.turns == 3]
+        values, landed, totals = tie(
+            (values, [share.flying for share in flying], [share.total for share in summed])
+        )
+        for share, item in zip(summed, totals):
+            share.total = item
+        for share, item in zip(flying, landed):
+            share.land(item)
+        for share in [share for share in flying if share.beside is not None]:
+            if not share.hops:
+                share.made = jnp.concatenate([share.made, share.beside.made], 1)
+                share.beside.flying = None
+                flying.remove(share.beside)
+        values, made = tie((values, [share.made for share in flying]))
+        for share, item in zip(flying, made):
+            share.made = item
+            share.send()
+        return values
+
+
+def own_rows(total, core):
+    halves = total.reshape(2, total.shape[0] // 2, total.shape[1])
+    mine, other = pick(halves, core), swap_core(pick(halves, 1 - core))
+    return jnp.stack(in_order(core, mine, other))
+
+
+def tp_backward(
+    incoming, incoming_low, kept, mats, gain_one, gain_two, slopes, valid, spot, scalars, flow
+):
+    stream, normed, joint, context, middle, normed_two, upper, hidden = kept
+    (joint_out, jo), (expand, ex), (reduce, re) = mats
+    d_upper = piece_dot_back(incoming_low, reduce, re, 128, upper=upper)
+    d_normed = piece_dot_back(d_upper, expand, ex, 64)
+    incoming, d_upper, d_normed = flow.turn(incoming, d_upper, d_normed)
+    d_normed, g_reduce, g_expand = flow.add(
+        (d_normed,), (hidden, incoming_low, spot, False), (normed_two, d_upper, spot, True)
+    )
+    d_middle, _, d_middle_low, d_gain_two = norm_backward(
+        d_normed, swap_core(d_normed), middle, gain_two, incoming, scalars
+    )
+    mine, other = piece_dot_back(d_middle_low, joint_out, jo + 192, 64, split=True)
+    mine, other, d_middle, d_middle_low = flow.turn(mine, other, d_middle, d_middle_low)
+    d_joint = attend_back(
+        joint, mine, swap_core(other), slopes, valid, stream.shape[1] // HEADS
+    )
+    d_normed = piece_dot_back(d_joint, joint_out, jo, 64)
+    d_joint, d_normed = flow.turn(d_joint, d_normed)
+    d_normed, g_output, g_joint = flow.add(
+        (d_normed,), (context, d_middle_low, spot, False), (normed, d_joint, spot, True)
+    )
+    g_joint.beside = g_output
+    result = norm_backward(d_normed, swap_core(d_normed), stream, gain_one, d_middle, scalars)
+    return result, (g_joint, g_expand, g_reduce), d_gain_two
+
+
+def paired_shards(
+    spectra,
+    gaussian,
+    flow_times,
+    lengths,
+    span_flags,
+    phone_ids,
+    input_master,
+    input_moment,
+    input_square,
+    kernel_master,
+    kernel_moment,
+    kernel_square,
+    joint_master,
+    joint_moment,
+    joint_square,
+    output_master,
+    output_moment,
+    output_square,
+    expand_master,
+    expand_moment,
+    expand_square,
+    reduce_master,
+    reduce_moment,
+    reduce_square,
+    bridge_master,
+    bridge_moment,
+    bridge_square,
+    readout_master,
+    readout_moment,
+    readout_square,
+    gains_master,
+    gains_moment,
+    gains_square,
+):
+    dp_index, fsdp_index = lax.axis_index("dp"), lax.axis_index("fsdp")
+    y, x = dp_index // 2, dp_index % 2
+    z, core = fsdp_index // 2, fsdp_index % 2
+    spot = (y, x)
+    corners = [2 * y + x, 2 * y + 1 - x, 2 * (1 - y) + x, 2 * (1 - y) + 1 - x]
+    behind = [(z - hops) % 4 for hops in range(4)]
+    in_place = jnp.stack([*range(16), core]).astype(jnp.int32)
+    all_shifted = [4 * corner + line for corner in corners for line in behind]
+    all_shifted = jnp.stack([*all_shifted, core]).astype(jnp.int32)
+    both_shifted = [4 * corner + line for line in behind for corner in corners]
+    both_shifted = jnp.stack([*both_shifted, core]).astype(jnp.int32)
+    chip = 8 * y + 4 * x + z
+    mel_count, frame_count = spectra.shape[1:]
+    taps, outs, group = kernel_master.shape
+    width = outs * 32
+    blocks = frame_count // TAPS_OUT
+
+    with jax.named_scope("features"):
+        flags = span_flags[0].astype(WIDE)
+        valid_own = (jnp.arange(frame_count) < lengths[0]).astype(WIDE)
+        clean, noise = spectra[0].astype(WIDE), gaussian[0].astype(WIDE)
+        time = flow_times[0]
+        noisy = (1.0 - (1.0 - SIGMA_MIN) * time) * noise + time * clean
+        shown = clean * (1.0 - flags[None, :])
+        small = jnp.concatenate(
+            [readout_master.astype(LOW), gains_master.astype(LOW).T], 1
+        )
+        small = jnp.pad(small, ((0, 0), (0, frame_count - small.shape[1])))
+        packed = jnp.concatenate(
+            [
+                noisy.astype(LOW),
+                shown.astype(LOW),
+                phone_ids.astype(LOW),
+                valid_own[None].astype(LOW),
+                jnp.zeros((14, frame_count), LOW),
+                small,
+            ],
+            0,
+        )
+        line = z_line(packed, z)
+        beside, across = swap_x(line), swap_y(line)
+        corner = swap_y(beside)
+        whole = jnp.zeros((4,) + line.shape, LOW)
+        for number, part in enumerate((line, beside, across, corner)):
+            whole = lax.dynamic_update_index_in_dim(whole, part, corners[number], 0)
+        whole = whole.reshape((16,) + packed.shape)
+        whole = jnp.stack(in_order(core, whole, swap_core(whole)), 1)
+        whole = whole.reshape((32,) + packed.shape)
+        mels = whole[:, : 2 * mel_count]
+        onehot = (whole[:, 2 * mel_count][:, None, :] == jnp.arange(VOCAB, dtype=LOW)[None, :, None]).astype(LOW)
+        features = jnp.concatenate([mels, onehot], 1)
+        valid_all = whole[:, 2 * mel_count + 1].astype(WIDE)
+        small = whole[:, 2 * mel_count + 16 :].reshape(width, frame_count)
+        readout_full = small[:, :mel_count]
+        gains_full = small[:, mel_count : mel_count + 5].T.astype(WIDE)
+
+    with jax.named_scope("weights"):
+        layers, rows = joint_master.shape[:2]
+        tiles = expand_master.shape[2] // (2 * 128 * 4)
+        cut_joint = joint_master.astype(LOW).reshape(layers, rows, 3, 2, LANES)
+        cut_output = output_master.astype(LOW).reshape(layers, rows, 1, 2, LANES)
+        cut_expand = expand_master.astype(LOW).reshape(layers, rows, tiles, 4, 2, 128)
+        cut_bridge = bridge_master.astype(LOW).reshape(2, rows, 2, LANES)
+
+        def columns_of(which):
+            joint = lax.dynamic_index_in_dim(cut_joint, which, 3, keepdims=False)
+            out = lax.dynamic_index_in_dim(cut_output, which, 3, keepdims=False)
+            expand = lax.dynamic_index_in_dim(cut_expand, which, 4, keepdims=False)
+            expand = expand.reshape(layers, rows, tiles, LANES)
+            bridge = lax.dynamic_index_in_dim(cut_bridge, which, 2, keepdims=False)
+            blocks = jnp.concatenate([joint, out, expand], 2).transpose(0, 2, 1, 3)
+            blocks = blocks.reshape(layers * (4 + tiles), rows, LANES)
+            return jnp.concatenate([blocks, bridge], 0)
+
+        mine, other = in_order(core, columns_of(core), swap_core(columns_of(1 - core)))
+        blocks = layers * (4 + tiles)
+        paired = jnp.stack([mine[:blocks], other[:blocks]], 1)
+        paired = paired.reshape(layers, 4 + tiles, 2 * rows, LANES)
+        bridge = jnp.concatenate([mine[blocks:], other[blocks:]], 0).reshape(-1, LANES)
+        lowered = reduce_master.astype(LOW).reshape(layers, -1, 2, LANES)
+        lowered = lowered.transpose(0, 2, 1, 3).reshape(layers, -1, LANES)
+
+        def flat(item):
+            return item.reshape(-1, LANES)
+
+        def along_z(own):
+            parts = [own]
+            for _ in range(3):
+                parts.append(shift_z(parts[-1], 1))
+            return parts
+
+        def by_permutes(own, after_line, after_square, x_first):
+            line = jnp.concatenate(along_z(tie((own, after_line))[0]), 0)
+            line = tie((line, after_square))[0]
+            beside, across = swap_x(line), swap_y(line)
+            corner = swap_y(beside) if x_first else swap_x(across)
+            whole = jnp.concatenate([line, beside, across, corner], 0)
+            return line, (beside, across), (whole.reshape((16,) + own.shape), all_shifted)
+
+        same_core = [[half + 2 * i for i in range(16)] for half in range(2)]
+
+        def in_background(*parts):
+            own = jnp.concatenate(parts, 0)
+            whole = lax.all_gather(own, BOTH, axis=0, axis_index_groups=same_core)
+            return whole, in_place
+
+        third = in_background(lowered[0], bridge, flat(paired[1, :4]))
+        fourth = in_background(flat(paired[1, 4:]))
+        first_line, first_square, first = by_permutes(flat(paired[0, :4]), line, line, True)
+        last_own = tie((lowered[1], line))[0]
+        beside, across = swap_x(last_own), swap_y(last_own)
+        square = jnp.concatenate([last_own, beside, across, swap_y(beside)], 0)
+        second_line, _, second = by_permutes(
+            flat(paired[0, 4:]), first_line, first_square, False
+        )
+        last = along_z(tie((square, second_line))[0])
+        fifth = (jnp.concatenate(last, 0).reshape((16,) + last_own.shape), both_shifted)
+        mats_zero = ((first, 0), (second, 0), (third, 0))
+        mats_one = ((third, lowered.shape[1] + bridge.shape[0]), (fourth, 0), (fifth, 0))
+        bridge_mat = (third, lowered.shape[1])
+
+    with jax.named_scope("embedding"):
+        columns = input_master.astype(LOW)
+        columns = jnp.concatenate(in_order(core, columns, swap_core(columns)), -1)
+        start = jnp.einsum("nzv,zr->nvr", features, columns, preferred_element_type=WIDE)
+        start = start * valid_all[:, :, None]
+        padded = start.astype(LOW).reshape(32, blocks, TAPS_OUT * group)
+        padded = jnp.pad(padded, ((0, 0), (2, 2), (0, 0)))
+        windows = jnp.concatenate([padded[:, i : i + blocks] for i in range(5)], -1)
+        windows = windows.reshape(32 * blocks, 5 * TAPS_OUT * group)
+        turned = jnp.pad(
+            kernel_master.astype(LOW).transpose(0, 2, 1), ((TAPS_OUT, TAPS_OUT), (0, 0), (0, 0))
+        )
+        banded = jnp.stack([turned[7 - j : 47 - j] for j in range(TAPS_OUT)], 2)
+        banded = banded.reshape(5, TAPS_OUT * group, TAPS_OUT * outs)
+        conv_out = banded_dot(windows, banded)
+        start_own = lax.dynamic_slice_in_dim(start, core * outs, outs, 2)
+        start_own = start_own.reshape(32 * blocks, TAPS_OUT * outs)
+        embedded = start_own + jax.nn.gelu(conv_out)
+        embedded = lax.all_to_all(embedded.astype(LOW), BOTH, 0, 0, tiled=True)
+        embedded = embedded.reshape(32, frame_count, outs).transpose(1, 0, 2)
+        embedded = embedded.reshape(frame_count, width)
+        embedded = jnp.concatenate(in_order(core, embedded, swap_core(embedded)), 0)
+        embedded = embedded.astype(WIDE)
+
+    slopes = 2.0 ** (
+        -8.0 * (jnp.arange(HEADS // 2) + core * (HEADS // 2) + 1.0).astype(WIDE) / HEADS
+    )
+    valid = lax.dynamic_slice_in_dim(valid_all, 2 * chip, 2, 0)[:, None, :]
+    scalars = in_place
+    gain = [gains_full[row : row + 1] for row in range(5)]
+
+    with jax.named_scope("forward_layers"):
+        embedded, normed = norm_forward(embedded, None, None, gain[0], scalars, False)
+        middle, lowered, kept_zero = tp_forward(
+            embedded, normed, mats_zero, gain[1], slopes, valid, scalars, last[2]
+        )
+        encoded = middle + (lowered + swap_core(lowered))
+        joined = jnp.concatenate([encoded, embedded], -1).astype(LOW)
+        joined, _ = tie((joined, last[3]))
+        bridged = piece_dot(joined, *bridge_mat, 128, 1)
+        bridged, normed = norm_forward(
+            None, bridged, swap_core(bridged), gain[2], scalars, True
+        )
+        middle, lowered, kept_one = tp_forward(
+            bridged, normed, mats_one, gain[3], slopes, valid, scalars
+        )
+        decoded = middle + (lowered + swap_core(lowered))
+
+    with jax.named_scope("readout_loss"):
+        last = pick(decoded.reshape(2, frame_count, width), core)
+        final_low = (norm_parts(last) * gains_full[4]).astype(LOW)
+        predict = jnp.dot(final_low, readout_full, preferred_element_type=WIDE)
+        target = (clean - (1.0 - SIGMA_MIN) * noise).T
+        weight = (flags * valid_own)[:, None]
+        missed = predict - target
+        loss_local = jnp.sum(weight * missed * missed)
+        count_local = jnp.sum(weight)
+        d_predict = (2.0 * weight * missed).astype(LOW)
+        d_readout = lax.dot_general(
+            final_low, d_predict, (((0,), (0,)), ((), ())), preferred_element_type=WIDE
+        )
+        d_final = lax.dot_general(
+            d_predict, readout_full, (((1,), (1,)), ((), ())), preferred_element_type=WIDE
+        )
+        back, gain_terms = norm_back(last, gains_full[4], d_final)
+        d_gain_last = jnp.sum(gain_terms, 0)
+        d_decoded = jnp.concatenate(in_order(core, back, swap_core(back)), 0)
+
+    with jax.named_scope("backward_layers"):
+        flow = Flow()
+        parts = (slopes, valid, spot, scalars, flow)
+        result, shares_one, d_gain_three = tp_backward(
+            d_decoded, d_decoded.astype(LOW), kept_one, mats_one, gain[2], gain[3], *parts
+        )
+        d_gain_two = result[3]
+        d_joined = piece_dot_back(result[2], *bridge_mat, 128)
+        d_joined, d_bridged_low = flow.turn(d_joined, result[2])
+        d_joined, g_bridge = flow.add((d_joined,), (joined, d_bridged_low, spot, True))
+        d_joined = d_joined + swap_core(d_joined)
+        d_encoded = d_joined[:, :width]
+        result, shares_zero, d_gain_one = tp_backward(
+            d_encoded, d_encoded.astype(LOW), kept_zero, mats_zero, gain[0], gain[1], *parts
+        )
+        d_gain_zero = result[3]
+        d_embedded = result[0] + d_joined[:, width:]
+        (d_embedded,) = flow.turn(d_embedded)
+
+    with jax.named_scope("embedding_back"):
+        own = pick(d_embedded.astype(LOW).reshape(2, frame_count, width), core)
+        own = own.reshape(frame_count, 32, outs).transpose(1, 0, 2)
+        own = lax.all_to_all(
+            own.reshape(32 * blocks, TAPS_OUT * outs), BOTH, 0, 0, tiled=True
+        ).astype(WIDE)
+        d_conv = jax.vjp(jax.nn.gelu, conv_out)[1](own)[0].astype(LOW)
+        padded = jnp.pad(
+            d_conv.reshape(32, blocks, TAPS_OUT * outs), ((0, 0), (2, 2), (0, 0))
+        )
+        shifted = jnp.concatenate([padded[:, 4 - i : 4 - i + blocks] for i in range(5)], -1)
+        d_start = banded_back(
+            shifted.reshape(32 * blocks, 5 * TAPS_OUT * outs), banded
+        )
+        d_start = d_start.reshape(32 * blocks, TAPS_OUT, 2, outs)
+        mine = lax.dynamic_index_in_dim(d_start, core, 2, keepdims=False)
+        other = lax.dynamic_index_in_dim(d_start, 1 - core, 2, keepdims=False)
+        other = swap_core(other.reshape(32 * blocks, TAPS_OUT * outs))
+        d_start = own + mine.reshape(32 * blocks, TAPS_OUT * outs) + other
+        d_start = d_start.reshape(32, frame_count, outs) * valid_all[:, :, None]
+        grad_input = jnp.einsum(
+            "nzv,nvr->zr", features, d_start.astype(LOW), preferred_element_type=WIDE
+        )
+        spread = banded_outer(windows, d_conv)
+        spread = spread.reshape(5 * TAPS_OUT, group, TAPS_OUT, outs)
+        grad_kernel = sum(spread[j + 1 : j + 1 + taps, :, j, :] for j in range(TAPS_OUT))
+        grad_kernel = grad_kernel.transpose(0, 2, 1)
+
+    with jax.named_scope("small_grads"):
+        d_readout, d_gain_zero, _ = tie((d_readout, d_gain_zero, d_conv))
+        d_gains = jnp.concatenate(
+            [d_gain_zero, d_gain_one, d_gain_two, d_gain_three, d_gain_last[None]], 0
+        )
+        fill = jnp.zeros((width, 1), WIDE)
+        small = jnp.concatenate([d_readout, d_gains.T, fill + loss_local, fill + count_local], 1)
+        small = jnp.pad(small, ((0, 0), (0, 128 - small.shape[1])))
+        small = lax.all_to_all(small, BOTH, 0, 0, tiled=True)
+        small = jnp.sum(small.reshape(32, width // 32, 128), 0)
+        grad_readout = small[:, :mel_count]
+        grad_gains = small[:, mel_count : mel_count + 5].T
+        loss_sum = small[0, mel_count + 5]
+        frame_total = small[0, mel_count + 6]
+
+    with jax.named_scope("own_grads"):
+        flow.turn(d_conv)
+        for share in [*shares_zero, *shares_one, g_bridge]:
+            share.total = tie((share.total, d_conv))[0].astype(WIDE)
+
+        def unfolded(both, count):
+            cut = both.reshape(2, both.shape[1], count, both.shape[2] // count)
+            return jnp.moveaxis(cut, 0, 2).reshape(both.shape[1], 2 * both.shape[2])
+
+        layer_grads = []
+        for joint_share, expand_share, reduce_share in (shares_zero, shares_one):
+            both = own_rows(joint_share.total, core)
+            layer_grads.append(
+                (
+                    unfolded(both[:, :, : 3 * LANES], 3),
+                    unfolded(both[:, :, 3 * LANES :], 1),
+                    unfolded(own_rows(expand_share.total, core), 4 * tiles),
+                    reduce_share.total,
+                )
+            )
+        grads = [
+            grad_input,
+            grad_kernel,
+            *[jnp.stack(pair) for pair in zip(*layer_grads)],
+            unfolded(own_rows(g_bridge.total, core), 1),
+            grad_readout,
+            grad_gains,
+        ]
+
+    with jax.named_scope("clip_and_update"):
+        squares_local = sum((jnp.sum(item * item) for item in grads))
+        squared = lax.all_to_all(
+            jnp.zeros((32, 128), WIDE) + squares_local, BOTH, 0, 0, tiled=True
+        )
+        squared = jnp.sum(squared[:, 0])
+        grad_norm = jnp.sqrt(squared) / frame_total
+        factor = jnp.minimum(1.0, CLIP_LIMIT / grad_norm) / frame_total
+        masters = (
+            input_master,
+            kernel_master,
+            joint_master,
+            output_master,
+            expand_master,
+            reduce_master,
+            bridge_master,
+            readout_master,
+            gains_master,
+        )
+        moments = (
+            input_moment,
+            kernel_moment,
+            joint_moment,
+            output_moment,
+            expand_moment,
+            reduce_moment,
+            bridge_moment,
+            readout_moment,
+            gains_moment,
+        )
+        squares = (
+            input_square,
+            kernel_square,
+            joint_square,
+            output_square,
+            expand_square,
+            reduce_square,
+            bridge_square,
+            readout_square,
+            gains_square,
+        )
+        decays = [DECAY_RATE] * 8 + [0.0]
+        results = []
+        for master, moment, square, grad, rate, decay in zip(
+            masters, moments, squares, grads, weight_rates(), decays
+        ):
+            results.extend(adamw(master, moment, square, factor * grad, rate, decay))
+    return (loss_sum, frame_total, grad_norm, *results)
+
+
 def solution(mesh):
     in_specs = (
         P(("dp", "fsdp"), None, None),
@@ -434,4 +1405,6 @@
         P(None, ("dp", "fsdp")),
         P(None, ("dp", "fsdp")),
     )
-    return jax.shard_map(shards, mesh=mesh, in_specs=in_specs, out_specs=out_specs, check_vma=False)
+    paired = mesh.shape["dp"] == 4 and mesh.shape["fsdp"] == 8
+    step = paired_shards if paired else shards
+    return jax.shard_map(step, mesh=mesh, in_specs=in_specs, out_specs=out_specs, check_vma=False)

time: 2970 us -> 750 us (0.25)
  waiting for transfers between devices: 2300 us -> 237 us
  matrix products: 190 us -> 9.06 us
  blocking collectives: 162 us -> 0 us
  Pallas kernels: 0 us -> 149 us
  local copies, waits for them, and re-layouts: 232 us -> 142 us
  starting transfers between devices: 1.91 us -> 90.6 us
  other arithmetic: 51.2 us -> 82.9 us
    reduce_scatter x12 -> x7, waiting for transfers between devices: 1860 us -> 11.1 us  [send(): lax.psum_scatter(self.made, 'fsdp', scatter_dimension=0, axis_index_group...]
    all_gather x10 -> x2, waiting for transfers between devices: 434 us -> 0.01 us  [in_background(): whole = lax.all_gather(own, BOTH, axis=0, axis_index_groups=same_core)]
    ppermute x0 -> x67, waiting for transfers between devices: none -> 213 us  [the longest x12 97.6 us: shift_z(): lax.ppermute(item, 'fsdp', [(i, (i + 2 * hops) % 8) for i in range(8)])]
    dot_general x47 -> x5, matrix products: 190 us -> 9.06 us  [the longest x1 3.83 us: paired_shards(): jnp.einsum('nzv,nvr->zr', features, d_start.astype(LOW), preferred_elemen...]
    pallas_call x0 -> x60, Pallas kernels: none -> 149 us  [the longest x9 29.5 us: piece_dot_back(): pl.pallas_call(body, grid_spec=pltpu.PrefetchScalarGridSpec(num_scalar_pr...]
    all_gather x3 -> x0, blocking collectives: 124 us -> none  [the longest x1 47.5 us: shards(): lax.all_gather(input_master.astype(low_type), ('dp', 'fsdp'), axis=1, til...]
    ppermute x0 -> x67, starting transfers between devices: none -> 76.1 us  [the longest x12 42.6 us: shift_z(): lax.ppermute(item, 'fsdp', [(i, (i + 2 * hops) % 8) for i in range(8)])]
    unnamed x342 -> x393, local copies, waits for them, and re-layouts: 123 us -> 69.8 us
  transfers between devices with their start and end apart: 23 -> 80, of which waited for: 19 -> 37; matrix products, arithmetic and copies ran while one was open for 13% -> 18% of each run, Pallas kernels for 0% -> 18%
where the time goes in v1:
time: 750 us; the launch traced here: 739 us
  waiting for transfers between devices  237 us (32%)
  Pallas kernels  149 us (20%)
  local copies, waits for them, and re-layouts  142 us (19%)
  starting transfers between devices  90.6 us (12%)
  other arithmetic  82.9 us (11%)
  between operations  28.3 us (4%)
  matrix products  9.06 us (1%)
    ppermute x12, waiting for transfers between devices, shift_z(): lax.ppermute(item, 'fsdp', [(i, (i + 2 * hops) % 8) for i in range(8)])  97.6 us
    unnamed x393, local copies, waits for them, and re-layouts  69.8 us
    ppermute x14, waiting for transfers between devices, swap_x(): return lax.ppermute(item, 'dp', [(i, i ^ 1) for i in range(4)])  58.6 us
    ppermute x12, starting transfers between devices, shift_z(): lax.ppermute(item, 'fsdp', [(i, (i + 2 * hops) % 8) for i in range(8)])  42.6 us
    ppermute x16, waiting for transfers between devices, swap_y(): return lax.ppermute(item, 'dp', [(i, i ^ 2) for i in range(4)])  38.1 us
    pallas_call x9, Pallas kernels, piece_dot_back(): pl.pallas_call(body, grid_spec=pltpu.PrefetchScalarGridSpec(num_scalar_pr...  29.5 us
    pallas_call x9, Pallas kernels, piece_dot(): pl.pallas_call(body, grid_spec=pltpu.PrefetchScalarGridSpec(num_scalar_pr...  29 us
    pallas_call x17, Pallas kernels, one_step(): pl.pallas_call(body, grid_spec=pltpu.PrefetchScalarGridSpec(num_scalar_pr...  28.8 us
  transfers between devices with their start and end apart: 80, of which 37 were waited for; matrix products, arithmetic and copies ran while one was open for 18% of the time, Pallas kernels for 18%

profile of v1, /device:TPU:0, one launch (start us, length us, event | category | flops | bytes accessed | tf_op | source)
XLA Modules:
  0.0 739.2 jit_solution(14015556545338047056)
XLA Ops:
  11.7 3.3 dynamic-slice_reduce_fusion.1
  22.5 5.0 collective-permute-start.2
  30.3 3.2 collective-permute-done
  36.8 7.3 collective-permute-done.3
  45.6 4.9 collective-permute-done.5
  57.7 6.8 collective-permute-done.10
  64.5 3.7 collective-permute-start.11
  69.0 6.4 copy.459
  75.3 7.4 reshape.414.refs_1_
  85.1 2.8 collective-permute-start.12
  94.1 7.1 collective-permute-done.12
  109.4 7.7 %collective-permute-done.20 = bf16[256,512]{1,0:T(8,128)(2,1)} collective-permute-done((bf16[256,512]{1,0:T(8,128)(2,1)S(1)}, bf16[256,512]{1,0:T(8,128)(2,1)}, u32[]{:S(2)}, u32[]{:S(2)}) %collective-permute-start.20) | collective-permute-done | bytes 262176 | tf_op jit(solution)/shard_map/weights/ppermute | solution.py:396
  117.1 4.4 collective-permute-start.21
  125.3 3.2 copy.412
  130.6 4.5 collective-permute-done.21
  135.2 9.2 %collective-permute-start.22 = (bf16[256,512]{1,0:T(8,128)(2,1)}, bf16[256,512]{1,0:T(8,128)(2,1)S(1)}, u32[]{:S(2)}, u32[]{:S(2)}) collective-permute-start(bf16[256,512]{1,0:T(8,128)(2,1)} %collective-permute-done.21), channel_id=1, source_target_pairs={{0,2},{1,3},{2,4},{3,5},{4,6},{5,7},{6,0},{7,1},{8,10},{9,11},{10,... | collective-permute-start | bytes 786440 | tf_op jit(solution)/shard_map/weights/ppermute | solution.py:396
  145.2 3.5 all-to-all-start
  150.1 5.9 collective-permute-done.22
  158.1 5.5 collective-permute-start.23
  166.8 5.0 all-to-all-done
  177.0 23.2 %collective-permute-done.23 = bf16[1024,512]{1,0:T(8,128)(2,1)} collective-permute-done((bf16[1024,512]{1,0:T(8,128)(2,1)S(1)}, bf16[1024,512]{1,0:T(8,128)(2,1)}, u32[]{:S(2)}, u32[]{:S(2)}) %collective-permute-start.23) | collective-permute-done | bytes 1048608 | tf_op jit(solution)/shard_map/weights/ppermute | solution.py:396
  200.2 8.5 %collective-permute-start.24 = (bf16[1024,512]{1,0:T(8,128)(2,1)}, bf16[1024,512]{1,0:T(8,128)(2,1)S(1)}, u32[]{:S(2)}, u32[]{:S(2)}) collective-permute-start(bf16[1024,512]{1,0:T(8,128)(2,1)} %collective-permute-done.23), channel_id=1, source_target_pairs={{0,2},{1,3},{2,4},{3,5},{4,6},{5,7},{6,0},{7,1},{8,10},{9,11},{10,... | collective-permute-start | bytes 3145736 | tf_op jit(solution)/shard_map/weights/ppermute | solution.py:396
  208.7 3.8 collective-permute-done.15
  217.3 6.4 forward_layers.17
  232.3 3.5 forward_layers.20
  240.0 4.4 copy-done
  250.2 36.3 %collective-permute-done.30 = bf16[1024,512]{1,0:T(8,128)(2,1)} collective-permute-done((bf16[1024,512]{1,0:T(8,128)(2,1)S(1)}, bf16[1024,512]{1,0:T(8,128)(2,1)}, u32[]{:S(2)}, u32[]{:S(2)}) %collective-permute-start.30) | collective-permute-done | bytes 1048608 | tf_op jit(solution)/shard_map/weights/ppermute | solution.py:396
  290.8 10.9 %forward_layers.24.joint_ref = bf16[256,1536]{1,0:T(8,128)(2,1)S(1)} custom-call(s32[17]{0:T(128)S(1)} %stack.229.scalars_ref.places_ref, bf16[256,1024]{1,0:T(8,128)(2,1)S(1)} %get-tuple-element.177.rows_ref.left_ref, bf16[16,640,512]{2,1,0:T(8,128)(2,1)S(1)} %bitcast.363), custom_call_target="tpu_custom_call" | custom-call | flops 1000 | bytes 1000 | tf_op jit(solution)/shard_map/forward_layers/pallas_call | solution.py:443
  301.8 6.4 forward_layers.25
  310.0 4.0 copy-done.2
  315.5 3.4 pad_maximum_fusion.2
  323.1 3.5 forward_layers.28
  341.1 4.2 backward_layers.42.grads_ref.right_ref
  345.5 3.5 backward_layers.43.mine_ref
  357.6 19.5 %collective-permute-done.37.far_left_ref.far_right_ref = bf16[256,2048]{1,0:T(8,128)(2,1)S(1)} collective-permute-done((bf16[256,2048]{1,0:T(8,128)(2,1)S(1)}, bf16[256,2048]{1,0:T(8,128)(2,1)S(1)}, u32[]{:S(2)}, u32[]{:S(2)}) %collective-permute-start.37) | collective-permute-done | bytes 1048608 | tf_op jit(solution)/shard_map/backward_layers/ppermute | solution.py:384
  377.0 4.2 collective-permute-done.38.far_left_ref.far_right_ref
  389.3 8.4 %backward_layers.50.grads_ref.right_ref = bf16[256,1536]{1,0:T(8,128)(2,1)S(1)} custom-call(f32[8]{0:T(128)S(1)} %multiply_power_fusion.slopes_ref, bf16[256,1536]{1,0:T(8,128)(2,1)S(1)} %copy-done.46, f32[256,512]{1,0:T(8,128)S(1)} %get-tuple-element.198.mine_ref, f32[256,512]{1,0:T(8,128)S(1)} %collective-permute-done.39.other_ref, ...), custom_call_target="tpu_custom_call" | custom-call | flops 1000 | bytes 1000 | tf_op jit(solution)/shard_map/backward_layers/pallas_call | solution.py:688
  399.1 3.8 backward_layers.51.mine_ref
  402.9 5.6 collective-permute-done.40
  410.7 3.2 add_convert_fusion.3
  421.0 4.1 backward_layers.56
  425.1 4.1 copy-done.3
  432.0 9.3 %collective-permute-done.44.far_left_ref.far_right_ref = bf16[256,2048]{1,0:T(8,128)(2,1)S(1)} collective-permute-done((bf16[256,2048]{1,0:T(8,128)(2,1)}, bf16[256,2048]{1,0:T(8,128)(2,1)S(1)}, u32[]{:S(2)}, u32[]{:S(2)}) %collective-permute-start.44) | collective-permute-done | bytes 1048608 | tf_op jit(solution)/shard_map/backward_layers/ppermute | solution.py:388
  449.9 2.9 add.577
  452.9 4.8 copy-done.4
  457.7 4.6 backward_layers.61.grads_ref.right_ref
  466.5 4.5 backward_layers.62.mine_ref
  484.9 4.0 backward_layers.68
  493.3 22.9 %collective-permute-done.50 = bf16[512,512]{1,0:T(8,128)(2,1)} collective-permute-done((bf16[512,512]{1,0:T(8,128)(2,1)}, bf16[512,512]{1,0:T(8,128)(2,1)}, u32[]{:S(2)}, u32[]{:S(2)}) %collective-permute-start.50) | collective-permute-done | bytes 524320 | tf_op jit(solution)/shard_map/backward_layers/ppermute | solution.py:384
  517.3 2.9 backward_layers.71
  532.4 8.6 %backward_layers.73.grads_ref.right_ref = bf16[256,1536]{1,0:T(8,128)(2,1)S(1)} custom-call(f32[8]{0:T(128)S(1)} %multiply_power_fusion.slopes_ref, bf16[256,1536]{1,0:T(8,128)(2,1)S(1)} %copy-done.48, f32[256,512]{1,0:T(8,128)S(1)} %copy-done.87, f32[256,512]{1,0:T(8,128)S(1)} %copy-done.89, f32[2,1,128]{2,1,0:T(1,128)S(1)} %constant_dynamic-slice_fusion.3.valid_ref), custom_call_target="tpu_custom_call" | custom-call | flops 1000 | bytes 1000 | tf_op jit(solution)/shard_map/backward_layers/pallas_call | solution.py:688
  547.7 3.8 backward_layers.74.mine_ref
  554.1 3.2 add_convert_fusion
  563.2 3.5 backward_layers.79
  567.7 8.1 %collective-permute-done.57.far_left_ref.far_right_ref = bf16[256,1024]{1,0:T(8,128)(2,1)S(1)} collective-permute-done((bf16[256,1024]{1,0:T(8,128)(2,1)}, bf16[256,1024]{1,0:T(8,128)(2,1)S(1)}, u32[]{:S(2)}, u32[]{:S(2)}) %collective-permute-start.57) | collective-permute-done | bytes 524320 | tf_op jit(solution)/shard_map/backward_layers/ppermute | solution.py:384
  575.8 10.3 %collective-permute-done.58.far_left_ref.far_right_ref = bf16[256,2048]{1,0:T(8,128)(2,1)S(1)} collective-permute-done((bf16[256,2048]{1,0:T(8,128)(2,1)}, bf16[256,2048]{1,0:T(8,128)(2,1)S(1)}, u32[]{:S(2)}, u32[]{:S(2)}) %collective-permute-start.58) | collective-permute-done | bytes 1048608 | tf_op jit(solution)/shard_map/backward_layers/ppermute | solution.py:388
  597.6 3.3 all-to-all-start.1
  620.3 3.7 all-to-all-start.2
  636.4 2.9 reshape.372
  639.2 4.3 multiply_reduce_fusion.2
  662.1 3.8 multiply_reduce_fusion.9
  671.4 11.1 %reduce-scatter.16.cloned.1.call-done = bf16[64,2048]{1,0:T(8,128)(2,1)} async-done(((bf16[256,2048]{1,0:T(8,128)(2,1)}), bf16[64,2048]{1,0:T(8,128)(2,1)}) %reduce-scatter.16.cloned.1.call-update) | async-done | bytes 262160 | tf_op jit(solution)/shard_map/own_grads/reduce_scatter | solution.py:889
  698.5 3.6 all-to-all-start.3
  703.3 5.9 all-to-all-done.3
  (775 shorter events, 297.4 us)
Async XLA Ops:
  7.2 232.8 %all-gather.6.cloned.1.call-start = ((), (), s32[]{:S(2)}) async-start(), calls=%async_computation.19 | async-start | bytes 11141120 | tf_op jit(solution)/shard_map/weights/all_gather | solution.py:1113
  20.7 300.2 %all-gather.4.cloned.1.call-start = ((), (), s32[]{:S(2)}) async-start(), calls=%async_computation.11 | async-start | bytes 4456448 | tf_op jit(solution)/shard_map/weights/all_gather | solution.py:1113
  22.5 11.0 %collective-permute-start.2 = (bf16[208,128]{1,0:T(8,128)(2,1)S(1)}, bf16[208,128]{1,0:T(8,128)(2,1)S(1)}, u32[]{:S(2)}, u32[]{:S(2)}) collective-permute-start(bf16[208,128]{1,0:T(8,128)(2,1)S(1)} %concatenate.105), channel_id=1, source_target_pairs={{0,6},{1,7},{2,0},{3,1},{4,2},{5,3},{6,4},{7,5},{8,14},{9,15},{10,... | collective-permute-start | bytes 159752 | tf_op jit(solution)/shard_map/features/ppermute | solution.py:396
  27.5 6.0 collective-permute-start.1
  27.5 6.0 collective-permute-start
  28.5 54.4 %collective-permute-start.7 = (bf16[256,32]{0,1:T(8,128)(2,1)S(1)}, bf16[256,32]{0,1:T(8,128)(2,1)S(1)}, u32[]{:S(2)}, u32[]{:S(2)}) collective-permute-start(bf16[256,32]{0,1:T(8,128)(2,1)S(1)} %convert_element_type.224), channel_id=1, source_target_pairs={{0,1},{1,0},{2,3},{3,2},{4,5},{5,4},{6,7},{7,6},{8,9},{9,8},{10,11... | collective-permute-start | bytes 49160 | tf_op jit(solution)/shard_map/embedding/ppermute | solution.py:392
  33.6 12.0 %collective-permute-start.4 = (bf16[4,208,128]{2,1,0:T(8,128)(2,1)S(1)}, bf16[4,208,128]{2,1,0:T(8,128)(2,1)S(1)}, u32[]{:S(2)}, u32[]{:S(2)}) collective-permute-start(bf16[4,208,128]{2,1,0:T(8,128)(2,1)S(1)} %bitcast_dynamic-update-slice_fusion.4), channel_id=1, source_target_pairs={{0,16},{8,24},{16,0},{24,8},{1,17},{9,25},{17,1},{25,9},{2,18},{10... | collective-permute-start | bytes 638984 | tf_op jit(solution)/shard_map/features/ppermute | solution.py:388
  35.1 8.9 %collective-permute-start.3 = (bf16[4,208,128]{2,1,0:T(8,128)(2,1)S(1)}, bf16[4,208,128]{2,1,0:T(8,128)(2,1)S(1)}, u32[]{:S(2)}, u32[]{:S(2)}) collective-permute-start(bf16[4,208,128]{2,1,0:T(8,128)(2,1)S(1)} %bitcast_dynamic-update-slice_fusion.4), channel_id=1, source_target_pairs={{0,8},{8,0},{16,24},{24,16},{1,9},{9,1},{17,25},{25,17},{2,10},{10... | collective-permute-start | bytes 638984 | tf_op jit(solution)/shard_map/features/ppermute | solution.py:384
  44.1 6.5 collective-permute-start.5
  50.6 37.3 %collective-permute-start.6 = (bf16[16,208,128]{2,1,0:T(8,128)(2,1)S(1)}, bf16[16,208,128]{2,1,0:T(8,128)(2,1)}, u32[]{:S(2)}, u32[]{:S(2)}) collective-permute-start(bf16[16,208,128]{2,1,0:T(8,128)(2,1)S(1)} %bitcast.392), channel_id=1, source_target_pairs={{0,1},{1,0},{2,3},{3,2},{4,5},{5,4},{6,7},{7,6},{8,9},{9,8},{10,11... | collective-permute-start | bytes 2555912 | tf_op jit(solution)/shard_map/features/ppermute | solution.py:392
  52.2 12.3 %collective-permute-start.10 = (bf16[256,512]{1,0:T(8,128)(2,1)S(1)}, bf16[256,512]{1,0:T(8,128)(2,1)S(1)}, u32[]{:S(2)}, u32[]{:S(2)}) collective-permute-start(bf16[256,512]{1,0:T(8,128)(2,1)S(1)} %bitcast.429), channel_id=1, source_target_pairs={{0,2},{1,3},{2,4},{3,5},{4,6},{5,7},{6,0},{7,1},{8,10},{9,11},{10,... | collective-permute-start | bytes 786440 | tf_op jit(solution)/shard_map/weights/ppermute | solution.py:396
  57.0 26.0 %collective-permute-start.17 = (bf16[256,512]{1,0:T(8,128)(2,1)}, bf16[256,512]{1,0:T(8,128)(2,1)}, u32[]{:S(2)}, u32[]{:S(2)}) collective-permute-start(bf16[256,512]{1,0:T(8,128)(2,1)} %bitcast.72), channel_id=1, source_target_pairs={{0,8},{8,0},{16,24},{24,16},{1,9},{9,1},{17,25},{25,17},{2,10},{10... | collective-permute-start | bytes 786440 | tf_op jit(solution)/shard_map/weights/ppermute | solution.py:384
  64.5 20.5 %collective-permute-start.11 = (bf16[256,512]{1,0:T(8,128)(2,1)S(1)}, bf16[256,512]{1,0:T(8,128)(2,1)}, u32[]{:S(2)}, u32[]{:S(2)}) collective-permute-start(bf16[256,512]{1,0:T(8,128)(2,1)S(1)} %collective-permute-done.10), channel_id=1, source_target_pairs={{0,2},{1,3},{2,4},{3,5},{4,6},{5,7},{6,0},{7,1},{8,10},{9,11},{10,... | collective-permute-start | bytes 786440 | tf_op jit(solution)/shard_map/weights/ppermute | solution.py:396
  82.9 65.9 %collective-permute-start.18 = (bf16[256,512]{1,0:T(8,128)(2,1)}, bf16[256,512]{1,0:T(8,128)(2,1)}, u32[]{:S(2)}, u32[]{:S(2)}) collective-permute-start(bf16[256,512]{1,0:T(8,128)(2,1)} %bitcast.72), channel_id=1, source_target_pairs={{0,16},{8,24},{16,0},{24,8},{1,17},{9,25},{17,1},{25,9},{2,18},{10... | collective-permute-start | bytes 786440 | tf_op jit(solution)/shard_map/weights/ppermute | solution.py:388
  83.0 65.8 %collective-permute-start.19 = (bf16[256,512]{1,0:T(8,128)(2,1)}, bf16[256,512]{1,0:T(8,128)(2,1)}, u32[]{:S(2)}, u32[]{:S(2)}) collective-permute-start(bf16[256,512]{1,0:T(8,128)(2,1)} %collective-permute-done.17), channel_id=1, source_target_pairs={{0,16},{8,24},{16,0},{24,8},{1,17},{9,25},{17,1},{25,9},{2,18},{10... | collective-permute-start | bytes 786440 | tf_op jit(solution)/shard_map/weights/ppermute | solution.py:388
  85.1 16.1 %collective-permute-start.12 = (bf16[256,512]{1,0:T(8,128)(2,1)}, bf16[256,512]{1,0:T(8,128)(2,1)}, u32[]{:S(2)}, u32[]{:S(2)}) collective-permute-start(bf16[256,512]{1,0:T(8,128)(2,1)} %collective-permute-done.11), channel_id=1, source_target_pairs={{0,2},{1,3},{2,4},{3,5},{4,6},{5,7},{6,0},{7,1},{8,10},{9,11},{10,... | collective-permute-start | bytes 786440 | tf_op jit(solution)/shard_map/weights/ppermute | solution.py:396
  103.3 13.8 %collective-permute-start.20 = (bf16[256,512]{1,0:T(8,128)(2,1)S(1)}, bf16[256,512]{1,0:T(8,128)(2,1)}, u32[]{:S(2)}, u32[]{:S(2)}) collective-permute-start(bf16[256,512]{1,0:T(8,128)(2,1)S(1)} %bitcast.427), channel_id=1, source_target_pairs={{0,2},{1,3},{2,4},{3,5},{4,6},{5,7},{6,0},{7,1},{8,10},{9,11},{10,... | collective-permute-start | bytes 786440 | tf_op jit(solution)/shard_map/weights/ppermute | solution.py:396
  103.7 54.4 %collective-permute-start.14 = (bf16[1024,512]{1,0:T(8,128)(2,1)}, bf16[1024,512]{1,0:T(8,128)(2,1)}, u32[]{:S(2)}, u32[]{:S(2)}) collective-permute-start(bf16[1024,512]{1,0:T(8,128)(2,1)} %pad_maximum_fusion.10), channel_id=1, source_target_pairs={{0,16},{8,24},{16,0},{24,8},{1,17},{9,25},{17,1},{25,9},{2,18},{10... | collective-permute-start | bytes 3145736 | tf_op jit(solution)/shard_map/weights/ppermute | solution.py:388
  104.9 53.2 %collective-permute-start.13 = (bf16[1024,512]{1,0:T(8,128)(2,1)}, bf16[1024,512]{1,0:T(8,128)(2,1)}, u32[]{:S(2)}, u32[]{:S(2)}) collective-permute-start(bf16[1024,512]{1,0:T(8,128)(2,1)} %pad_maximum_fusion.10), channel_id=1, source_target_pairs={{0,8},{8,0},{16,24},{24,16},{1,9},{9,1},{17,25},{25,17},{2,10},{10... | collective-permute-start | bytes 3145736 | tf_op jit(solution)/shard_map/weights/ppermute | solution.py:384
  117.1 18.1 %collective-permute-start.21 = (bf16[256,512]{1,0:T(8,128)(2,1)}, bf16[256,512]{1,0:T(8,128)(2,1)}, u32[]{:S(2)}, u32[]{:S(2)}) collective-permute-start(bf16[256,512]{1,0:T(8,128)(2,1)} %collective-permute-done.20), channel_id=1, source_target_pairs={{0,2},{1,3},{2,4},{3,5},{4,6},{5,7},{6,0},{7,1},{8,10},{9,11},{10,... | collective-permute-start | bytes 786440 | tf_op jit(solution)/shard_map/weights/ppermute | solution.py:396
  135.2 20.9 %collective-permute-start.22 = (bf16[256,512]{1,0:T(8,128)(2,1)}, bf16[256,512]{1,0:T(8,128)(2,1)S(1)}, u32[]{:S(2)}, u32[]{:S(2)}) collective-permute-start(bf16[256,512]{1,0:T(8,128)(2,1)} %collective-permute-done.21), channel_id=1, source_target_pairs={{0,2},{1,3},{2,4},{3,5},{4,6},{5,7},{6,0},{7,1},{8,10},{9,11},{10,... | collective-permute-start | bytes 786440 | tf_op jit(solution)/shard_map/weights/ppermute | solution.py:396
  145.2 26.6 %all-to-all-start = ((bf16[32,16,256]{2,1,0:T(8,128)(2,1)}), bf16[32,16,256]{2,1,0:T(8,128)(2,1)S(1)}, u32[]{:S(2)}, u32[]{:S(2)}) async-start(bf16[32,16,256]{2,1,0:T(8,128)(2,1)} %bitcast.36), calls=%async_computation | async-start | bytes 524288 | tf_op jit(solution)/shard_map/embedding/all_to_all | solution.py:1149
  148.8 344.6 %reduce-scatter.8.cloned.1.call-start = ((), (), s32[]{:S(2)}) async-start(), calls=%async_computation.12 | async-start | bytes 1310720 | tf_op jit(solution)/shard_map/backward_layers/reduce_scatter | solution.py:889
  158.1 50.6 %collective-permute-start.27 = (bf16[1024,512]{1,0:T(8,128)(2,1)}, bf16[1024,512]{1,0:T(8,128)(2,1)}, u32[]{:S(2)}, u32[]{:S(2)}) collective-permute-start(bf16[1024,512]{1,0:T(8,128)(2,1)} %pad_maximum_fusion.12), channel_id=1, source_target_pairs={{0,16},{8,24},{16,0},{24,8},{1,17},{9,25},{17,1},{25,9},{2,18},{10... | collective-permute-start | bytes 3145736 | tf_op jit(solution)/shard_map/weights/ppermute | solution.py:388
  158.1 42.1 %collective-permute-start.23 = (bf16[1024,512]{1,0:T(8,128)(2,1)S(1)}, bf16[1024,512]{1,0:T(8,128)(2,1)}, u32[]{:S(2)}, u32[]{:S(2)}) collective-permute-start(bf16[1024,512]{1,0:T(8,128)(2,1)S(1)} %pad_maximum_fusion.11), channel_id=1, source_target_pairs={{0,2},{1,3},{2,4},{3,5},{4,6},{5,7},{6,0},{7,1},{8,10},{9,11},{10,... | collective-permute-start | bytes 3145736 | tf_op jit(solution)/shard_map/weights/ppermute | solution.py:396
  163.7 48.9 %collective-permute-start.15 = (bf16[1024,512]{1,0:T(8,128)(2,1)}, bf16[1024,512]{1,0:T(8,128)(2,1)}, u32[]{:S(2)}, u32[]{:S(2)}) collective-permute-start(bf16[1024,512]{1,0:T(8,128)(2,1)} %collective-permute-done.13), channel_id=1, source_target_pairs={{0,16},{8,24},{16,0},{24,8},{1,17},{9,25},{17,1},{25,9},{2,18},{10... | collective-permute-start | bytes 3145736 | tf_op jit(solution)/shard_map/weights/ppermute | solution.py:388
  175.6 53.6 %collective-permute-start.26 = (bf16[1024,512]{1,0:T(8,128)(2,1)}, bf16[1024,512]{1,0:T(8,128)(2,1)S(1)}, u32[]{:S(2)}, u32[]{:S(2)}) collective-permute-start(bf16[1024,512]{1,0:T(8,128)(2,1)} %pad_maximum_fusion.12), channel_id=1, source_target_pairs={{0,8},{8,0},{16,24},{24,16},{1,9},{9,1},{17,25},{25,17},{2,10},{10... | collective-permute-start | bytes 3145736 | tf_op jit(solution)/shard_map/weights/ppermute | solution.py:384
  200.2 29.0 %collective-permute-start.24 = (bf16[1024,512]{1,0:T(8,128)(2,1)}, bf16[1024,512]{1,0:T(8,128)(2,1)S(1)}, u32[]{:S(2)}, u32[]{:S(2)}) collective-permute-start(bf16[1024,512]{1,0:T(8,128)(2,1)} %collective-permute-done.23), channel_id=1, source_target_pairs={{0,2},{1,3},{2,4},{3,5},{4,6},{5,7},{6,0},{7,1},{8,10},{9,11},{10,... | collective-permute-start | bytes 3145736 | tf_op jit(solution)/shard_map/weights/ppermute | solution.py:396
  208.7 20.5 %collective-permute-start.28 = (bf16[1024,512]{1,0:T(8,128)(2,1)}, bf16[1024,512]{1,0:T(8,128)(2,1)S(1)}, u32[]{:S(2)}, u32[]{:S(2)}) collective-permute-start(bf16[1024,512]{1,0:T(8,128)(2,1)} %collective-permute-done.27), channel_id=1, source_target_pairs={{0,8},{8,0},{16,24},{24,16},{1,9},{9,1},{17,25},{25,17},{2,10},{10... | collective-permute-start | bytes 3145736 | tf_op jit(solution)/shard_map/weights/ppermute | solution.py:384
  247.2 39.3 %collective-permute-start.30 = (bf16[1024,512]{1,0:T(8,128)(2,1)S(1)}, bf16[1024,512]{1,0:T(8,128)(2,1)}, u32[]{:S(2)}, u32[]{:S(2)}) collective-permute-start(bf16[1024,512]{1,0:T(8,128)(2,1)S(1)} %copy-done.137), channel_id=1, source_target_pairs={{0,2},{1,3},{2,4},{3,5},{4,6},{5,7},{6,0},{7,1},{8,10},{9,11},{10,... | collective-permute-start | bytes 3145736 | tf_op jit(solution)/shard_map/weights/ppermute | solution.py:396
  350.3 30.9 %collective-permute-start.38 = (bf16[256,2560]{1,0:T(8,128)(2,1)S(1)}, bf16[256,2560]{1,0:T(8,128)(2,1)S(1)}, u32[]{:S(2)}, u32[]{:S(2)}) collective-permute-start(bf16[256,2560]{1,0:T(8,128)(2,1)S(1)} %backward_layers.45), channel_id=1, source_target_pairs={{0,16},{8,24},{16,0},{24,8},{1,17},{9,25},{17,1},{25,9},{2,18},{10... | collective-permute-start | bytes 3932168 | tf_op jit(solution)/shard_map/backward_layers/ppermute | solution.py:388
  351.5 25.6 %collective-permute-start.37 = (bf16[256,2048]{1,0:T(8,128)(2,1)S(1)}, bf16[256,2048]{1,0:T(8,128)(2,1)S(1)}, u32[]{:S(2)}, u32[]{:S(2)}) collective-permute-start(bf16[256,2048]{1,0:T(8,128)(2,1)S(1)} %backward_layers.44), channel_id=1, source_target_pairs={{0,8},{8,0},{16,24},{24,16},{1,9},{9,1},{17,25},{25,17},{2,10},{10... | collective-permute-start | bytes 3145736 | tf_op jit(solution)/shard_map/backward_layers/ppermute | solution.py:384
  384.0 24.4 %collective-permute-start.40 = (bf16[512,1024]{1,0:T(8,128)(2,1)S(1)}, bf16[512,1024]{1,0:T(8,128)(2,1)S(1)}, u32[]{:S(2)}, u32[]{:S(2)}) collective-permute-start(bf16[512,1024]{1,0:T(8,128)(2,1)S(1)} %backward_layers.48), channel_id=1, source_target_pairs={{0,16},{8,24},{16,0},{24,8},{1,17},{9,25},{17,1},{25,9},{2,18},{10... | collective-permute-start | bytes 3145736 | tf_op jit(solution)/shard_map/backward_layers/ppermute | solution.py:388
  385.2 24.1 %collective-permute-start.41 = (bf16[256,2048]{1,0:T(8,128)(2,1)S(1)}, bf16[256,2048]{1,0:T(8,128)(2,1)S(1)}, u32[]{:S(2)}, u32[]{:S(2)}) collective-permute-start(bf16[256,2048]{1,0:T(8,128)(2,1)S(1)} %backward_layers.49), channel_id=1, source_target_pairs={{0,8},{8,0},{16,24},{24,16},{1,9},{9,1},{17,25},{25,17},{2,10},{10... | collective-permute-start | bytes 3145736 | tf_op jit(solution)/shard_map/backward_layers/ppermute | solution.py:384
  415.5 25.8 %collective-permute-start.44 = (bf16[256,2048]{1,0:T(8,128)(2,1)}, bf16[256,2048]{1,0:T(8,128)(2,1)S(1)}, u32[]{:S(2)}, u32[]{:S(2)}) collective-permute-start(bf16[256,2048]{1,0:T(8,128)(2,1)} %backward_layers.55), channel_id=1, source_target_pairs={{0,16},{8,24},{16,0},{24,8},{1,17},{9,25},{17,1},{25,9},{2,18},{10... | collective-permute-start | bytes 3145736 | tf_op jit(solution)/shard_map/backward_layers/ppermute | solution.py:388
  416.6 76.7 %reduce-scatter.10.cloned.1.call-start = ((), (), s32[]{:S(2)}) async-start(), calls=%async_computation.13 | async-start | bytes 1310720 | tf_op jit(solution)/shard_map/backward_layers/reduce_scatter | solution.py:889
  416.7 15.3 %collective-permute-start.43 = (bf16[256,1024]{1,0:T(8,128)(2,1)}, bf16[256,1024]{1,0:T(8,128)(2,1)S(1)}, u32[]{:S(2)}, u32[]{:S(2)}) collective-permute-start(bf16[256,1024]{1,0:T(8,128)(2,1)} %copy-done.84), channel_id=1, source_target_pairs={{0,8},{8,0},{16,24},{24,16},{1,9},{9,1},{17,25},{25,17},{2,10},{10... | collective-permute-start | bytes 1572872 | tf_op jit(solution)/shard_map/backward_layers/ppermute | solution.py:384
  445.4 4.5 collective-permute-start.45
  445.4 26.7 %collective-permute-start.48 = (bf16[256,1536]{1,0:T(8,128)(2,1)}, bf16[256,1536]{1,0:T(8,128)(2,1)}, u32[]{:S(2)}, u32[]{:S(2)}) collective-permute-start(bf16[256,1536]{1,0:T(8,128)(2,1)} %backward_layers.60), channel_id=1, source_target_pairs={{0,16},{8,24},{16,0},{24,8},{1,17},{9,25},{17,1},{25,9},{2,18},{10... | collective-permute-start | bytes 2359304 | tf_op jit(solution)/shard_map/backward_layers/ppermute | solution.py:388
  446.5 25.6 %collective-permute-start.47 = (bf16[256,1536]{1,0:T(8,128)(2,1)}, bf16[256,1536]{1,0:T(8,128)(2,1)}, u32[]{:S(2)}, u32[]{:S(2)}) collective-permute-start(bf16[256,1536]{1,0:T(8,128)(2,1)} %backward_layers.59), channel_id=1, source_target_pairs={{0,8},{8,0},{16,24},{24,16},{1,9},{9,1},{17,25},{25,17},{2,10},{10... | collective-permute-start | bytes 2359304 | tf_op jit(solution)/shard_map/backward_layers/ppermute | solution.py:384
  447.4 120.3 %reduce-scatter.12.cloned.1.call-start = ((), (), s32[]{:S(2)}) async-start(), calls=%async_computation.14 | async-start | bytes 1310720 | tf_op jit(solution)/shard_map/backward_layers/reduce_scatter | solution.py:889
  447.4 24.7 %collective-permute-start.46 = (bf16[256,512]{1,0:T(8,128)(2,1)}, bf16[256,512]{1,0:T(8,128)(2,1)S(1)}, u32[]{:S(2)}, u32[]{:S(2)}) collective-permute-start(bf16[256,512]{1,0:T(8,128)(2,1)} %copy-done.90), channel_id=1, source_target_pairs={{0,16},{8,24},{16,0},{24,8},{1,17},{9,25},{17,1},{25,9},{2,18},{10... | collective-permute-start | bytes 786440 | tf_op jit(solution)/shard_map/backward_layers/ppermute | solution.py:388
  478.1 38.2 %collective-permute-start.52 = (bf16[256,2560]{1,0:T(8,128)(2,1)}, bf16[256,2560]{1,0:T(8,128)(2,1)S(1)}, u32[]{:S(2)}, u32[]{:S(2)}) collective-permute-start(bf16[256,2560]{1,0:T(8,128)(2,1)} %backward_layers.67), channel_id=1, source_target_pairs={{0,16},{8,24},{16,0},{24,8},{1,17},{9,25},{17,1},{25,9},{2,18},{10... | collective-permute-start | bytes 3932168 | tf_op jit(solution)/shard_map/backward_layers/ppermute | solution.py:388
  479.1 5.8 collective-permute-start.49
  479.1 37.1 %collective-permute-start.51 = (bf16[256,2048]{1,0:T(8,128)(2,1)}, bf16[256,2048]{1,0:T(8,128)(2,1)}, u32[]{:S(2)}, u32[]{:S(2)}) collective-permute-start(bf16[256,2048]{1,0:T(8,128)(2,1)} %backward_layers.66), channel_id=1, source_target_pairs={{0,8},{8,0},{16,24},{24,16},{1,9},{9,1},{17,25},{25,17},{2,10},{10... | collective-permute-start | bytes 3145736 | tf_op jit(solution)/shard_map/backward_layers/ppermute | solution.py:384
  479.9 169.2 %reduce-scatter.14.cloned.1.call-start = ((), (), s32[]{:S(2)}) async-start(), calls=%async_computation.15 | async-start | bytes 655360 | tf_op jit(solution)/shard_map/backward_layers/reduce_scatter | solution.py:889
  479.9 36.3 %collective-permute-start.50 = (bf16[512,512]{1,0:T(8,128)(2,1)}, bf16[512,512]{1,0:T(8,128)(2,1)}, u32[]{:S(2)}, u32[]{:S(2)}) collective-permute-start(bf16[512,512]{1,0:T(8,128)(2,1)} %copy-done.85), channel_id=1, source_target_pairs={{0,8},{8,0},{16,24},{24,16},{1,9},{9,1},{17,25},{25,17},{2,10},{10... | collective-permute-start | bytes 1572872 | tf_op jit(solution)/shard_map/backward_layers/ppermute | solution.py:384
  524.9 26.6 %collective-permute-start.54 = (bf16[512,1024]{1,0:T(8,128)(2,1)}, bf16[512,1024]{1,0:T(8,128)(2,1)}, u32[]{:S(2)}, u32[]{:S(2)}) collective-permute-start(bf16[512,1024]{1,0:T(8,128)(2,1)} %backward_layers.71), channel_id=1, source_target_pairs={{0,16},{8,24},{16,0},{24,8},{1,17},{9,25},{17,1},{25,9},{2,18},{10... | collective-permute-start | bytes 3145736 | tf_op jit(solution)/shard_map/backward_layers/ppermute | solution.py:388
  525.8 25.6 %collective-permute-start.55 = (bf16[256,2048]{1,0:T(8,128)(2,1)}, bf16[256,2048]{1,0:T(8,128)(2,1)}, u32[]{:S(2)}, u32[]{:S(2)}) collective-permute-start(bf16[256,2048]{1,0:T(8,128)(2,1)} %backward_layers.72), channel_id=1, source_target_pairs={{0,8},{8,0},{16,24},{24,16},{1,9},{9,1},{17,25},{25,17},{2,10},{10... | collective-permute-start | bytes 3145736 | tf_op jit(solution)/shard_map/backward_layers/ppermute | solution.py:384
  526.5 132.9 %reduce-scatter.18.cloned.1.call-start = ((), (), s32[]{:S(2)}) async-start(), calls=%async_computation.17 | async-start | bytes 1310720 | tf_op jit(solution)/shard_map/backward_layers/reduce_scatter | solution.py:889
  560.4 25.7 %collective-permute-start.58 = (bf16[256,2048]{1,0:T(8,128)(2,1)}, bf16[256,2048]{1,0:T(8,128)(2,1)S(1)}, u32[]{:S(2)}, u32[]{:S(2)}) collective-permute-start(bf16[256,2048]{1,0:T(8,128)(2,1)} %backward_layers.78), channel_id=1, source_target_pairs={{0,16},{8,24},{16,0},{24,8},{1,17},{9,25},{17,1},{25,9},{2,18},{10... | collective-permute-start | bytes 3145736 | tf_op jit(solution)/shard_map/backward_layers/ppermute | solution.py:388
  561.6 14.2 %collective-permute-start.57 = (bf16[256,1024]{1,0:T(8,128)(2,1)}, bf16[256,1024]{1,0:T(8,128)(2,1)S(1)}, u32[]{:S(2)}, u32[]{:S(2)}) collective-permute-start(bf16[256,1024]{1,0:T(8,128)(2,1)} %backward_layers.77), channel_id=1, source_target_pairs={{0,8},{8,0},{16,24},{24,16},{1,9},{9,1},{17,25},{25,17},{2,10},{10... | collective-permute-start | bytes 1572872 | tf_op jit(solution)/shard_map/backward_layers/ppermute | solution.py:384
  597.6 13.7 %all-to-all-start.1 = ((bf16[32,16,256]{2,1,0:T(8,128)(2,1)}), bf16[32,16,256]{2,1,0:T(8,128)(2,1)}, u32[]{:S(2)}, u32[]{:S(2)}) async-start(bf16[32,16,256]{2,1,0:T(8,128)(2,1)} %all_to_all.26), calls=%async_computation.4 | async-start | bytes 524288 | tf_op jit(solution)/shard_map/embedding_back/all_to_all | solution.py:1221
  600.9 66.3 %reduce-scatter.20.cloned.1.call-start = ((), (), s32[]{:S(2)}) async-start(), calls=%async_computation.18 | async-start | bytes 1310720 | tf_op jit(solution)/shard_map/backward_layers/reduce_scatter | solution.py:889
  608.3 40.7 %collective-permute-start.60 = (bf16[256,512]{1,0:T(8,128)(2,1)}, bf16[256,512]{1,0:T(8,128)(2,1)}, u32[]{:S(2)}, u32[]{:S(2)}) collective-permute-start(bf16[256,512]{1,0:T(8,128)(2,1)} %backward_layers.80), channel_id=1, source_target_pairs={{0,16},{8,24},{16,0},{24,8},{1,17},{9,25},{17,1},{25,9},{2,18},{10... | collective-permute-start | bytes 786440 | tf_op jit(solution)/shard_map/backward_layers/ppermute | solution.py:388
  612.7 36.4 %collective-permute-start.61 = (bf16[256,1536]{1,0:T(8,128)(2,1)}, bf16[256,1536]{1,0:T(8,128)(2,1)}, u32[]{:S(2)}, u32[]{:S(2)}) collective-permute-start(bf16[256,1536]{1,0:T(8,128)(2,1)} %copy-done.83), channel_id=1, source_target_pairs={{0,8},{8,0},{16,24},{24,16},{1,9},{9,1},{17,25},{25,17},{2,10},{10... | collective-permute-start | bytes 2359304 | tf_op jit(solution)/shard_map/backward_layers/ppermute | solution.py:384
  620.3 64.1 %all-to-all-start.2 = ((f32[32,32,128]{2,1,0:T(8,128)}), f32[32,32,128]{2,1,0:T(8,128)}, u32[]{:S(2)}, u32[]{:S(2)}) async-start(f32[32,32,128]{2,1,0:T(8,128)} %bitcast.98), calls=%async_computation.5 | async-start | bytes 1048576 | tf_op jit(solution)/shard_map/small_grads/all_to_all | solution.py:1254
  624.0 58.4 %reduce-scatter.16.cloned.1.call-start = ((), (), s32[]{:S(2)}) async-start(), calls=%async_computation.16 | async-start | bytes 1310720 | tf_op jit(solution)/shard_map/own_grads/reduce_scatter | solution.py:889
  625.8 17.8 %collective-permute-start.63 = (f32[32,2048]{1,0:T(8,128)}, f32[32,2048]{1,0:T(8,128)S(1)}, u32[]{:S(2)}, u32[]{:S(2)}) collective-permute-start(f32[32,2048]{1,0:T(8,128)} %dynamic-slice_bitcast_fusion.2), channel_id=1, source_target_pairs={{0,1},{1,0},{2,3},{3,2},{4,5},{5,4},{6,7},{7,6},{8,9},{9,8},{10,11... | collective-permute-start | bytes 786440 | tf_op jit(solution)/shard_map/own_grads/ppermute | solution.py:392
  626.4 19.8 %collective-permute-start.65 = (f32[32,2048]{1,0:T(8,128)}, f32[32,2048]{1,0:T(8,128)}, u32[]{:S(2)}, u32[]{:S(2)}) collective-permute-start(f32[32,2048]{1,0:T(8,128)} %dynamic-slice_bitcast_fusion), channel_id=1, source_target_pairs={{0,1},{1,0},{2,3},{3,2},{4,5},{5,4},{6,7},{7,6},{8,9},{9,8},{10,11... | collective-permute-start | bytes 786440 | tf_op jit(solution)/shard_map/own_grads/ppermute | solution.py:392
  636.2 19.5 %collective-permute-start.59 = (f32[512,256]{1,0:T(8,128)}, f32[512,256]{1,0:T(8,128)}, u32[]{:S(2)}, u32[]{:S(2)}) collective-permute-start(f32[512,256]{1,0:T(8,128)} %copy.437), channel_id=1, source_target_pairs={{0,1},{1,0},{2,3},{3,2},{4,5},{5,4},{6,7},{7,6},{8,9},{9,8},{10,11... | collective-permute-start | bytes 1572872 | tf_op jit(solution)/shard_map/embedding_back/ppermute | solution.py:392
  650.1 3.9 collective-permute-start.66
  661.9 7.2 collective-permute-start.64
  698.5 10.7 %all-to-all-start.3 = ((f32[32,1,128]{2,1,0:T(1,128)}), f32[32,1,128]{2,1,0:T(1,128)S(1)}, u32[]{:S(2)}, u32[]{:S(2)}) async-start(f32[32,1,128]{2,1,0:T(1,128)} %add.606), calls=%async_computation.10 | async-start | bytes 32768 | tf_op jit(solution)/shard_map/clip_and_update/all_to_all | solution.py:1292
  (196 other events, 1191.8 us)
Sparse Core Ops, SparseCore 0:
  20.8 210.3 all-gather.5
  234.6 82.5 all-gather.3
  416.8 24.3 reduce-scatter.7
  447.5 24.4 reduce-scatter.9
  480.0 24.6 reduce-scatter.11
  526.6 19.3 reduce-scatter.13
  557.4 24.8 reduce-scatter.17
  604.6 31.4 reduce-scatter.19
  654.1 28.2 reduce-scatter.15

commit v2 on v1

--- a/solution.py
+++ b/solution.py
@@ -789,41 +789,238 @@
     )
 
 
-def banded_back(grads, banded):
-    rows, (_, depth, width) = grads.shape[0], banded.shape
-    dims = (((1,), (1,)), ((), ()))
-    return banded_kernel(
-        lambda left, right: lax.dot_general(
-            left[...], right[0], dims, preferred_element_type=WIDE
+def banded_back(own, conv_out, windows, banded, scalars):
+    rows, width = own.shape
+    count, depth, _ = banded.shape
+    blocks = rows // 32
+    half = depth // 2
+
+    def body(scalars_ref, own_ref, conv_ref, windows_ref, banded_ref, *refs):
+        mine_ref, other_ref, outer_ref, padded_ref, low_ref, total_ref = refs
+        step = pl.program_id(0)
+
+        @pl.when(step == 0)
+        def _():
+            grads = own_ref[...].astype(WIDE) * gelu_slope(conv_ref[...])
+            low_ref[...] = grads.astype(LOW)
+            padded_ref[...] = jnp.zeros_like(padded_ref)
+            padded_ref[:, 8 : 8 + blocks, :] = low_ref[...].astype(WIDE).reshape(32, blocks, width)
+            total_ref[...] = jnp.zeros_like(total_ref)
+
+        for number in range(count):
+
+            @pl.when(step == number)
+            def _():
+                shifted = padded_ref[:, 10 - number : 10 - number + blocks, :]
+                total_ref[...] += lax.dot_general(
+                    shifted.reshape(rows, width).astype(LOW),
+                    banded_ref[0],
+                    (((1,), (1,)), ((), ())),
+                    preferred_element_type=WIDE,
+                )
+
+        outer_ref[...] = lax.dot_general(
+            windows_ref[...], low_ref[...], (((0,), (0,)), ((), ())), preferred_element_type=WIDE
+        )
+
+        @pl.when(step == count - 1)
+        def _():
+            core = scalars_ref[16]
+            mine_ref[...] = total_ref[:, pl.ds(pl.multiple_of(core * half, 128), half)]
+            other_ref[...] = total_ref[:, pl.ds(pl.multiple_of((1 - core) * half, 128), half)]
+
+    def fixed(shape):
+        return pl.BlockSpec(shape, lambda i, s: (0, 0))
+
+    return pl.pallas_call(
+        body,
+        grid_spec=pltpu.PrefetchScalarGridSpec(
+            num_scalar_prefetch=1,
+            grid=(count,),
+            in_specs=[
+                fixed((rows, width)),
+                fixed((rows, width)),
+                pl.BlockSpec((rows, depth), lambda i, s: (0, i)),
+                pl.BlockSpec((1, depth, width), lambda i, s: (i, 0, 0)),
+            ],
+            out_specs=[
+                fixed((rows, half)),
+                fixed((rows, half)),
+                pl.BlockSpec((depth, width), lambda i, s: (i, 0)),
+            ],
+            scratch_shapes=[
+                pltpu.VMEM((32, blocks + 16, width), WIDE),
+                pltpu.VMEM((rows, width), LOW),
+                pltpu.VMEM((rows, depth), WIDE),
+            ],
         ),
-        (grads, banded),
-        [
-            pl.BlockSpec((rows, width), lambda i: (0, i)),
-            pl.BlockSpec((1, depth, width), lambda i: (i, 0, 0)),
+        out_shape=[
+            jax.ShapeDtypeStruct((rows, half), WIDE),
+            jax.ShapeDtypeStruct((rows, half), WIDE),
+            jax.ShapeDtypeStruct((count * depth, width), WIDE),
         ],
-        pl.BlockSpec((rows, depth), lambda i: (0, 0)),
-        (rows, depth),
-        True,
-    )
-
-
-def banded_outer(windows, grads):
-    rows, width = grads.shape
-    depth = windows.shape[1] // 5
-    dims = (((0,), (0,)), ((), ()))
-    return banded_kernel(
-        lambda left, right: lax.dot_general(
-            left[...], right[...], dims, preferred_element_type=WIDE
+        compiler_params=GRANT,
+        cost_estimate=SHORT,
+    )(scalars, own, conv_out, windows, banded)
+
+
+def input_grad(own, mine, other, valid, strided, scalars):
+    frames, channels, _ = strided.shape
+    outs = own.shape[1] // frames
+
+    def body(scalars_ref, own_ref, mine_ref, other_ref, valid_ref, strided_ref, out_ref):
+        total = None
+        grads = own_ref[...].astype(WIDE) + mine_ref[...] + other_ref[...]
+        for frame in range(frames):
+            part = grads[:, frame * outs : (frame + 1) * outs] * valid_ref[:, frame : frame + 1]
+            product = jnp.dot(
+                strided_ref[frame], part.astype(LOW), preferred_element_type=WIDE
+            )
+            total = product if total is None else total + product
+        out_ref[...] = total.T
+
+    shapes = [jax.ShapeDtypeStruct((outs, channels), WIDE)]
+    return one_step(body, scalars, (own, mine, other, valid, strided), shapes)[0]
+
+
+def kernel_grad(spread, taps, outs, scalars):
+    count = spread.shape[0] // (2 * TAPS_OUT * outs)
+
+    def body(scalars_ref, spread_ref, out_ref):
+        for tap in range(taps):
+            for side in range(2):
+                total = None
+                for frame in range(TAPS_OUT):
+                    block, spot = divmod(tap + frame + 1, TAPS_OUT)
+                    row = ((block * 2 + side) * TAPS_OUT + spot) * outs
+                    part = spread_ref[row : row + outs, frame * outs : (frame + 1) * outs]
+                    total = part if total is None else total + part
+                out_ref[tap, :, side * outs : (side + 1) * outs] = total.T
+
+    shapes = [jax.ShapeDtypeStruct((taps, outs, 2 * outs), WIDE)]
+    return one_step(body, scalars, (spread,), shapes)[0]
+
+
+def packed_exchange(stream, joined, readout, gains, scalars):
+    rows, width = stream.shape
+    frames, outs = rows // 2, width // 32
+    blocks = frames // TAPS_OUT
+    mel_count, gain_count = readout.shape[1], gains.shape[0]
+
+    def body(scalars_ref, stream_ref, joined_ref, readout_ref, gains_ref, out_ref, own_ref):
+        first = pl.multiple_of(scalars_ref[16] * frames, 8)
+        for lanes in range(width // 128):
+            cut = pl.ds(lanes * 128, 128)
+            beyond = pl.ds(width + lanes * 128, 128)
+            own_ref[lanes] = (
+                stream_ref[pl.ds(first, frames), cut] + joined_ref[pl.ds(first, frames), beyond]
+            )
+        out_ref[:, blocks:, :] = jnp.zeros((32, blocks, TAPS_OUT * outs), LOW)
+        each = 128 // outs
+        for frame in range(TAPS_OUT):
+            for lanes in range(width // 128):
+                part = own_ref[lanes, pl.ds(frame, blocks, stride=TAPS_OUT), :].astype(LOW)
+                for spot in range(each):
+                    piece = part[:, spot * outs : (spot + 1) * outs]
+                    device = lanes * each + spot
+                    out_ref[device, :blocks, frame * outs : (frame + 1) * outs] = piece
+        for device in range(32):
+            for side in range(2):
+                row = device * outs + side * blocks
+                piece = readout_ref[row : row + blocks, :].astype(LOW)
+                out_ref[device, blocks:, side * 128 : side * 128 + mel_count] = piece
+            piece = gains_ref[:, device * outs : (device + 1) * outs].astype(LOW)
+            out_ref[device, blocks : blocks + gain_count, 96 : 96 + outs] = piece
+
+    shapes = [jax.ShapeDtypeStruct((32, 2 * blocks, TAPS_OUT * outs), LOW)]
+    scratch = [pltpu.VMEM((width // 128, frames, 128), WIDE)]
+    return one_step(body, scalars, (stream, joined, readout, gains), shapes, scratch)[0]
+
+
+def squares_of(items, scalars, extras=()):
+    def body(scalars_ref, *refs):
+        out_ref = refs[-1]
+        out_ref[...] = refs[len(items)][...] if extras else jnp.zeros_like(out_ref)
+        for ref in refs[: len(items)]:
+            values = ref[...].astype(WIDE)
+            values = values * values
+            while values.ndim > 2:
+                values = jnp.sum(values, 0)
+            row = jnp.sum(values, 0, keepdims=True)
+            width = row.shape[1]
+            for start in range(0, width, 128):
+                stop = min(start + 128, width)
+                out_ref[0:1, : stop - start] += row[:, start:stop]
+
+    shapes = [jax.ShapeDtypeStruct((8, 128), WIDE)]
+    return one_step(body, scalars, (*items, *extras), shapes)[0]
+
+
+def all_updates(totals, weights, scalars):
+    rates, decays = weight_rates(), [DECAY_RATE] * 8 + [0.0]
+    count = len(weights)
+
+    steps = 8
+
+    def split(item):
+        return item.shape[-1] % (steps * 128) == 0
+
+    def block(item):
+        if not split(item):
+            return pl.BlockSpec(item.shape, lambda j, s, n=item.ndim: (0,) * n)
+        lead = item.ndim - 1
+        shape = item.shape[:-1] + (item.shape[-1] // steps,)
+        return pl.BlockSpec(shape, lambda j, s, n=lead: (0,) * n + (j,))
+
+    def body(scalars_ref, totals_ref, *refs):
+        ins, stats_ref, outs = refs[: 4 * count], refs[4 * count], refs[4 * count + 1 :]
+        whole = jnp.sum(totals_ref[...].reshape(32, 8, 128), 0)
+        squared, loss, frames = [
+            jnp.sum(whole[row : row + 1], 1, keepdims=True) for row in range(3)
+        ]
+        norm = jnp.sqrt(squared) / frames
+        factor = jnp.minimum(1.0, CLIP_LIMIT / norm) / frames
+
+        def update(number):
+            master, moment, square, grad = [
+                ref[...].astype(WIDE) for ref in ins[4 * number : 4 * number + 4]
+            ]
+            scale = factor.reshape((1,) * grad.ndim)
+            new = adamw(master, moment, square, scale * grad, rates[number], decays[number])
+            for ref, item in zip(outs[3 * number : 3 * number + 3], new):
+                ref[...] = item
+
+        @pl.when(pl.program_id(0) == 0)
+        def _():
+            for row, item in enumerate((loss, frames, norm)):
+                stats_ref[row : row + 1, :] = jnp.broadcast_to(item, (1, 128))
+            for number, (master, *_) in enumerate(weights):
+                if not split(master):
+                    update(number)
+
+        for number, (master, *_) in enumerate(weights):
+            if split(master):
+                update(number)
+
+    stats_shape = jax.ShapeDtypeStruct((8, 128), WIDE)
+    shapes, out_specs = [stats_shape], [pl.BlockSpec((8, 128), lambda j, s: (0, 0))]
+    for master, *_ in weights:
+        shapes += [jax.ShapeDtypeStruct(master.shape, WIDE)] * 3
+        out_specs += [block(master)] * 3
+    operands = (totals, *[item for weight in weights for item in weight])
+    stats, *new = pl.pallas_call(
+        body,
+        grid_spec=pltpu.PrefetchScalarGridSpec(
+            num_scalar_prefetch=1,
+            grid=(steps,),
+            in_specs=[block(item) for item in operands],
+            out_specs=out_specs,
         ),
-        (windows, grads),
-        [
-            pl.BlockSpec((rows, depth), lambda i: (0, i)),
-            pl.BlockSpec((rows, width), lambda i: (0, 0)),
-        ],
-        pl.BlockSpec((depth, width), lambda i: (i, 0)),
-        (windows.shape[1], width),
-        False,
-    )
+        out_shape=shapes,
+        compiler_params=pltpu.CompilerParams(vmem_limit_bytes=60 * 2**20),
+        cost_estimate=SHORT,
+    )(scalars, *operands)
+    return stats, new
 
 
 def norm_parts(values):
@@ -917,7 +1114,7 @@
         summed = [share for share in self.shares if share.total is not None]
         for share in summed:
             share.turns += 1
-        summed = [share for share in summed if share.turns == 3]
+        summed = [share for share in summed if share.turns == 2]
         values, landed, totals = tie(
             (values, [share.flying for share in flying], [share.total for share in summed])
         )
@@ -1133,7 +1330,8 @@
         columns = jnp.concatenate(in_order(core, columns, swap_core(columns)), -1)
         start = jnp.einsum("nzv,zr->nvr", features, columns, preferred_element_type=WIDE)
         start = start * valid_all[:, :, None]
-        padded = start.astype(LOW).reshape(32, blocks, TAPS_OUT * group)
+        padded = start.astype(LOW).reshape(32, blocks, TAPS_OUT, 2, outs)
+        padded = padded.transpose(0, 1, 3, 2, 4).reshape(32, blocks, TAPS_OUT * group)
         padded = jnp.pad(padded, ((0, 0), (2, 2), (0, 0)))
         windows = jnp.concatenate([padded[:, i : i + blocks] for i in range(5)], -1)
         windows = windows.reshape(32 * blocks, 5 * TAPS_OUT * group)
@@ -1141,8 +1339,13 @@
             kernel_master.astype(LOW).transpose(0, 2, 1), ((TAPS_OUT, TAPS_OUT), (0, 0), (0, 0))
         )
         banded = jnp.stack([turned[7 - j : 47 - j] for j in range(TAPS_OUT)], 2)
+        banded = banded.reshape(5, TAPS_OUT, 2, outs, TAPS_OUT * outs).transpose(0, 2, 1, 3, 4)
         banded = banded.reshape(5, TAPS_OUT * group, TAPS_OUT * outs)
         conv_out = banded_dot(windows, banded)
+        strided = features.reshape(32, -1, blocks, TAPS_OUT).transpose(3, 1, 0, 2)
+        strided = strided.reshape(TAPS_OUT, -1, 32 * blocks)
+        valid_rows = valid_all.reshape(32 * blocks, TAPS_OUT)
+        conv_out, strided, valid_rows = tie((conv_out, strided, valid_rows))
         start_own = lax.dynamic_slice_in_dim(start, core * outs, outs, 2)
         start_own = start_own.reshape(32 * blocks, TAPS_OUT * outs)
         embedded = start_own + jax.nn.gelu(conv_out)
@@ -1211,57 +1414,33 @@
         result, shares_zero, d_gain_one = tp_backward(
             d_encoded, d_encoded.astype(LOW), kept_zero, mats_zero, gain[0], gain[1], *parts
         )
-        d_gain_zero = result[3]
-        d_embedded = result[0] + d_joined[:, width:]
-        (d_embedded,) = flow.turn(d_embedded)
+        d_stream, d_gain_zero = result[0], result[3]
 
     with jax.named_scope("embedding_back"):
-        own = pick(d_embedded.astype(LOW).reshape(2, frame_count, width), core)
-        own = own.reshape(frame_count, 32, outs).transpose(1, 0, 2)
-        own = lax.all_to_all(
-            own.reshape(32 * blocks, TAPS_OUT * outs), BOTH, 0, 0, tiled=True
-        ).astype(WIDE)
-        d_conv = jax.vjp(jax.nn.gelu, conv_out)[1](own)[0].astype(LOW)
-        padded = jnp.pad(
-            d_conv.reshape(32, blocks, TAPS_OUT * outs), ((0, 0), (2, 2), (0, 0))
-        )
-        shifted = jnp.concatenate([padded[:, 4 - i : 4 - i + blocks] for i in range(5)], -1)
-        d_start = banded_back(
-            shifted.reshape(32 * blocks, 5 * TAPS_OUT * outs), banded
-        )
-        d_start = d_start.reshape(32 * blocks, TAPS_OUT, 2, outs)
-        mine = lax.dynamic_index_in_dim(d_start, core, 2, keepdims=False)
-        other = lax.dynamic_index_in_dim(d_start, 1 - core, 2, keepdims=False)
-        other = swap_core(other.reshape(32 * blocks, TAPS_OUT * outs))
-        d_start = own + mine.reshape(32 * blocks, TAPS_OUT * outs) + other
-        d_start = d_start.reshape(32, frame_count, outs) * valid_all[:, :, None]
-        grad_input = jnp.einsum(
-            "nzv,nvr->zr", features, d_start.astype(LOW), preferred_element_type=WIDE
-        )
-        spread = banded_outer(windows, d_conv)
-        spread = spread.reshape(5 * TAPS_OUT, group, TAPS_OUT, outs)
-        grad_kernel = sum(spread[j + 1 : j + 1 + taps, :, j, :] for j in range(TAPS_OUT))
-        grad_kernel = grad_kernel.transpose(0, 2, 1)
-
-    with jax.named_scope("small_grads"):
-        d_readout, d_gain_zero, _ = tie((d_readout, d_gain_zero, d_conv))
         d_gains = jnp.concatenate(
             [d_gain_zero, d_gain_one, d_gain_two, d_gain_three, d_gain_last[None]], 0
         )
-        fill = jnp.zeros((width, 1), WIDE)
-        small = jnp.concatenate([d_readout, d_gains.T, fill + loss_local, fill + count_local], 1)
-        small = jnp.pad(small, ((0, 0), (0, 128 - small.shape[1])))
-        small = lax.all_to_all(small, BOTH, 0, 0, tiled=True)
-        small = jnp.sum(small.reshape(32, width // 32, 128), 0)
-        grad_readout = small[:, :mel_count]
-        grad_gains = small[:, mel_count : mel_count + 5].T
-        loss_sum = small[0, mel_count + 5]
-        frame_total = small[0, mel_count + 6]
+        d_gains = jnp.pad(d_gains, ((0, 3), (0, 0)))
+        both = packed_exchange(d_stream, d_joined, d_readout, d_gains, scalars)
+        (both,) = flow.turn(both)
+        (both,) = flow.turn(both)
+        own_sent = both = both.reshape(64 * blocks, TAPS_OUT * outs)
+        both = lax.all_to_all(both, BOTH, 0, 0, tiled=True)
+        both, shares_zero[0].total = tie((both, shares_zero[0].total))
+        both = both.reshape(32, 2 * blocks, TAPS_OUT * outs)
+        own = both[:, :blocks].reshape(32 * blocks, TAPS_OUT * outs)
+        mine, other, spread = banded_back(own, conv_out, windows, banded, scalars)
+        grad_input = input_grad(own, mine, swap_core(other), valid_rows, strided, scalars)
+        spread, small = tie((spread, both[:, blocks:]))
+        grad_kernel = kernel_grad(spread, taps, outs, scalars)
+        small = jnp.sum(small.astype(WIDE), 0)
+        grad_readout = jnp.concatenate([small[:, :mel_count], small[:, 128 : 128 + mel_count]], 0)
+        grad_gains = small[:5, 96 : 96 + outs]
 
     with jax.named_scope("own_grads"):
-        flow.turn(d_conv)
-        for share in [*shares_zero, *shares_one, g_bridge]:
-            share.total = tie((share.total, d_conv))[0].astype(WIDE)
+        shares = [*shares_zero, *shares_one, g_bridge]
+        for share in shares:
+            share.total = tie((share.total, own_sent))[0]
 
         def unfolded(both, count):
             cut = both.reshape(2, both.shape[1], count, both.shape[2] // count)
@@ -1288,15 +1467,17 @@
         ]
 
     with jax.named_scope("clip_and_update"):
-        squares_local = sum((jnp.sum(item * item) for item in grads))
-        squared = lax.all_to_all(
-            jnp.zeros((32, 128), WIDE) + squares_local, BOTH, 0, 0, tiled=True
-        )
-        squared = jnp.sum(squared[:, 0])
-        grad_norm = jnp.sqrt(squared) / frame_total
-        factor = jnp.minimum(1.0, CLIP_LIMIT / grad_norm) / frame_total
+        early = squares_of([share.total for share in shares[1:]], scalars)
+        row = lax.broadcasted_iota(jnp.int32, (8, 128), 0)
+        lane = lax.broadcasted_iota(jnp.int32, (8, 128), 1)
+        told = jnp.where(row == 1, loss_local, jnp.where(row == 2, count_local, 0.0))
+        early = early + jnp.where(lane == 0, told, 0.0)
+        late = [shares[0].total, grad_input, grad_kernel, grad_readout, grad_gains]
+        totals = squares_of(late, scalars, (early,))
+        totals = jnp.broadcast_to(totals[None], (32, 8, 128)).reshape(256, 128)
+        totals = lax.all_to_all(totals, BOTH, 0, 0, tiled=True)
         masters = (
-            input_master,
+            input_master.T,
             kernel_master,
             joint_master,
             output_master,
@@ -1307,7 +1488,7 @@
             gains_master,
         )
         moments = (
-            input_moment,
+            input_moment.T,
             kernel_moment,
             joint_moment,
             output_moment,
@@ -1318,7 +1499,7 @@
             gains_moment,
         )
         squares = (
-            input_square,
+            input_square.T,
             kernel_square,
             joint_square,
             output_square,
@@ -1328,12 +1509,11 @@
             readout_square,
             gains_square,
         )
-        decays = [DECAY_RATE] * 8 + [0.0]
-        results = []
-        for master, moment, square, grad, rate, decay in zip(
-            masters, moments, squares, grads, weight_rates(), decays
-        ):
-            results.extend(adamw(master, moment, square, factor * grad, rate, decay))
+        stats, results = all_updates(
+            totals, list(zip(masters, moments, squares, grads)), scalars
+        )
+        results[:3] = [item.T for item in results[:3]]
+        loss_sum, frame_total, grad_norm = stats[0, 0], stats[1, 0], stats[2, 0]
     return (loss_sum, frame_total, grad_norm, *results)
 
 

time: 750 us -> 726 us (0.968)
  other arithmetic: 82.9 us -> 56.4 us
  waiting for transfers between devices: 237 us -> 258 us
  Pallas kernels: 149 us -> 161 us
  between operations: 28.3 us -> 18.2 us
  starting transfers between devices: 90.6 us -> 80.9 us
    pallas_call x0 -> x2, Pallas kernels: none -> 20.1 us  [the longest x1 14.5 us: all_updates(): pl.pallas_call(body, grid_spec=pltpu.PrefetchScalarGridSpec(num_scalar_pr...]
    ppermute x12, starting transfers between devices: 42.6 us -> 28.7 us  [shift_z(): lax.ppermute(item, 'fsdp', [(i, (i + 2 * hops) % 8) for i in range(8)])]
    sub x9 -> x0, other arithmetic: 12.6 us -> none  [adamw(): master - rate * (fixed_moment / (jnp.sqrt(fixed_square) + ADAM_EPS) + dec...]
    reduce_sum x12 -> x3, other arithmetic: 12.7 us -> 0.37 us  [the longest x1 0.2 us: norm_back(): spread = jnp.mean(center * center, -1, keepdims=True)]
    reshape x7 -> x3, local copies, waits for them, and re-layouts: 22.2 us -> 10.4 us  [the longest x1 6.52 us: paired_shards(): banded.reshape(5, TAPS_OUT, 2, outs, TAPS_OUT * outs)]
    pallas_call x9, Pallas kernels: 29 us -> 20.6 us  [piece_dot(): pl.pallas_call(body, grid_spec=pltpu.PrefetchScalarGridSpec(num_scalar_pr...]
    pallas_call x17 -> x22, Pallas kernels: 28.8 us -> 37 us  [one_step(): pl.pallas_call(body, grid_spec=pltpu.PrefetchScalarGridSpec(num_scalar_pr...]
    unnamed x393 -> x352, local copies, waits for them, and re-layouts: 69.8 us -> 71.1 us
  transfers between devices with their start and end apart: 80 -> 79, of which waited for: 37 -> 39; matrix products, arithmetic and copies ran while one was open for 18% -> 14% of each run, Pallas kernels for 18% -> 16%
where the time goes in v2:
time: 726 us; the launch traced here: 716 us
  waiting for transfers between devices  258 us (36%)
  Pallas kernels  161 us (22%)
  local copies, waits for them, and re-layouts  136 us (19%)
  starting transfers between devices  80.9 us (11%)
  other arithmetic  56.4 us (8%)
  between operations  18.2 us (3%)
    ppermute x12, waiting for transfers between devices, shift_z(): lax.ppermute(item, 'fsdp', [(i, (i + 2 * hops) % 8) for i in range(8)])  99 us
    unnamed x352, local copies, waits for them, and re-layouts  71.1 us
    ppermute x14, waiting for transfers between devices, swap_x(): return lax.ppermute(item, 'dp', [(i, i ^ 1) for i in range(4)])  65.5 us
    ppermute x16, waiting for transfers between devices, swap_y(): return lax.ppermute(item, 'dp', [(i, i ^ 2) for i in range(4)])  41.6 us
    pallas_call x22, Pallas kernels, one_step(): pl.pallas_call(body, grid_spec=pltpu.PrefetchScalarGridSpec(num_scalar_pr...  37 us
    ppermute x12, starting transfers between devices, shift_z(): lax.ppermute(item, 'fsdp', [(i, (i + 2 * hops) % 8) for i in range(8)])  28.7 us
    pallas_call x9, Pallas kernels, piece_dot_back(): pl.pallas_call(body, grid_spec=pltpu.PrefetchScalarGridSpec(num_scalar_pr...  27.5 us
    pallas_call x18, Pallas kernels, outer_sum(): pl.pallas_call(body, grid_spec=pltpu.PrefetchScalarGridSpec(num_scalar_pr...  24.1 us
  transfers between devices with their start and end apart: 79, of which 39 were waited for; matrix products, arithmetic and copies ran while one was open for 14% of the time, Pallas kernels for 16%

profile of v2, /device:TPU:0, one launch (start us, length us, event | category | flops | bytes accessed | tf_op | source)
XLA Modules:
  0.0 715.9 jit_solution(1240905773937379617)
XLA Ops:
  11.7 3.3 dynamic-slice_reduce_fusion.1
  22.5 5.0 collective-permute-start.2
  30.3 3.2 collective-permute-done
  36.8 7.3 %collective-permute-done.3 = bf16[4,208,128]{2,1,0:T(8,128)(2,1)S(1)} collective-permute-done((bf16[4,208,128]{2,1,0:T(8,128)(2,1)S(1)}, bf16[4,208,128]{2,1,0:T(8,128)(2,1)S(1)}, u32[]{:S(2)}, u32[]{:S(2)}) %collective-permute-start.3) | collective-permute-done | bytes 213024 | tf_op jit(solution)/shard_map/features/ppermute | solution.py:384
  45.7 4.9 collective-permute-done.5
  57.7 6.8 collective-permute-done.10
  64.5 3.6 collective-permute-start.11
  69.0 6.4 copy.212
  75.3 6.5 reshape.314
  85.4 2.8 collective-permute-start.12
  99.5 4.1 concatenate.98
  113.1 11.3 %collective-permute-done.20 = bf16[256,512]{1,0:T(8,128)(2,1)} collective-permute-done((bf16[256,512]{1,0:T(8,128)(2,1)S(1)}, bf16[256,512]{1,0:T(8,128)(2,1)}, u32[]{:S(2)}, u32[]{:S(2)}) %collective-permute-start.20) | collective-permute-done | bytes 262176 | tf_op jit(solution)/shard_map/weights/ppermute | solution.py:396
  130.2 3.3 copy.214
  136.5 5.8 collective-permute-done.21
  142.3 4.2 collective-permute-start.22
  147.3 6.4 all-to-all-start
  155.1 5.8 collective-permute-done.22
  171.0 4.6 collective-permute-start.26
  175.6 26.4 %collective-permute-done.23 = bf16[1024,512]{1,0:T(8,128)(2,1)} collective-permute-done((bf16[1024,512]{1,0:T(8,128)(2,1)S(1)}, bf16[1024,512]{1,0:T(8,128)(2,1)}, u32[]{:S(2)}, u32[]{:S(2)}) %collective-permute-start.23) | collective-permute-done | bytes 1048608 | tf_op jit(solution)/shard_map/weights/ppermute | solution.py:396
  202.0 6.5 collective-permute-start.24
  208.5 7.2 collective-permute-done.15
  220.4 6.4 forward_layers.17
  229.6 4.0 collective-permute-done.24
  236.7 3.5 forward_layers.20
  244.4 4.4 copy-done
  254.6 35.7 %collective-permute-done.30 = bf16[1024,512]{1,0:T(8,128)(2,1)} collective-permute-done((bf16[1024,512]{1,0:T(8,128)(2,1)S(1)}, bf16[1024,512]{1,0:T(8,128)(2,1)}, u32[]{:S(2)}, u32[]{:S(2)}) %collective-permute-start.30) | collective-permute-done | bytes 1048608 | tf_op jit(solution)/shard_map/weights/ppermute | solution.py:396
  297.2 6.4 forward_layers.25
  305.4 4.0 copy-done.2
  311.0 3.4 pad_maximum_fusion.2
  316.4 3.9 all-gather.4.cloned.1.call-done.weights_ref
  322.5 3.5 forward_layers.28
  340.6 4.2 backward_layers.38.grads_ref.right_ref
  344.9 3.5 backward_layers.39.mine_ref
  357.3 19.5 %collective-permute-done.37.far_left_ref.far_right_ref = bf16[256,2048]{1,0:T(8,128)(2,1)S(1)} collective-permute-done((bf16[256,2048]{1,0:T(8,128)(2,1)S(1)}, bf16[256,2048]{1,0:T(8,128)(2,1)S(1)}, u32[]{:S(2)}, u32[]{:S(2)}) %collective-permute-start.37) | collective-permute-done | bytes 1048608 | tf_op jit(solution)/shard_map/backward_layers/ppermute | solution.py:384
  376.8 3.8 collective-permute-done.38.far_left_ref.far_right_ref
  387.4 8.6 %backward_layers.46.grads_ref.right_ref = bf16[256,1536]{1,0:T(8,128)(2,1)S(1)} custom-call(f32[8]{0:T(128)S(1)} %multiply_power_fusion.slopes_ref, bf16[256,1536]{1,0:T(8,128)(2,1)S(1)} %copy-done.56, f32[256,512]{1,0:T(8,128)S(1)} %get-tuple-element.240.mine_ref, f32[256,512]{1,0:T(8,128)S(1)} %collective-permute-done.39.other_ref, ...), custom_call_target="tpu_custom_call" | custom-call | flops 1000 | bytes 1000 | tf_op jit(solution)/shard_map/backward_layers/pallas_call | solution.py:688
  400.4 2.8 backward_layers.47.mine_ref
  403.2 4.7 collective-permute-done.40
  410.3 3.2 add_convert_fusion.3
  420.5 4.1 copy-done.3
  424.6 2.8 backward_layers.53
  427.4 3.3 collective-permute-done.43.far_left_ref.far_right_ref
  430.6 10.3 %collective-permute-done.44.far_left_ref.far_right_ref = bf16[256,2048]{1,0:T(8,128)(2,1)S(1)} collective-permute-done((bf16[256,2048]{1,0:T(8,128)(2,1)S(1)}, bf16[256,2048]{1,0:T(8,128)(2,1)S(1)}, u32[]{:S(2)}, u32[]{:S(2)}) %collective-permute-start.44) | collective-permute-done | bytes 1048608 | tf_op jit(solution)/shard_map/backward_layers/ppermute | solution.py:388
  452.4 4.8 copy-done.4
  457.2 4.6 backward_layers.57.grads_ref.right_ref
  466.0 4.5 backward_layers.58.mine_ref
  487.4 3.7 backward_layers.64
  494.0 24.4 %collective-permute-done.50 = bf16[512,512]{1,0:T(8,128)(2,1)S(1)} collective-permute-done((bf16[512,512]{1,0:T(8,128)(2,1)}, bf16[512,512]{1,0:T(8,128)(2,1)S(1)}, u32[]{:S(2)}, u32[]{:S(2)}) %collective-permute-start.50) | collective-permute-done | bytes 524320 | tf_op jit(solution)/shard_map/backward_layers/ppermute | solution.py:384
  518.5 2.9 backward_layers.67
  532.9 8.6 %backward_layers.69.grads_ref.right_ref = bf16[256,1536]{1,0:T(8,128)(2,1)S(1)} custom-call(f32[8]{0:T(128)S(1)} %multiply_power_fusion.slopes_ref, bf16[256,1536]{1,0:T(8,128)(2,1)S(1)} %copy-done.58, f32[256,512]{1,0:T(8,128)S(1)} %copy-done.116, f32[256,512]{1,0:T(8,128)S(1)} %copy-done.118, f32[2,1,128]{2,1,0:T(1,128)S(1)} %constant_dynamic-slice_fusion.valid_ref), custom_call_target="tpu_custom_call" | custom-call | flops 1000 | bytes 1000 | tf_op jit(solution)/shard_map/backward_layers/pallas_call | solution.py:688
  549.6 2.8 backward_layers.70.mine_ref
  553.4 3.3 add_convert_fusion.1
  578.4 10.7 %collective-permute-done.58.far_left_ref.far_right_ref = bf16[256,2048]{1,0:T(8,128)(2,1)S(1)} collective-permute-done((bf16[256,2048]{1,0:T(8,128)(2,1)}, bf16[256,2048]{1,0:T(8,128)(2,1)S(1)}, u32[]{:S(2)}, u32[]{:S(2)}) %collective-permute-start.58) | collective-permute-done | bytes 1048608 | tf_op jit(solution)/shard_map/backward_layers/ppermute | solution.py:388
  596.0 3.9 copy.231.strided_ref
  604.5 8.2 %collective-permute-done.60 = bf16[256,1536]{1,0:T(8,128)(2,1)} collective-permute-done((bf16[256,1536]{1,0:T(8,128)(2,1)}, bf16[256,1536]{1,0:T(8,128)(2,1)}, u32[]{:S(2)}, u32[]{:S(2)}) %collective-permute-start.60) | collective-permute-done | bytes 786464 | tf_op jit(solution)/shard_map/embedding_back/ppermute | solution.py:384
  618.0 3.4 all-to-all-start.1
  634.2 3.9 all-to-all-done.1
  638.1 15.4 %reduce-scatter.20.cloned.1.call-done.refs_0_ = bf16[64,2048]{1,0:T(8,128)(2,1)} async-done(((bf16[256,2048]{1,0:T(8,128)(2,1)}), bf16[64,2048]{1,0:T(8,128)(2,1)}) %reduce-scatter.20.cloned.1.call-update) | async-done | bytes 262160 | tf_op jit(solution)/shard_map/embedding_back/reduce_scatter | solution.py:1086
  655.9 5.6 embedding_back.13
  661.7 6.6 embedding_back.15.refs_2_.refs_7_
  675.0 2.9 embedding_back.14.refs_1_.refs_3_
  680.9 3.6 all-to-all-start.2
  686.2 6.5 all-to-all-done.2
  693.3 14.5 %clip_and_update.5 = (f32[8,128]{1,0:T(8,128)}, f32[32,256]{1,0:T(8,128)}, f32[32,256]{1,0:T(8,128)}, f32[32,256]{1,0:T(8,128)}, f32[31,32,64]{2,1,0:T(8,128)}, ...) custom-call(s32[17]{0:T(128)} %copy-done.120, ...), custom_call_target="tpu_custom_call" | custom-call | flops 1000 | bytes 1000 | tf_op jit(solution)/shard_map/clip_and_update/pallas_call | solution.py:1011
  (713 shorter events, 271.6 us)
Async XLA Ops:
  7.2 237.2 %all-gather.6.cloned.1.call-start = ((), (), s32[]{:S(2)}) async-start(), calls=%async_computation.18 | async-start | bytes 11141120 | tf_op jit(solution)/shard_map/weights/all_gather | solution.py:1310
  20.7 299.6 %all-gather.4.cloned.1.call-start = ((), (), s32[]{:S(2)}) async-start(), calls=%async_computation.10 | async-start | bytes 4456448 | tf_op jit(solution)/shard_map/weights/all_gather | solution.py:1310
  22.5 11.0 %collective-permute-start.2 = (bf16[208,128]{1,0:T(8,128)(2,1)S(1)}, bf16[208,128]{1,0:T(8,128)(2,1)S(1)}, u32[]{:S(2)}, u32[]{:S(2)}) collective-permute-start(bf16[208,128]{1,0:T(8,128)(2,1)S(1)} %concatenate.93), channel_id=1, source_target_pairs={{0,6},{1,7},{2,0},{3,1},{4,2},{5,3},{6,4},{7,5},{8,14},{9,15},{10,... | collective-permute-start | bytes 159752 | tf_op jit(solution)/shard_map/features/ppermute | solution.py:396
  27.6 6.0 collective-permute-start.1
  27.6 6.0 collective-permute-start
  28.6 54.6 %collective-permute-start.7 = (bf16[256,32]{0,1:T(8,128)(2,1)S(1)}, bf16[256,32]{0,1:T(8,128)(2,1)S(1)}, u32[]{:S(2)}, u32[]{:S(2)}) collective-permute-start(bf16[256,32]{0,1:T(8,128)(2,1)S(1)} %convert_element_type.210), channel_id=1, source_target_pairs={{0,1},{1,0},{2,3},{3,2},{4,5},{5,4},{6,7},{7,6},{8,9},{9,8},{10,11... | collective-permute-start | bytes 49160 | tf_op jit(solution)/shard_map/embedding/ppermute | solution.py:392
  33.6 12.0 %collective-permute-start.4 = (bf16[4,208,128]{2,1,0:T(8,128)(2,1)S(1)}, bf16[4,208,128]{2,1,0:T(8,128)(2,1)S(1)}, u32[]{:S(2)}, u32[]{:S(2)}) collective-permute-start(bf16[4,208,128]{2,1,0:T(8,128)(2,1)S(1)} %bitcast_dynamic-update-slice_fusion.4), channel_id=1, source_target_pairs={{0,16},{8,24},{16,0},{24,8},{1,17},{9,25},{17,1},{25,9},{2,18},{10... | collective-permute-start | bytes 638984 | tf_op jit(solution)/shard_map/features/ppermute | solution.py:388
  35.2 8.9 %collective-permute-start.3 = (bf16[4,208,128]{2,1,0:T(8,128)(2,1)S(1)}, bf16[4,208,128]{2,1,0:T(8,128)(2,1)S(1)}, u32[]{:S(2)}, u32[]{:S(2)}) collective-permute-start(bf16[4,208,128]{2,1,0:T(8,128)(2,1)S(1)} %bitcast_dynamic-update-slice_fusion.4), channel_id=1, source_target_pairs={{0,8},{8,0},{16,24},{24,16},{1,9},{9,1},{17,25},{25,17},{2,10},{10... | collective-permute-start | bytes 638984 | tf_op jit(solution)/shard_map/features/ppermute | solution.py:384
  44.1 6.5 collective-permute-start.5
  50.6 37.6 %collective-permute-start.6 = (bf16[16,208,128]{2,1,0:T(8,128)(2,1)S(1)}, bf16[16,208,128]{2,1,0:T(8,128)(2,1)}, u32[]{:S(2)}, u32[]{:S(2)}) collective-permute-start(bf16[16,208,128]{2,1,0:T(8,128)(2,1)S(1)} %bitcast.385), channel_id=1, source_target_pairs={{0,1},{1,0},{2,3},{3,2},{4,5},{5,4},{6,7},{7,6},{8,9},{9,8},{10,11... | collective-permute-start | bytes 2555912 | tf_op jit(solution)/shard_map/features/ppermute | solution.py:392
  52.3 12.3 %collective-permute-start.10 = (bf16[256,512]{1,0:T(8,128)(2,1)S(1)}, bf16[256,512]{1,0:T(8,128)(2,1)S(1)}, u32[]{:S(2)}, u32[]{:S(2)}) collective-permute-start(bf16[256,512]{1,0:T(8,128)(2,1)S(1)} %bitcast.404), channel_id=1, source_target_pairs={{0,2},{1,3},{2,4},{3,5},{4,6},{5,7},{6,0},{7,1},{8,10},{9,11},{10,... | collective-permute-start | bytes 786440 | tf_op jit(solution)/shard_map/weights/ppermute | solution.py:396
  57.1 26.2 %collective-permute-start.17 = (bf16[256,512]{1,0:T(8,128)(2,1)}, bf16[256,512]{1,0:T(8,128)(2,1)}, u32[]{:S(2)}, u32[]{:S(2)}) collective-permute-start(bf16[256,512]{1,0:T(8,128)(2,1)} %bitcast.78), channel_id=1, source_target_pairs={{0,8},{8,0},{16,24},{24,16},{1,9},{9,1},{17,25},{25,17},{2,10},{10... | collective-permute-start | bytes 786440 | tf_op jit(solution)/shard_map/weights/ppermute | solution.py:384
  64.5 20.8 %collective-permute-start.11 = (bf16[256,512]{1,0:T(8,128)(2,1)S(1)}, bf16[256,512]{1,0:T(8,128)(2,1)}, u32[]{:S(2)}, u32[]{:S(2)}) collective-permute-start(bf16[256,512]{1,0:T(8,128)(2,1)S(1)} %collective-permute-done.10), channel_id=1, source_target_pairs={{0,2},{1,3},{2,4},{3,5},{4,6},{5,7},{6,0},{7,1},{8,10},{9,11},{10,... | collective-permute-start | bytes 786440 | tf_op jit(solution)/shard_map/weights/ppermute | solution.py:396
  83.2 70.5 %collective-permute-start.18 = (bf16[256,512]{1,0:T(8,128)(2,1)}, bf16[256,512]{1,0:T(8,128)(2,1)}, u32[]{:S(2)}, u32[]{:S(2)}) collective-permute-start(bf16[256,512]{1,0:T(8,128)(2,1)} %bitcast.78), channel_id=1, source_target_pairs={{0,16},{8,24},{16,0},{24,8},{1,17},{9,25},{17,1},{25,9},{2,18},{10... | collective-permute-start | bytes 786440 | tf_op jit(solution)/shard_map/weights/ppermute | solution.py:388
  83.3 70.4 %collective-permute-start.19 = (bf16[256,512]{1,0:T(8,128)(2,1)}, bf16[256,512]{1,0:T(8,128)(2,1)}, u32[]{:S(2)}, u32[]{:S(2)}) collective-permute-start(bf16[256,512]{1,0:T(8,128)(2,1)} %collective-permute-done.17), channel_id=1, source_target_pairs={{0,16},{8,24},{16,0},{24,8},{1,17},{9,25},{17,1},{25,9},{2,18},{10... | collective-permute-start | bytes 786440 | tf_op jit(solution)/shard_map/weights/ppermute | solution.py:388
  85.4 21.6 %collective-permute-start.12 = (bf16[256,512]{1,0:T(8,128)(2,1)}, bf16[256,512]{1,0:T(8,128)(2,1)}, u32[]{:S(2)}, u32[]{:S(2)}) collective-permute-start(bf16[256,512]{1,0:T(8,128)(2,1)} %collective-permute-done.11), channel_id=1, source_target_pairs={{0,2},{1,3},{2,4},{3,5},{4,6},{5,7},{6,0},{7,1},{8,10},{9,11},{10,... | collective-permute-start | bytes 786440 | tf_op jit(solution)/shard_map/weights/ppermute | solution.py:396
  109.2 15.2 %collective-permute-start.20 = (bf16[256,512]{1,0:T(8,128)(2,1)S(1)}, bf16[256,512]{1,0:T(8,128)(2,1)}, u32[]{:S(2)}, u32[]{:S(2)}) collective-permute-start(bf16[256,512]{1,0:T(8,128)(2,1)S(1)} %bitcast.402), channel_id=1, source_target_pairs={{0,2},{1,3},{2,4},{3,5},{4,6},{5,7},{6,0},{7,1},{8,10},{9,11},{10,... | collective-permute-start | bytes 786440 | tf_op jit(solution)/shard_map/weights/ppermute | solution.py:396
  109.6 53.3 %collective-permute-start.14 = (bf16[1024,512]{1,0:T(8,128)(2,1)}, bf16[1024,512]{1,0:T(8,128)(2,1)}, u32[]{:S(2)}, u32[]{:S(2)}) collective-permute-start(bf16[1024,512]{1,0:T(8,128)(2,1)} %pad_maximum_fusion.6), channel_id=1, source_target_pairs={{0,16},{8,24},{16,0},{24,8},{1,17},{9,25},{17,1},{25,9},{2,18},{10... | collective-permute-start | bytes 3145736 | tf_op jit(solution)/shard_map/weights/ppermute | solution.py:388
  111.0 51.9 %collective-permute-start.13 = (bf16[1024,512]{1,0:T(8,128)(2,1)}, bf16[1024,512]{1,0:T(8,128)(2,1)}, u32[]{:S(2)}, u32[]{:S(2)}) collective-permute-start(bf16[1024,512]{1,0:T(8,128)(2,1)} %pad_maximum_fusion.6), channel_id=1, source_target_pairs={{0,8},{8,0},{16,24},{24,16},{1,9},{9,1},{17,25},{25,17},{2,10},{10... | collective-permute-start | bytes 3145736 | tf_op jit(solution)/shard_map/weights/ppermute | solution.py:384
  124.4 17.9 %collective-permute-start.21 = (bf16[256,512]{1,0:T(8,128)(2,1)}, bf16[256,512]{1,0:T(8,128)(2,1)}, u32[]{:S(2)}, u32[]{:S(2)}) collective-permute-start(bf16[256,512]{1,0:T(8,128)(2,1)} %collective-permute-done.20), channel_id=1, source_target_pairs={{0,2},{1,3},{2,4},{3,5},{4,6},{5,7},{6,0},{7,1},{8,10},{9,11},{10,... | collective-permute-start | bytes 786440 | tf_op jit(solution)/shard_map/weights/ppermute | solution.py:396
  142.3 18.5 %collective-permute-start.22 = (bf16[256,512]{1,0:T(8,128)(2,1)}, bf16[256,512]{1,0:T(8,128)(2,1)S(1)}, u32[]{:S(2)}, u32[]{:S(2)}) collective-permute-start(bf16[256,512]{1,0:T(8,128)(2,1)} %collective-permute-done.21), channel_id=1, source_target_pairs={{0,2},{1,3},{2,4},{3,5},{4,6},{5,7},{6,0},{7,1},{8,10},{9,11},{10,... | collective-permute-start | bytes 786440 | tf_op jit(solution)/shard_map/weights/ppermute | solution.py:396
  147.3 20.0 %all-to-all-start = ((bf16[32,16,256]{2,1,0:T(8,128)(2,1)}), bf16[32,16,256]{2,1,0:T(8,128)(2,1)S(1)}, u32[]{:S(2)}, u32[]{:S(2)}) async-start(bf16[32,16,256]{2,1,0:T(8,128)(2,1)} %bitcast.58), calls=%async_computation | async-start | bytes 524288 | tf_op jit(solution)/shard_map/embedding/all_to_all | solution.py:1352
  153.7 319.5 %reduce-scatter.8.cloned.1.call-start = ((), (), s32[]{:S(2)}) async-start(), calls=%async_computation.11 | async-start | bytes 1310720 | tf_op jit(solution)/shard_map/backward_layers/reduce_scatter | solution.py:1086
  162.9 45.6 %collective-permute-start.27 = (bf16[1024,512]{1,0:T(8,128)(2,1)}, bf16[1024,512]{1,0:T(8,128)(2,1)}, u32[]{:S(2)}, u32[]{:S(2)}) collective-permute-start(bf16[1024,512]{1,0:T(8,128)(2,1)} %pad_maximum_fusion.8), channel_id=1, source_target_pairs={{0,16},{8,24},{16,0},{24,8},{1,17},{9,25},{17,1},{25,9},{2,18},{10... | collective-permute-start | bytes 3145736 | tf_op jit(solution)/shard_map/weights/ppermute | solution.py:388
  163.5 38.5 %collective-permute-start.23 = (bf16[1024,512]{1,0:T(8,128)(2,1)S(1)}, bf16[1024,512]{1,0:T(8,128)(2,1)}, u32[]{:S(2)}, u32[]{:S(2)}) collective-permute-start(bf16[1024,512]{1,0:T(8,128)(2,1)S(1)} %pad_maximum_fusion.7), channel_id=1, source_target_pairs={{0,2},{1,3},{2,4},{3,5},{4,6},{5,7},{6,0},{7,1},{8,10},{9,11},{10,... | collective-permute-start | bytes 3145736 | tf_op jit(solution)/shard_map/weights/ppermute | solution.py:396
  163.9 51.8 %collective-permute-start.15 = (bf16[1024,512]{1,0:T(8,128)(2,1)}, bf16[1024,512]{1,0:T(8,128)(2,1)}, u32[]{:S(2)}, u32[]{:S(2)}) collective-permute-start(bf16[1024,512]{1,0:T(8,128)(2,1)} %collective-permute-done.13), channel_id=1, source_target_pairs={{0,16},{8,24},{16,0},{24,8},{1,17},{9,25},{17,1},{25,9},{2,18},{10... | collective-permute-start | bytes 3145736 | tf_op jit(solution)/shard_map/weights/ppermute | solution.py:388
  171.0 62.6 %collective-permute-start.26 = (bf16[1024,512]{1,0:T(8,128)(2,1)}, bf16[1024,512]{1,0:T(8,128)(2,1)S(1)}, u32[]{:S(2)}, u32[]{:S(2)}) collective-permute-start(bf16[1024,512]{1,0:T(8,128)(2,1)} %pad_maximum_fusion.8), channel_id=1, source_target_pairs={{0,8},{8,0},{16,24},{24,16},{1,9},{9,1},{17,25},{25,17},{2,10},{10... | collective-permute-start | bytes 3145736 | tf_op jit(solution)/shard_map/weights/ppermute | solution.py:384
  202.0 31.6 %collective-permute-start.24 = (bf16[1024,512]{1,0:T(8,128)(2,1)}, bf16[1024,512]{1,0:T(8,128)(2,1)S(1)}, u32[]{:S(2)}, u32[]{:S(2)}) collective-permute-start(bf16[1024,512]{1,0:T(8,128)(2,1)} %collective-permute-done.23), channel_id=1, source_target_pairs={{0,2},{1,3},{2,4},{3,5},{4,6},{5,7},{6,0},{7,1},{8,10},{9,11},{10,... | collective-permute-start | bytes 3145736 | tf_op jit(solution)/shard_map/weights/ppermute | solution.py:396
  208.5 25.1 %collective-permute-start.28 = (bf16[1024,512]{1,0:T(8,128)(2,1)}, bf16[1024,512]{1,0:T(8,128)(2,1)S(1)}, u32[]{:S(2)}, u32[]{:S(2)}) collective-permute-start(bf16[1024,512]{1,0:T(8,128)(2,1)} %collective-permute-done.27), channel_id=1, source_target_pairs={{0,8},{8,0},{16,24},{24,16},{1,9},{9,1},{17,25},{25,17},{2,10},{10... | collective-permute-start | bytes 3145736 | tf_op jit(solution)/shard_map/weights/ppermute | solution.py:384
  251.6 38.6 %collective-permute-start.30 = (bf16[1024,512]{1,0:T(8,128)(2,1)S(1)}, bf16[1024,512]{1,0:T(8,128)(2,1)}, u32[]{:S(2)}, u32[]{:S(2)}) collective-permute-start(bf16[1024,512]{1,0:T(8,128)(2,1)S(1)} %copy-done.144), channel_id=1, source_target_pairs={{0,2},{1,3},{2,4},{3,5},{4,6},{5,7},{6,0},{7,1},{8,10},{9,11},{10,... | collective-permute-start | bytes 3145736 | tf_op jit(solution)/shard_map/weights/ppermute | solution.py:396
  349.8 30.9 %collective-permute-start.38 = (bf16[256,2560]{1,0:T(8,128)(2,1)S(1)}, bf16[256,2560]{1,0:T(8,128)(2,1)S(1)}, u32[]{:S(2)}, u32[]{:S(2)}) collective-permute-start(bf16[256,2560]{1,0:T(8,128)(2,1)S(1)} %backward_layers.41), channel_id=1, source_target_pairs={{0,16},{8,24},{16,0},{24,8},{1,17},{9,25},{17,1},{25,9},{2,18},{10... | collective-permute-start | bytes 3932168 | tf_op jit(solution)/shard_map/backward_layers/ppermute | solution.py:388
  351.2 25.6 %collective-permute-start.37 = (bf16[256,2048]{1,0:T(8,128)(2,1)S(1)}, bf16[256,2048]{1,0:T(8,128)(2,1)S(1)}, u32[]{:S(2)}, u32[]{:S(2)}) collective-permute-start(bf16[256,2048]{1,0:T(8,128)(2,1)S(1)} %backward_layers.40), channel_id=1, source_target_pairs={{0,8},{8,0},{16,24},{24,16},{1,9},{9,1},{17,25},{25,17},{2,10},{10... | collective-permute-start | bytes 3145736 | tf_op jit(solution)/shard_map/backward_layers/ppermute | solution.py:384
  383.5 24.4 %collective-permute-start.40 = (bf16[512,1024]{1,0:T(8,128)(2,1)S(1)}, bf16[512,1024]{1,0:T(8,128)(2,1)S(1)}, u32[]{:S(2)}, u32[]{:S(2)}) collective-permute-start(bf16[512,1024]{1,0:T(8,128)(2,1)S(1)} %backward_layers.44), channel_id=1, source_target_pairs={{0,16},{8,24},{16,0},{24,8},{1,17},{9,25},{17,1},{25,9},{2,18},{10... | collective-permute-start | bytes 3145736 | tf_op jit(solution)/shard_map/backward_layers/ppermute | solution.py:388
  385.0 24.1 %collective-permute-start.41 = (bf16[256,2048]{1,0:T(8,128)(2,1)S(1)}, bf16[256,2048]{1,0:T(8,128)(2,1)S(1)}, u32[]{:S(2)}, u32[]{:S(2)}) collective-permute-start(bf16[256,2048]{1,0:T(8,128)(2,1)S(1)} %backward_layers.45), channel_id=1, source_target_pairs={{0,8},{8,0},{16,24},{24,16},{1,9},{9,1},{17,25},{25,17},{2,10},{10... | collective-permute-start | bytes 3145736 | tf_op jit(solution)/shard_map/backward_layers/ppermute | solution.py:384
  413.6 59.6 %reduce-scatter.10.cloned.1.call-start = ((), (), s32[]{:S(2)}) async-start(), calls=%async_computation.12 | async-start | bytes 1310720 | tf_op jit(solution)/shard_map/backward_layers/reduce_scatter | solution.py:1086
  415.3 25.6 %collective-permute-start.44 = (bf16[256,2048]{1,0:T(8,128)(2,1)S(1)}, bf16[256,2048]{1,0:T(8,128)(2,1)S(1)}, u32[]{:S(2)}, u32[]{:S(2)}) collective-permute-start(bf16[256,2048]{1,0:T(8,128)(2,1)S(1)} %backward_layers.51), channel_id=1, source_target_pairs={{0,16},{8,24},{16,0},{24,8},{1,17},{9,25},{17,1},{25,9},{2,18},{10... | collective-permute-start | bytes 3145736 | tf_op jit(solution)/shard_map/backward_layers/ppermute | solution.py:388
  416.6 14.0 %collective-permute-start.43 = (bf16[256,1024]{1,0:T(8,128)(2,1)S(1)}, bf16[256,1024]{1,0:T(8,128)(2,1)S(1)}, u32[]{:S(2)}, u32[]{:S(2)}) collective-permute-start(bf16[256,1024]{1,0:T(8,128)(2,1)S(1)} %backward_layers.50), channel_id=1, source_target_pairs={{0,8},{8,0},{16,24},{24,16},{1,9},{9,1},{17,25},{25,17},{2,10},{10... | collective-permute-start | bytes 1572872 | tf_op jit(solution)/shard_map/backward_layers/ppermute | solution.py:384
  445.0 4.5 collective-permute-start.45
  445.0 108.4 %reduce-scatter.12.cloned.1.call-start = ((), (), s32[]{:S(2)}) async-start(), calls=%async_computation.13 | async-start | bytes 1310720 | tf_op jit(solution)/shard_map/backward_layers/reduce_scatter | solution.py:1086
  445.1 26.6 %collective-permute-start.48 = (bf16[256,1536]{1,0:T(8,128)(2,1)}, bf16[256,1536]{1,0:T(8,128)(2,1)S(1)}, u32[]{:S(2)}, u32[]{:S(2)}) collective-permute-start(bf16[256,1536]{1,0:T(8,128)(2,1)} %copy-done.111), channel_id=1, source_target_pairs={{0,16},{8,24},{16,0},{24,8},{1,17},{9,25},{17,1},{25,9},{2,18},{10... | collective-permute-start | bytes 2359304 | tf_op jit(solution)/shard_map/backward_layers/ppermute | solution.py:388
  446.4 26.8 %collective-permute-start.47 = (bf16[256,1536]{1,0:T(8,128)(2,1)}, bf16[256,1536]{1,0:T(8,128)(2,1)}, u32[]{:S(2)}, u32[]{:S(2)}) collective-permute-start(bf16[256,1536]{1,0:T(8,128)(2,1)} %copy-done.110), channel_id=1, source_target_pairs={{0,8},{8,0},{16,24},{24,16},{1,9},{9,1},{17,25},{25,17},{2,10},{10... | collective-permute-start | bytes 2359304 | tf_op jit(solution)/shard_map/backward_layers/ppermute | solution.py:384
  447.2 24.5 %collective-permute-start.46 = (bf16[256,512]{1,0:T(8,128)(2,1)}, bf16[256,512]{1,0:T(8,128)(2,1)S(1)}, u32[]{:S(2)}, u32[]{:S(2)}) collective-permute-start(bf16[256,512]{1,0:T(8,128)(2,1)} %copy-done.122), channel_id=1, source_target_pairs={{0,16},{8,24},{16,0},{24,8},{1,17},{9,25},{17,1},{25,9},{2,18},{10... | collective-permute-start | bytes 786440 | tf_op jit(solution)/shard_map/backward_layers/ppermute | solution.py:388
  480.1 38.4 %collective-permute-start.52 = (bf16[256,2560]{1,0:T(8,128)(2,1)}, bf16[256,2560]{1,0:T(8,128)(2,1)S(1)}, u32[]{:S(2)}, u32[]{:S(2)}) collective-permute-start(bf16[256,2560]{1,0:T(8,128)(2,1)} %backward_layers.63), channel_id=1, source_target_pairs={{0,16},{8,24},{16,0},{24,8},{1,17},{9,25},{17,1},{25,9},{2,18},{10... | collective-permute-start | bytes 3932168 | tf_op jit(solution)/shard_map/backward_layers/ppermute | solution.py:388
  481.5 4.7 collective-permute-start.49
  481.5 37.0 %collective-permute-start.51 = (bf16[256,2048]{1,0:T(8,128)(2,1)}, bf16[256,2048]{1,0:T(8,128)(2,1)}, u32[]{:S(2)}, u32[]{:S(2)}) collective-permute-start(bf16[256,2048]{1,0:T(8,128)(2,1)} %backward_layers.62), channel_id=1, source_target_pairs={{0,8},{8,0},{16,24},{24,16},{1,9},{9,1},{17,25},{25,17},{2,10},{10... | collective-permute-start | bytes 3145736 | tf_op jit(solution)/shard_map/backward_layers/ppermute | solution.py:384
  482.3 94.5 %reduce-scatter.14.cloned.1.call-start = ((), (), s32[]{:S(2)}) async-start(), calls=%async_computation.14 | async-start | bytes 655360 | tf_op jit(solution)/shard_map/backward_layers/reduce_scatter | solution.py:1086
  482.3 36.2 %collective-permute-start.50 = (bf16[512,512]{1,0:T(8,128)(2,1)}, bf16[512,512]{1,0:T(8,128)(2,1)S(1)}, u32[]{:S(2)}, u32[]{:S(2)}) collective-permute-start(bf16[512,512]{1,0:T(8,128)(2,1)} %copy-done.114), channel_id=1, source_target_pairs={{0,8},{8,0},{16,24},{24,16},{1,9},{9,1},{17,25},{25,17},{2,10},{10... | collective-permute-start | bytes 1572872 | tf_op jit(solution)/shard_map/backward_layers/ppermute | solution.py:384
  525.0 28.5 %collective-permute-start.54 = (bf16[512,1024]{1,0:T(8,128)(2,1)}, bf16[512,1024]{1,0:T(8,128)(2,1)}, u32[]{:S(2)}, u32[]{:S(2)}) collective-permute-start(bf16[512,1024]{1,0:T(8,128)(2,1)} %backward_layers.67), channel_id=1, source_target_pairs={{0,16},{8,24},{16,0},{24,8},{1,17},{9,25},{17,1},{25,9},{2,18},{10... | collective-permute-start | bytes 3145736 | tf_op jit(solution)/shard_map/backward_layers/ppermute | solution.py:388
  525.6 27.8 %collective-permute-start.55 = (bf16[256,2048]{1,0:T(8,128)(2,1)}, bf16[256,2048]{1,0:T(8,128)(2,1)}, u32[]{:S(2)}, u32[]{:S(2)}) collective-permute-start(bf16[256,2048]{1,0:T(8,128)(2,1)} %backward_layers.68), channel_id=1, source_target_pairs={{0,8},{8,0},{16,24},{24,16},{1,9},{9,1},{17,25},{25,17},{2,10},{10... | collective-permute-start | bytes 3145736 | tf_op jit(solution)/shard_map/backward_layers/ppermute | solution.py:384
  527.0 85.7 %reduce-scatter.16.cloned.1.call-start = ((), (), s32[]{:S(2)}) async-start(), calls=%async_computation.15 | async-start | bytes 1310720 | tf_op jit(solution)/shard_map/backward_layers/reduce_scatter | solution.py:1086
  559.2 54.6 %reduce-scatter.18.cloned.1.call-start = ((), (), s32[]{:S(2)}) async-start(), calls=%async_computation.16 | async-start | bytes 1310720 | tf_op jit(solution)/shard_map/backward_layers/reduce_scatter | solution.py:1086
  563.3 4.3 collective-permute-start.56
  563.4 25.7 %collective-permute-start.58 = (bf16[256,2048]{1,0:T(8,128)(2,1)}, bf16[256,2048]{1,0:T(8,128)(2,1)S(1)}, u32[]{:S(2)}, u32[]{:S(2)}) collective-permute-start(bf16[256,2048]{1,0:T(8,128)(2,1)} %backward_layers.74), channel_id=1, source_target_pairs={{0,16},{8,24},{16,0},{24,8},{1,17},{9,25},{17,1},{25,9},{2,18},{10... | collective-permute-start | bytes 3145736 | tf_op jit(solution)/shard_map/backward_layers/ppermute | solution.py:388
  564.2 14.2 %collective-permute-start.57 = (bf16[256,1024]{1,0:T(8,128)(2,1)}, bf16[256,1024]{1,0:T(8,128)(2,1)S(1)}, u32[]{:S(2)}, u32[]{:S(2)}) collective-permute-start(bf16[256,1024]{1,0:T(8,128)(2,1)} %backward_layers.73), channel_id=1, source_target_pairs={{0,8},{8,0},{16,24},{24,16},{1,9},{9,1},{17,25},{25,17},{2,10},{10... | collective-permute-start | bytes 1572872 | tf_op jit(solution)/shard_map/backward_layers/ppermute | solution.py:384
  593.3 19.4 %collective-permute-start.60 = (bf16[256,1536]{1,0:T(8,128)(2,1)}, bf16[256,1536]{1,0:T(8,128)(2,1)}, u32[]{:S(2)}, u32[]{:S(2)}) collective-permute-start(bf16[256,1536]{1,0:T(8,128)(2,1)} %embedding_back.10), channel_id=1, source_target_pairs={{0,8},{8,0},{16,24},{24,16},{1,9},{9,1},{17,25},{25,17},{2,10},{10... | collective-permute-start | bytes 2359304 | tf_op jit(solution)/shard_map/embedding_back/ppermute | solution.py:384
  594.0 10.5 %collective-permute-start.59 = (bf16[256,512]{1,0:T(8,128)(2,1)}, bf16[256,512]{1,0:T(8,128)(2,1)}, u32[]{:S(2)}, u32[]{:S(2)}) collective-permute-start(bf16[256,512]{1,0:T(8,128)(2,1)} %embedding_back.9), channel_id=1, source_target_pairs={{0,16},{8,24},{16,0},{24,8},{1,17},{9,25},{17,1},{25,9},{2,18},{10... | collective-permute-start | bytes 786440 | tf_op jit(solution)/shard_map/embedding_back/ppermute | solution.py:388
  618.0 20.1 %all-to-all-start.1 = ((bf16[32,32,256]{2,1,0:T(8,128)(2,1)}), bf16[32,32,256]{2,1,0:T(8,128)(2,1)}, u32[]{:S(2)}, u32[]{:S(2)}) async-start(bf16[32,32,256]{2,1,0:T(8,128)(2,1)} %embedding_back.8), calls=%async_computation.7 | async-start | bytes 1048576 | tf_op jit(solution)/shard_map/embedding_back/all_to_all | solution.py:1428
  621.4 32.2 %reduce-scatter.20.cloned.1.call-start = ((), (), s32[]{:S(2)}) async-start(), calls=%async_computation.17 | async-start | bytes 1310720 | tf_op jit(solution)/shard_map/embedding_back/reduce_scatter | solution.py:1086
  622.5 4.3 collective-permute-start.65
  622.9 5.2 collective-permute-start.63
  623.0 7.1 collective-permute-start.64
  661.6 7.2 %collective-permute-start.62 = (bf16[32,2048]{1,0:T(8,128)(2,1)S(1)}, bf16[32,2048]{1,0:T(8,128)(2,1)S(1)}, u32[]{:S(2)}, u32[]{:S(2)}) collective-permute-start(bf16[32,2048]{1,0:T(8,128)(2,1)S(1)} %dynamic-slice_bitcast_fusion.3), channel_id=1, source_target_pairs={{0,1},{1,0},{2,3},{3,2},{4,5},{5,4},{6,7},{7,6},{8,9},{9,8},{10,11... | collective-permute-start | bytes 393224 | tf_op jit(solution)/shard_map/own_grads/ppermute | solution.py:392
  668.4 5.5 collective-permute-start.61
  680.9 11.7 %all-to-all-start.2 = ((f32[32,8,128]{2,1,0:T(8,128)}), f32[32,8,128]{2,1,0:T(8,128)S(1)}, u32[]{:S(2)}, u32[]{:S(2)}) async-start(f32[32,8,128]{2,1,0:T(8,128)} %broadcast_in_dim.109), calls=%async_computation.9 | async-start | bytes 262144 | tf_op jit(solution)/shard_map/clip_and_update/all_to_all | solution.py:1478
  (181 other events, 1141.2 us)
Sparse Core Ops, SparseCore 0:
  20.9 191.1 all-gather.5
  215.4 104.9 all-gather.3
  413.7 25.7 reduce-scatter.7
  445.1 25.8 reduce-scatter.9
  482.4 25.7 reduce-scatter.11
  527.1 20.3 reduce-scatter.13
  559.4 25.6 reduce-scatter.15
  588.0 25.8 reduce-scatter.17
  625.2 28.2 reduce-scatter.19

commit v3 on v2

--- a/solution.py
+++ b/solution.py
@@ -986,7 +986,12 @@
                 ref[...].astype(WIDE) for ref in ins[4 * number : 4 * number + 4]
             ]
             scale = factor.reshape((1,) * grad.ndim)
-            new = adamw(master, moment, square, scale * grad, rates[number], decays[number])
+            grad = scale * grad
+            moment = BETA_ONE * moment + (1.0 - BETA_ONE) * grad
+            square = BETA_TWO * square + (1.0 - BETA_TWO) * grad * grad
+            root = jnp.sqrt(square * (1.0 / (1.0 - BETA_TWO**STEP))) + ADAM_EPS
+            step = moment * (1.0 / (1.0 - BETA_ONE**STEP)) / root
+            new = (moment, square, master - rates[number] * (step + decays[number] * master))
             for ref, item in zip(outs[3 * number : 3 * number + 3], new):
                 ref[...] = item
 
@@ -1311,9 +1316,9 @@
             return whole, in_place
 
         third = in_background(lowered[0], bridge, flat(paired[1, :4]))
-        fourth = in_background(flat(paired[1, 4:]))
+        fourth = in_background(lowered[1])
         first_line, first_square, first = by_permutes(flat(paired[0, :4]), line, line, True)
-        last_own = tie((lowered[1], line))[0]
+        last_own = tie((flat(paired[1, 4:]), line))[0]
         beside, across = swap_x(last_own), swap_y(last_own)
         square = jnp.concatenate([last_own, beside, across, swap_y(beside)], 0)
         second_line, _, second = by_permutes(
@@ -1322,7 +1327,7 @@
         last = along_z(tie((square, second_line))[0])
         fifth = (jnp.concatenate(last, 0).reshape((16,) + last_own.shape), both_shifted)
         mats_zero = ((first, 0), (second, 0), (third, 0))
-        mats_one = ((third, lowered.shape[1] + bridge.shape[0]), (fourth, 0), (fifth, 0))
+        mats_one = ((third, lowered.shape[1] + bridge.shape[0]), (fifth, 0), (fourth, 0))
         bridge_mat = (third, lowered.shape[1])
 
     with jax.named_scope("embedding"):
@@ -1426,13 +1431,15 @@
         (both,) = flow.turn(both)
         own_sent = both = both.reshape(64 * blocks, TAPS_OUT * outs)
         both = lax.all_to_all(both, BOTH, 0, 0, tiled=True)
-        both, shares_zero[0].total = tie((both, shares_zero[0].total))
         both = both.reshape(32, 2 * blocks, TAPS_OUT * outs)
         own = both[:, :blocks].reshape(32 * blocks, TAPS_OUT * outs)
         mine, other, spread = banded_back(own, conv_out, windows, banded, scalars)
+        small = tie((both[:, blocks:], mine))[0]
+        grad_kernel = kernel_grad(spread, taps, outs, scalars)
+        mine, other, grad_kernel, shares_zero[0].total = tie(
+            (mine, other, grad_kernel, shares_zero[0].total)
+        )
         grad_input = input_grad(own, mine, swap_core(other), valid_rows, strided, scalars)
-        spread, small = tie((spread, both[:, blocks:]))
-        grad_kernel = kernel_grad(spread, taps, outs, scalars)
         small = jnp.sum(small.astype(WIDE), 0)
         grad_readout = jnp.concatenate([small[:, :mel_count], small[:, 128 : 128 + mel_count]], 0)
         grad_gains = small[:5, 96 : 96 + outs]
@@ -1447,8 +1454,10 @@
             return jnp.moveaxis(cut, 0, 2).reshape(both.shape[1], 2 * both.shape[2])
 
         layer_grads = []
+        last_total = tie((shares_zero[0].total, grad_input))[0]
         for joint_share, expand_share, reduce_share in (shares_zero, shares_one):
-            both = own_rows(joint_share.total, core)
+            joint_total = last_total if joint_share is shares_zero[0] else joint_share.total
+            both = own_rows(joint_total, core)
             layer_grads.append(
                 (
                     unfolded(both[:, :, : 3 * LANES], 3),

time: 726 us -> 713 us (0.982)
    reduce_scatter x7, waiting for transfers between devices: 16.6 us -> 4.06 us  [send(): lax.psum_scatter(self.made, 'fsdp', scatter_dimension=0, axis_index_group...]
    ppermute x12, waiting for transfers between devices: 99 us -> 111 us  [shift_z(): lax.ppermute(item, 'fsdp', [(i, (i + 2 * hops) % 8) for i in range(8)])]
    unnamed x352 -> x356, local copies, waits for them, and re-layouts: 71.1 us -> 76.6 us
  transfers between devices with their start and end apart: 79 -> 79, of which waited for: 39 -> 38; matrix products, arithmetic and copies ran while one was open for 14% -> 15% of each run, Pallas kernels for 16% -> 18%
where the time goes in v3:
time: 713 us; the launch traced here: 710 us
  waiting for transfers between devices  253 us (35%)
  Pallas kernels  160 us (22%)
  local copies, waits for them, and re-layouts  141 us (20%)
  starting transfers between devices  80 us (11%)
  other arithmetic  53.1 us (7%)
  between operations  18.1 us (3%)
    ppermute x12, waiting for transfers between devices, shift_z(): lax.ppermute(item, 'fsdp', [(i, (i + 2 * hops) % 8) for i in range(8)])  111 us
    unnamed x356, local copies, waits for them, and re-layouts  76.6 us
    ppermute x14, waiting for transfers between devices, swap_x(): return lax.ppermute(item, 'dp', [(i, i ^ 1) for i in range(4)])  65.7 us
    ppermute x16, waiting for transfers between devices, swap_y(): return lax.ppermute(item, 'dp', [(i, i ^ 2) for i in range(4)])  40.3 us
    pallas_call x22, Pallas kernels, one_step(): pl.pallas_call(body, grid_spec=pltpu.PrefetchScalarGridSpec(num_scalar_pr...  36.1 us
    pallas_call x9, Pallas kernels, piece_dot_back(): pl.pallas_call(body, grid_spec=pltpu.PrefetchScalarGridSpec(num_scalar_pr...  27.7 us
    ppermute x12, starting transfers between devices, shift_z(): lax.ppermute(item, 'fsdp', [(i, (i + 2 * hops) % 8) for i in range(8)])  27.1 us
    pallas_call x18, Pallas kernels, outer_sum(): pl.pallas_call(body, grid_spec=pltpu.PrefetchScalarGridSpec(num_scalar_pr...  24.1 us
  transfers between devices with their start and end apart: 79, of which 38 were waited for; matrix products, arithmetic and copies ran while one was open for 15% of the time, Pallas kernels for 18%

profile of v3, /device:TPU:0, one launch (start us, length us, event | category | flops | bytes accessed | tf_op | source)
XLA Modules:
  0.0 709.8 jit_solution(3808640827574709297)
XLA Ops:
  11.7 3.3 dynamic-slice_reduce_fusion.1
  21.6 5.0 collective-permute-start.2
  29.4 3.2 collective-permute-done
  35.9 7.3 %collective-permute-done.3 = bf16[4,208,128]{2,1,0:T(8,128)(2,1)S(1)} collective-permute-done((bf16[4,208,128]{2,1,0:T(8,128)(2,1)S(1)}, bf16[4,208,128]{2,1,0:T(8,128)(2,1)S(1)}, u32[]{:S(2)}, u32[]{:S(2)}) %collective-permute-start.3) | collective-permute-done | bytes 213024 | tf_op jit(solution)/shard_map/features/ppermute | solution.py:384
  44.7 4.9 collective-permute-done.5
  56.1 7.6 %collective-permute-done.10 = bf16[256,512]{1,0:T(8,128)(2,1)S(1)} collective-permute-done((bf16[256,512]{1,0:T(8,128)(2,1)S(1)}, bf16[256,512]{1,0:T(8,128)(2,1)S(1)}, u32[]{:S(2)}, u32[]{:S(2)}) %collective-permute-start.10) | collective-permute-done | bytes 262176 | tf_op jit(solution)/shard_map/weights/ppermute | solution.py:396
  63.7 3.4 collective-permute-start.11
  67.9 6.4 copy.175
  74.3 6.5 reshape.312
  84.4 3.1 collective-permute-start.12
  98.8 4.1 concatenate.98
  112.7 10.8 %collective-permute-done.20 = bf16[256,512]{1,0:T(8,128)(2,1)} collective-permute-done((bf16[256,512]{1,0:T(8,128)(2,1)S(1)}, bf16[256,512]{1,0:T(8,128)(2,1)}, u32[]{:S(2)}, u32[]{:S(2)}) %collective-permute-start.20) | collective-permute-done | bytes 262176 | tf_op jit(solution)/shard_map/weights/ppermute | solution.py:396
  129.6 3.3 copy.177
  135.8 6.8 collective-permute-done.21
  142.6 3.3 collective-permute-start.22
  146.8 5.8 all-to-all-start
  153.9 5.5 collective-permute-done.22
  166.4 4.0 collective-permute-start.8
  172.6 2.6 collective-permute-start.26
  175.2 25.4 %collective-permute-done.23 = bf16[1024,512]{1,0:T(8,128)(2,1)} collective-permute-done((bf16[1024,512]{1,0:T(8,128)(2,1)S(1)}, bf16[1024,512]{1,0:T(8,128)(2,1)}, u32[]{:S(2)}, u32[]{:S(2)}) %collective-permute-start.23) | collective-permute-done | bytes 1048608 | tf_op jit(solution)/shard_map/weights/ppermute | solution.py:396
  200.7 6.5 collective-permute-start.24
  208.6 5.7 collective-permute-done.15
  219.1 6.4 forward_layers.17
  228.3 9.8 %collective-permute-done.24 = bf16[1024,512]{1,0:T(8,128)(2,1)S(1)} collective-permute-done((bf16[1024,512]{1,0:T(8,128)(2,1)}, bf16[1024,512]{1,0:T(8,128)(2,1)S(1)}, u32[]{:S(2)}, u32[]{:S(2)}) %collective-permute-start.24) | collective-permute-done | bytes 1048608 | tf_op jit(solution)/shard_map/weights/ppermute | solution.py:396
  241.3 3.5 forward_layers.20
  249.0 4.4 copy-done
  253.4 2.6 forward_layers.21
  259.2 41.9 %collective-permute-done.30 = bf16[1024,512]{1,0:T(8,128)(2,1)} collective-permute-done((bf16[1024,512]{1,0:T(8,128)(2,1)S(1)}, bf16[1024,512]{1,0:T(8,128)(2,1)}, u32[]{:S(2)}, u32[]{:S(2)}) %collective-permute-start.30) | collective-permute-done | bytes 1048608 | tf_op jit(solution)/shard_map/weights/ppermute | solution.py:396
  308.0 6.4 forward_layers.25
  316.2 4.0 copy-done.2
  325.4 3.5 forward_layers.28
  334.4 2.6 forward_layers.29
  348.9 4.2 backward_layers.38.grads_ref.right_ref
  353.3 3.5 backward_layers.39.mine_ref
  359.5 2.7 collective-permute-done.36.other_ref
  365.5 19.5 %collective-permute-done.37.far_left_ref.far_right_ref = bf16[256,2048]{1,0:T(8,128)(2,1)S(1)} collective-permute-done((bf16[256,2048]{1,0:T(8,128)(2,1)S(1)}, bf16[256,2048]{1,0:T(8,128)(2,1)S(1)}, u32[]{:S(2)}, u32[]{:S(2)}) %collective-permute-start.37) | collective-permute-done | bytes 1048608 | tf_op jit(solution)/shard_map/backward_layers/ppermute | solution.py:384
  385.0 4.0 collective-permute-done.38.far_left_ref.far_right_ref
  395.1 8.6 %backward_layers.46.grads_ref.right_ref = bf16[256,1536]{1,0:T(8,128)(2,1)S(1)} custom-call(f32[8]{0:T(128)S(1)} %multiply_power_fusion.slopes_ref, bf16[256,1536]{1,0:T(8,128)(2,1)S(1)} %copy-done.56, f32[256,512]{1,0:T(8,128)S(1)} %get-tuple-element.242.mine_ref, f32[256,512]{1,0:T(8,128)S(1)} %collective-permute-done.39.other_ref, ...), custom_call_target="tpu_custom_call" | custom-call | flops 1000 | bytes 1000 | tf_op jit(solution)/shard_map/backward_layers/pallas_call | solution.py:688
  408.1 2.8 backward_layers.47.mine_ref
  411.0 5.3 collective-permute-done.40
  418.6 3.2 add_convert_fusion.3
  428.7 4.3 copy-done.3
  433.0 2.9 backward_layers.53
  435.9 3.0 collective-permute-done.43.far_left_ref.far_right_ref
  438.9 10.2 %collective-permute-done.44.far_left_ref.far_right_ref = bf16[256,2048]{1,0:T(8,128)(2,1)S(1)} collective-permute-done((bf16[256,2048]{1,0:T(8,128)(2,1)S(1)}, bf16[256,2048]{1,0:T(8,128)(2,1)S(1)}, u32[]{:S(2)}, u32[]{:S(2)}) %collective-permute-start.44) | collective-permute-done | bytes 1048608 | tf_op jit(solution)/shard_map/backward_layers/ppermute | solution.py:388
  457.7 2.7 add.370.joined_ref
  460.5 4.8 copy-done.4
  465.4 4.6 backward_layers.57.grads_ref.right_ref
  474.2 4.5 backward_layers.58.mine_ref
  497.1 3.8 backward_layers.64
  503.9 24.4 %collective-permute-done.50 = bf16[512,512]{1,0:T(8,128)(2,1)S(1)} collective-permute-done((bf16[512,512]{1,0:T(8,128)(2,1)}, bf16[512,512]{1,0:T(8,128)(2,1)S(1)}, u32[]{:S(2)}, u32[]{:S(2)}) %collective-permute-start.50) | collective-permute-done | bytes 524320 | tf_op jit(solution)/shard_map/backward_layers/ppermute | solution.py:384
  528.3 2.9 backward_layers.67
  542.7 8.6 %backward_layers.69.grads_ref.right_ref = bf16[256,1536]{1,0:T(8,128)(2,1)S(1)} custom-call(f32[8]{0:T(128)S(1)} %multiply_power_fusion.slopes_ref, bf16[256,1536]{1,0:T(8,128)(2,1)S(1)} %copy-done.58, f32[256,512]{1,0:T(8,128)S(1)} %copy-done.113, f32[256,512]{1,0:T(8,128)S(1)} %copy-done.117, f32[2,1,128]{2,1,0:T(1,128)S(1)} %constant_dynamic-slice_fusion.valid_ref), custom_call_target="tpu_custom_call" | custom-call | flops 1000 | bytes 1000 | tf_op jit(solution)/shard_map/backward_layers/pallas_call | solution.py:688
  559.5 2.8 backward_layers.70.mine_ref
  563.3 3.3 add_convert_fusion.1
  588.9 10.1 %collective-permute-done.58.far_left_ref.far_right_ref = bf16[256,2048]{1,0:T(8,128)(2,1)S(1)} collective-permute-done((bf16[256,2048]{1,0:T(8,128)(2,1)}, bf16[256,2048]{1,0:T(8,128)(2,1)S(1)}, u32[]{:S(2)}, u32[]{:S(2)}) %collective-permute-start.58) | collective-permute-done | bytes 1048608 | tf_op jit(solution)/shard_map/backward_layers/ppermute | solution.py:388
  605.9 3.9 copy.193.strided_ref
  614.3 8.3 %collective-permute-done.60 = bf16[256,1536]{1,0:T(8,128)(2,1)} collective-permute-done((bf16[256,1536]{1,0:T(8,128)(2,1)}, bf16[256,1536]{1,0:T(8,128)(2,1)}, u32[]{:S(2)}, u32[]{:S(2)}) %collective-permute-start.60) | collective-permute-done | bytes 786464 | tf_op jit(solution)/shard_map/embedding_back/ppermute | solution.py:384
  629.3 3.4 all-to-all-start.1
  652.5 4.8 embedding_back.13
  659.0 6.6 embedding_back.14.refs_2_.refs_7_
  675.8 2.6 all-to-all-start.2
  680.6 6.0 all-to-all-done.2
  687.2 14.4 %clip_and_update.5 = (f32[8,128]{1,0:T(8,128)}, f32[32,256]{1,0:T(8,128)}, f32[32,256]{1,0:T(8,128)}, f32[32,256]{1,0:T(8,128)}, f32[31,32,64]{2,1,0:T(8,128)}, ...) custom-call(s32[17]{0:T(128)} %copy-done.119, ...), custom_call_target="tpu_custom_call" | custom-call | flops 1000 | bytes 1000 | tf_op jit(solution)/shard_map/clip_and_update/pallas_call | solution.py:1016
  (715 shorter events, 275.2 us)
Async XLA Ops:
  7.2 241.7 %all-gather.6.cloned.1.call-start = ((), (), s32[]{:S(2)}) async-start(), calls=%async_computation.18 | async-start | bytes 11141120 | tf_op jit(solution)/shard_map/weights/all_gather | solution.py:1315
  19.8 312.4 %all-gather.4.cloned.1.call-start = ((), (), s32[]{:S(2)}) async-start(), calls=%async_computation.10 | async-start | bytes 4456448 | tf_op jit(solution)/shard_map/weights/all_gather | solution.py:1315
  21.6 11.0 %collective-permute-start.2 = (bf16[208,128]{1,0:T(8,128)(2,1)S(1)}, bf16[208,128]{1,0:T(8,128)(2,1)S(1)}, u32[]{:S(2)}, u32[]{:S(2)}) collective-permute-start(bf16[208,128]{1,0:T(8,128)(2,1)S(1)} %concatenate.93), channel_id=1, source_target_pairs={{0,6},{1,7},{2,0},{3,1},{4,2},{5,3},{6,4},{7,5},{8,14},{9,15},{10,... | collective-permute-start | bytes 159752 | tf_op jit(solution)/shard_map/features/ppermute | solution.py:396
  26.6 6.0 collective-permute-start.1
  26.6 6.0 collective-permute-start
  27.6 54.6 %collective-permute-start.7 = (bf16[256,32]{0,1:T(8,128)(2,1)S(1)}, bf16[256,32]{0,1:T(8,128)(2,1)S(1)}, u32[]{:S(2)}, u32[]{:S(2)}) collective-permute-start(bf16[256,32]{0,1:T(8,128)(2,1)S(1)} %convert_element_type.210), channel_id=1, source_target_pairs={{0,1},{1,0},{2,3},{3,2},{4,5},{5,4},{6,7},{7,6},{8,9},{9,8},{10,11... | collective-permute-start | bytes 49160 | tf_op jit(solution)/shard_map/embedding/ppermute | solution.py:392
  32.7 12.0 %collective-permute-start.4 = (bf16[4,208,128]{2,1,0:T(8,128)(2,1)S(1)}, bf16[4,208,128]{2,1,0:T(8,128)(2,1)S(1)}, u32[]{:S(2)}, u32[]{:S(2)}) collective-permute-start(bf16[4,208,128]{2,1,0:T(8,128)(2,1)S(1)} %bitcast_dynamic-update-slice_fusion.4), channel_id=1, source_target_pairs={{0,16},{8,24},{16,0},{24,8},{1,17},{9,25},{17,1},{25,9},{2,18},{10... | collective-permute-start | bytes 638984 | tf_op jit(solution)/shard_map/features/ppermute | solution.py:388
  34.2 8.9 %collective-permute-start.3 = (bf16[4,208,128]{2,1,0:T(8,128)(2,1)S(1)}, bf16[4,208,128]{2,1,0:T(8,128)(2,1)S(1)}, u32[]{:S(2)}, u32[]{:S(2)}) collective-permute-start(bf16[4,208,128]{2,1,0:T(8,128)(2,1)S(1)} %bitcast_dynamic-update-slice_fusion.4), channel_id=1, source_target_pairs={{0,8},{8,0},{16,24},{24,16},{1,9},{9,1},{17,25},{25,17},{2,10},{10... | collective-permute-start | bytes 638984 | tf_op jit(solution)/shard_map/features/ppermute | solution.py:384
  43.2 6.5 collective-permute-start.5
  49.7 37.8 %collective-permute-start.6 = (bf16[16,208,128]{2,1,0:T(8,128)(2,1)S(1)}, bf16[16,208,128]{2,1,0:T(8,128)(2,1)}, u32[]{:S(2)}, u32[]{:S(2)}) collective-permute-start(bf16[16,208,128]{2,1,0:T(8,128)(2,1)S(1)} %bitcast.389), channel_id=1, source_target_pairs={{0,1},{1,0},{2,3},{3,2},{4,5},{5,4},{6,7},{7,6},{8,9},{9,8},{10,11... | collective-permute-start | bytes 2555912 | tf_op jit(solution)/shard_map/features/ppermute | solution.py:392
  51.4 12.4 %collective-permute-start.10 = (bf16[256,512]{1,0:T(8,128)(2,1)S(1)}, bf16[256,512]{1,0:T(8,128)(2,1)S(1)}, u32[]{:S(2)}, u32[]{:S(2)}) collective-permute-start(bf16[256,512]{1,0:T(8,128)(2,1)S(1)} %bitcast.409), channel_id=1, source_target_pairs={{0,2},{1,3},{2,4},{3,5},{4,6},{5,7},{6,0},{7,1},{8,10},{9,11},{10,... | collective-permute-start | bytes 786440 | tf_op jit(solution)/shard_map/weights/ppermute | solution.py:396
  55.5 26.9 %collective-permute-start.17 = (bf16[256,512]{1,0:T(8,128)(2,1)}, bf16[256,512]{1,0:T(8,128)(2,1)}, u32[]{:S(2)}, u32[]{:S(2)}) collective-permute-start(bf16[256,512]{1,0:T(8,128)(2,1)} %bitcast.77), channel_id=1, source_target_pairs={{0,8},{8,0},{16,24},{24,16},{1,9},{9,1},{17,25},{25,17},{2,10},{10... | collective-permute-start | bytes 786440 | tf_op jit(solution)/shard_map/weights/ppermute | solution.py:384
  63.7 20.7 %collective-permute-start.11 = (bf16[256,512]{1,0:T(8,128)(2,1)S(1)}, bf16[256,512]{1,0:T(8,128)(2,1)}, u32[]{:S(2)}, u32[]{:S(2)}) collective-permute-start(bf16[256,512]{1,0:T(8,128)(2,1)S(1)} %collective-permute-done.10), channel_id=1, source_target_pairs={{0,2},{1,3},{2,4},{3,5},{4,6},{5,7},{6,0},{7,1},{8,10},{9,11},{10,... | collective-permute-start | bytes 786440 | tf_op jit(solution)/shard_map/weights/ppermute | solution.py:396
  82.3 70.3 %collective-permute-start.18 = (bf16[256,512]{1,0:T(8,128)(2,1)}, bf16[256,512]{1,0:T(8,128)(2,1)}, u32[]{:S(2)}, u32[]{:S(2)}) collective-permute-start(bf16[256,512]{1,0:T(8,128)(2,1)} %bitcast.77), channel_id=1, source_target_pairs={{0,16},{8,24},{16,0},{24,8},{1,17},{9,25},{17,1},{25,9},{2,18},{10... | collective-permute-start | bytes 786440 | tf_op jit(solution)/shard_map/weights/ppermute | solution.py:388
  82.4 70.2 %collective-permute-start.19 = (bf16[256,512]{1,0:T(8,128)(2,1)}, bf16[256,512]{1,0:T(8,128)(2,1)}, u32[]{:S(2)}, u32[]{:S(2)}) collective-permute-start(bf16[256,512]{1,0:T(8,128)(2,1)} %collective-permute-done.17), channel_id=1, source_target_pairs={{0,16},{8,24},{16,0},{24,8},{1,17},{9,25},{17,1},{25,9},{2,18},{10... | collective-permute-start | bytes 786440 | tf_op jit(solution)/shard_map/weights/ppermute | solution.py:388
  84.4 21.9 %collective-permute-start.12 = (bf16[256,512]{1,0:T(8,128)(2,1)}, bf16[256,512]{1,0:T(8,128)(2,1)}, u32[]{:S(2)}, u32[]{:S(2)}) collective-permute-start(bf16[256,512]{1,0:T(8,128)(2,1)} %collective-permute-done.11), channel_id=1, source_target_pairs={{0,2},{1,3},{2,4},{3,5},{4,6},{5,7},{6,0},{7,1},{8,10},{9,11},{10,... | collective-permute-start | bytes 786440 | tf_op jit(solution)/shard_map/weights/ppermute | solution.py:396
  108.3 15.2 %collective-permute-start.20 = (bf16[256,512]{1,0:T(8,128)(2,1)S(1)}, bf16[256,512]{1,0:T(8,128)(2,1)}, u32[]{:S(2)}, u32[]{:S(2)}) collective-permute-start(bf16[256,512]{1,0:T(8,128)(2,1)S(1)} %bitcast.407), channel_id=1, source_target_pairs={{0,2},{1,3},{2,4},{3,5},{4,6},{5,7},{6,0},{7,1},{8,10},{9,11},{10,... | collective-permute-start | bytes 786440 | tf_op jit(solution)/shard_map/weights/ppermute | solution.py:396
  109.2 52.3 %collective-permute-start.14 = (bf16[1024,512]{1,0:T(8,128)(2,1)}, bf16[1024,512]{1,0:T(8,128)(2,1)}, u32[]{:S(2)}, u32[]{:S(2)}) collective-permute-start(bf16[1024,512]{1,0:T(8,128)(2,1)} %pad_maximum_fusion.6), channel_id=1, source_target_pairs={{0,16},{8,24},{16,0},{24,8},{1,17},{9,25},{17,1},{25,9},{2,18},{10... | collective-permute-start | bytes 3145736 | tf_op jit(solution)/shard_map/weights/ppermute | solution.py:388
  110.5 51.0 %collective-permute-start.13 = (bf16[1024,512]{1,0:T(8,128)(2,1)}, bf16[1024,512]{1,0:T(8,128)(2,1)}, u32[]{:S(2)}, u32[]{:S(2)}) collective-permute-start(bf16[1024,512]{1,0:T(8,128)(2,1)} %pad_maximum_fusion.6), channel_id=1, source_target_pairs={{0,8},{8,0},{16,24},{24,16},{1,9},{9,1},{17,25},{25,17},{2,10},{10... | collective-permute-start | bytes 3145736 | tf_op jit(solution)/shard_map/weights/ppermute | solution.py:384
  123.5 19.1 %collective-permute-start.21 = (bf16[256,512]{1,0:T(8,128)(2,1)}, bf16[256,512]{1,0:T(8,128)(2,1)}, u32[]{:S(2)}, u32[]{:S(2)}) collective-permute-start(bf16[256,512]{1,0:T(8,128)(2,1)} %collective-permute-done.20), channel_id=1, source_target_pairs={{0,2},{1,3},{2,4},{3,5},{4,6},{5,7},{6,0},{7,1},{8,10},{9,11},{10,... | collective-permute-start | bytes 786440 | tf_op jit(solution)/shard_map/weights/ppermute | solution.py:396
  142.6 16.8 %collective-permute-start.22 = (bf16[256,512]{1,0:T(8,128)(2,1)}, bf16[256,512]{1,0:T(8,128)(2,1)S(1)}, u32[]{:S(2)}, u32[]{:S(2)}) collective-permute-start(bf16[256,512]{1,0:T(8,128)(2,1)} %collective-permute-done.21), channel_id=1, source_target_pairs={{0,2},{1,3},{2,4},{3,5},{4,6},{5,7},{6,0},{7,1},{8,10},{9,11},{10,... | collective-permute-start | bytes 786440 | tf_op jit(solution)/shard_map/weights/ppermute | solution.py:396
  146.8 18.7 %all-to-all-start = ((bf16[32,16,256]{2,1,0:T(8,128)(2,1)}), bf16[32,16,256]{2,1,0:T(8,128)(2,1)S(1)}, u32[]{:S(2)}, u32[]{:S(2)}) async-start(bf16[32,16,256]{2,1,0:T(8,128)(2,1)} %bitcast.58), calls=%async_computation | async-start | bytes 524288 | tf_op jit(solution)/shard_map/embedding/all_to_all | solution.py:1357
  152.5 328.9 %reduce-scatter.8.cloned.1.call-start = ((), (), s32[]{:S(2)}) async-start(), calls=%async_computation.11 | async-start | bytes 1310720 | tf_op jit(solution)/shard_map/backward_layers/reduce_scatter | solution.py:1091
  161.5 45.8 %collective-permute-start.27 = (bf16[1024,512]{1,0:T(8,128)(2,1)}, bf16[1024,512]{1,0:T(8,128)(2,1)}, u32[]{:S(2)}, u32[]{:S(2)}) collective-permute-start(bf16[1024,512]{1,0:T(8,128)(2,1)} %pad_maximum_fusion.8), channel_id=1, source_target_pairs={{0,16},{8,24},{16,0},{24,8},{1,17},{9,25},{17,1},{25,9},{2,18},{10... | collective-permute-start | bytes 3145736 | tf_op jit(solution)/shard_map/weights/ppermute | solution.py:388
  162.7 38.0 %collective-permute-start.23 = (bf16[1024,512]{1,0:T(8,128)(2,1)S(1)}, bf16[1024,512]{1,0:T(8,128)(2,1)}, u32[]{:S(2)}, u32[]{:S(2)}) collective-permute-start(bf16[1024,512]{1,0:T(8,128)(2,1)S(1)} %pad_maximum_fusion.7), channel_id=1, source_target_pairs={{0,2},{1,3},{2,4},{3,5},{4,6},{5,7},{6,0},{7,1},{8,10},{9,11},{10,... | collective-permute-start | bytes 3145736 | tf_op jit(solution)/shard_map/weights/ppermute | solution.py:396
  162.7 51.6 %collective-permute-start.15 = (bf16[1024,512]{1,0:T(8,128)(2,1)}, bf16[1024,512]{1,0:T(8,128)(2,1)}, u32[]{:S(2)}, u32[]{:S(2)}) collective-permute-start(bf16[1024,512]{1,0:T(8,128)(2,1)} %collective-permute-done.13), channel_id=1, source_target_pairs={{0,16},{8,24},{16,0},{24,8},{1,17},{9,25},{17,1},{25,9},{2,18},{10... | collective-permute-start | bytes 3145736 | tf_op jit(solution)/shard_map/weights/ppermute | solution.py:388
  166.4 5.1 collective-permute-start.8
  172.6 65.5 %collective-permute-start.26 = (bf16[1024,512]{1,0:T(8,128)(2,1)}, bf16[1024,512]{1,0:T(8,128)(2,1)S(1)}, u32[]{:S(2)}, u32[]{:S(2)}) collective-permute-start(bf16[1024,512]{1,0:T(8,128)(2,1)} %pad_maximum_fusion.8), channel_id=1, source_target_pairs={{0,8},{8,0},{16,24},{24,16},{1,9},{9,1},{17,25},{25,17},{2,10},{10... | collective-permute-start | bytes 3145736 | tf_op jit(solution)/shard_map/weights/ppermute | solution.py:384
  200.7 37.5 %collective-permute-start.24 = (bf16[1024,512]{1,0:T(8,128)(2,1)}, bf16[1024,512]{1,0:T(8,128)(2,1)S(1)}, u32[]{:S(2)}, u32[]{:S(2)}) collective-permute-start(bf16[1024,512]{1,0:T(8,128)(2,1)} %collective-permute-done.23), channel_id=1, source_target_pairs={{0,2},{1,3},{2,4},{3,5},{4,6},{5,7},{6,0},{7,1},{8,10},{9,11},{10,... | collective-permute-start | bytes 3145736 | tf_op jit(solution)/shard_map/weights/ppermute | solution.py:396
  207.2 30.9 %collective-permute-start.28 = (bf16[1024,512]{1,0:T(8,128)(2,1)}, bf16[1024,512]{1,0:T(8,128)(2,1)S(1)}, u32[]{:S(2)}, u32[]{:S(2)}) collective-permute-start(bf16[1024,512]{1,0:T(8,128)(2,1)} %collective-permute-done.27), channel_id=1, source_target_pairs={{0,8},{8,0},{16,24},{24,16},{1,9},{9,1},{17,25},{25,17},{2,10},{10... | collective-permute-start | bytes 3145736 | tf_op jit(solution)/shard_map/weights/ppermute | solution.py:384
  256.2 44.8 %collective-permute-start.30 = (bf16[1024,512]{1,0:T(8,128)(2,1)S(1)}, bf16[1024,512]{1,0:T(8,128)(2,1)}, u32[]{:S(2)}, u32[]{:S(2)}) collective-permute-start(bf16[1024,512]{1,0:T(8,128)(2,1)S(1)} %copy-done.145), channel_id=1, source_target_pairs={{0,2},{1,3},{2,4},{3,5},{4,6},{5,7},{6,0},{7,1},{8,10},{9,11},{10,... | collective-permute-start | bytes 3145736 | tf_op jit(solution)/shard_map/weights/ppermute | solution.py:396
  358.1 30.9 %collective-permute-start.38 = (bf16[256,2560]{1,0:T(8,128)(2,1)S(1)}, bf16[256,2560]{1,0:T(8,128)(2,1)S(1)}, u32[]{:S(2)}, u32[]{:S(2)}) collective-permute-start(bf16[256,2560]{1,0:T(8,128)(2,1)S(1)} %backward_layers.41), channel_id=1, source_target_pairs={{0,16},{8,24},{16,0},{24,8},{1,17},{9,25},{17,1},{25,9},{2,18},{10... | collective-permute-start | bytes 3932168 | tf_op jit(solution)/shard_map/backward_layers/ppermute | solution.py:388
  359.5 25.6 %collective-permute-start.37 = (bf16[256,2048]{1,0:T(8,128)(2,1)S(1)}, bf16[256,2048]{1,0:T(8,128)(2,1)S(1)}, u32[]{:S(2)}, u32[]{:S(2)}) collective-permute-start(bf16[256,2048]{1,0:T(8,128)(2,1)S(1)} %backward_layers.40), channel_id=1, source_target_pairs={{0,8},{8,0},{16,24},{24,16},{1,9},{9,1},{17,25},{25,17},{2,10},{10... | collective-permute-start | bytes 3145736 | tf_op jit(solution)/shard_map/backward_layers/ppermute | solution.py:384
  391.8 24.4 %collective-permute-start.40 = (bf16[512,1024]{1,0:T(8,128)(2,1)S(1)}, bf16[512,1024]{1,0:T(8,128)(2,1)S(1)}, u32[]{:S(2)}, u32[]{:S(2)}) collective-permute-start(bf16[512,1024]{1,0:T(8,128)(2,1)S(1)} %backward_layers.44), channel_id=1, source_target_pairs={{0,16},{8,24},{16,0},{24,8},{1,17},{9,25},{17,1},{25,9},{2,18},{10... | collective-permute-start | bytes 3145736 | tf_op jit(solution)/shard_map/backward_layers/ppermute | solution.py:388
  393.2 24.1 %collective-permute-start.41 = (bf16[256,2048]{1,0:T(8,128)(2,1)S(1)}, bf16[256,2048]{1,0:T(8,128)(2,1)S(1)}, u32[]{:S(2)}, u32[]{:S(2)}) collective-permute-start(bf16[256,2048]{1,0:T(8,128)(2,1)S(1)} %backward_layers.45), channel_id=1, source_target_pairs={{0,8},{8,0},{16,24},{24,16},{1,9},{9,1},{17,25},{25,17},{2,10},{10... | collective-permute-start | bytes 3145736 | tf_op jit(solution)/shard_map/backward_layers/ppermute | solution.py:384
  421.8 61.1 %reduce-scatter.10.cloned.1.call-start = ((), (), s32[]{:S(2)}) async-start(), calls=%async_computation.12 | async-start | bytes 1310720 | tf_op jit(solution)/shard_map/backward_layers/reduce_scatter | solution.py:1091
  423.5 25.6 %collective-permute-start.44 = (bf16[256,2048]{1,0:T(8,128)(2,1)S(1)}, bf16[256,2048]{1,0:T(8,128)(2,1)S(1)}, u32[]{:S(2)}, u32[]{:S(2)}) collective-permute-start(bf16[256,2048]{1,0:T(8,128)(2,1)S(1)} %backward_layers.51), channel_id=1, source_target_pairs={{0,16},{8,24},{16,0},{24,8},{1,17},{9,25},{17,1},{25,9},{2,18},{10... | collective-permute-start | bytes 3145736 | tf_op jit(solution)/shard_map/backward_layers/ppermute | solution.py:388
  424.9 14.0 %collective-permute-start.43 = (bf16[256,1024]{1,0:T(8,128)(2,1)S(1)}, bf16[256,1024]{1,0:T(8,128)(2,1)S(1)}, u32[]{:S(2)}, u32[]{:S(2)}) collective-permute-start(bf16[256,1024]{1,0:T(8,128)(2,1)S(1)} %backward_layers.50), channel_id=1, source_target_pairs={{0,8},{8,0},{16,24},{24,16},{1,9},{9,1},{17,25},{25,17},{2,10},{10... | collective-permute-start | bytes 1572872 | tf_op jit(solution)/shard_map/backward_layers/ppermute | solution.py:384
  453.2 4.5 collective-permute-start.45
  453.2 110.1 %reduce-scatter.12.cloned.1.call-start = ((), (), s32[]{:S(2)}) async-start(), calls=%async_computation.13 | async-start | bytes 1310720 | tf_op jit(solution)/shard_map/backward_layers/reduce_scatter | solution.py:1091
  453.3 26.6 %collective-permute-start.48 = (bf16[256,1536]{1,0:T(8,128)(2,1)}, bf16[256,1536]{1,0:T(8,128)(2,1)S(1)}, u32[]{:S(2)}, u32[]{:S(2)}) collective-permute-start(bf16[256,1536]{1,0:T(8,128)(2,1)} %copy-done.110), channel_id=1, source_target_pairs={{0,16},{8,24},{16,0},{24,8},{1,17},{9,25},{17,1},{25,9},{2,18},{10... | collective-permute-start | bytes 2359304 | tf_op jit(solution)/shard_map/backward_layers/ppermute | solution.py:388
  454.6 26.8 %collective-permute-start.47 = (bf16[256,1536]{1,0:T(8,128)(2,1)}, bf16[256,1536]{1,0:T(8,128)(2,1)}, u32[]{:S(2)}, u32[]{:S(2)}) collective-permute-start(bf16[256,1536]{1,0:T(8,128)(2,1)} %copy-done.109), channel_id=1, source_target_pairs={{0,8},{8,0},{16,24},{24,16},{1,9},{9,1},{17,25},{25,17},{2,10},{10... | collective-permute-start | bytes 2359304 | tf_op jit(solution)/shard_map/backward_layers/ppermute | solution.py:384
  454.6 25.2 %collective-permute-start.46 = (bf16[256,512]{1,0:T(8,128)(2,1)}, bf16[256,512]{1,0:T(8,128)(2,1)S(1)}, u32[]{:S(2)}, u32[]{:S(2)}) collective-permute-start(bf16[256,512]{1,0:T(8,128)(2,1)} %copy-done.121), channel_id=1, source_target_pairs={{0,16},{8,24},{16,0},{24,8},{1,17},{9,25},{17,1},{25,9},{2,18},{10... | collective-permute-start | bytes 786440 | tf_op jit(solution)/shard_map/backward_layers/ppermute | solution.py:388
  489.8 38.5 %collective-permute-start.52 = (bf16[256,2560]{1,0:T(8,128)(2,1)}, bf16[256,2560]{1,0:T(8,128)(2,1)S(1)}, u32[]{:S(2)}, u32[]{:S(2)}) collective-permute-start(bf16[256,2560]{1,0:T(8,128)(2,1)} %backward_layers.63), channel_id=1, source_target_pairs={{0,16},{8,24},{16,0},{24,8},{1,17},{9,25},{17,1},{25,9},{2,18},{10... | collective-permute-start | bytes 3932168 | tf_op jit(solution)/shard_map/backward_layers/ppermute | solution.py:388
  491.3 4.7 collective-permute-start.49
  491.3 37.0 %collective-permute-start.51 = (bf16[256,2048]{1,0:T(8,128)(2,1)}, bf16[256,2048]{1,0:T(8,128)(2,1)}, u32[]{:S(2)}, u32[]{:S(2)}) collective-permute-start(bf16[256,2048]{1,0:T(8,128)(2,1)} %backward_layers.62), channel_id=1, source_target_pairs={{0,8},{8,0},{16,24},{24,16},{1,9},{9,1},{17,25},{25,17},{2,10},{10... | collective-permute-start | bytes 3145736 | tf_op jit(solution)/shard_map/backward_layers/ppermute | solution.py:384
  492.8 93.9 %reduce-scatter.14.cloned.1.call-start = ((), (), s32[]{:S(2)}) async-start(), calls=%async_computation.14 | async-start | bytes 655360 | tf_op jit(solution)/shard_map/backward_layers/reduce_scatter | solution.py:1091
  492.8 35.5 %collective-permute-start.50 = (bf16[512,512]{1,0:T(8,128)(2,1)}, bf16[512,512]{1,0:T(8,128)(2,1)S(1)}, u32[]{:S(2)}, u32[]{:S(2)}) collective-permute-start(bf16[512,512]{1,0:T(8,128)(2,1)} %copy-done.111), channel_id=1, source_target_pairs={{0,8},{8,0},{16,24},{24,16},{1,9},{9,1},{17,25},{25,17},{2,10},{10... | collective-permute-start | bytes 1572872 | tf_op jit(solution)/shard_map/backward_layers/ppermute | solution.py:384
  534.8 28.5 %collective-permute-start.54 = (bf16[512,1024]{1,0:T(8,128)(2,1)}, bf16[512,1024]{1,0:T(8,128)(2,1)}, u32[]{:S(2)}, u32[]{:S(2)}) collective-permute-start(bf16[512,1024]{1,0:T(8,128)(2,1)} %backward_layers.67), channel_id=1, source_target_pairs={{0,16},{8,24},{16,0},{24,8},{1,17},{9,25},{17,1},{25,9},{2,18},{10... | collective-permute-start | bytes 3145736 | tf_op jit(solution)/shard_map/backward_layers/ppermute | solution.py:388
  535.3 28.0 %collective-permute-start.55 = (bf16[256,2048]{1,0:T(8,128)(2,1)}, bf16[256,2048]{1,0:T(8,128)(2,1)}, u32[]{:S(2)}, u32[]{:S(2)}) collective-permute-start(bf16[256,2048]{1,0:T(8,128)(2,1)} %backward_layers.68), channel_id=1, source_target_pairs={{0,8},{8,0},{16,24},{24,16},{1,9},{9,1},{17,25},{25,17},{2,10},{10... | collective-permute-start | bytes 3145736 | tf_op jit(solution)/shard_map/backward_layers/ppermute | solution.py:384
  536.9 85.8 %reduce-scatter.16.cloned.1.call-start = ((), (), s32[]{:S(2)}) async-start(), calls=%async_computation.15 | async-start | bytes 1310720 | tf_op jit(solution)/shard_map/backward_layers/reduce_scatter | solution.py:1091
  569.2 56.0 %reduce-scatter.18.cloned.1.call-start = ((), (), s32[]{:S(2)}) async-start(), calls=%async_computation.16 | async-start | bytes 1310720 | tf_op jit(solution)/shard_map/backward_layers/reduce_scatter | solution.py:1091
  573.3 25.7 %collective-permute-start.58 = (bf16[256,2048]{1,0:T(8,128)(2,1)}, bf16[256,2048]{1,0:T(8,128)(2,1)S(1)}, u32[]{:S(2)}, u32[]{:S(2)}) collective-permute-start(bf16[256,2048]{1,0:T(8,128)(2,1)} %backward_layers.74), channel_id=1, source_target_pairs={{0,16},{8,24},{16,0},{24,8},{1,17},{9,25},{17,1},{25,9},{2,18},{10... | collective-permute-start | bytes 3145736 | tf_op jit(solution)/shard_map/backward_layers/ppermute | solution.py:388
  574.7 14.2 %collective-permute-start.57 = (bf16[256,1024]{1,0:T(8,128)(2,1)}, bf16[256,1024]{1,0:T(8,128)(2,1)S(1)}, u32[]{:S(2)}, u32[]{:S(2)}) collective-permute-start(bf16[256,1024]{1,0:T(8,128)(2,1)} %backward_layers.73), channel_id=1, source_target_pairs={{0,8},{8,0},{16,24},{24,16},{1,9},{9,1},{17,25},{25,17},{2,10},{10... | collective-permute-start | bytes 1572872 | tf_op jit(solution)/shard_map/backward_layers/ppermute | solution.py:384
  603.2 19.4 %collective-permute-start.60 = (bf16[256,1536]{1,0:T(8,128)(2,1)}, bf16[256,1536]{1,0:T(8,128)(2,1)}, u32[]{:S(2)}, u32[]{:S(2)}) collective-permute-start(bf16[256,1536]{1,0:T(8,128)(2,1)} %embedding_back.10), channel_id=1, source_target_pairs={{0,8},{8,0},{16,24},{24,16},{1,9},{9,1},{17,25},{25,17},{2,10},{10... | collective-permute-start | bytes 2359304 | tf_op jit(solution)/shard_map/embedding_back/ppermute | solution.py:384
  603.7 10.6 %collective-permute-start.59 = (bf16[256,512]{1,0:T(8,128)(2,1)}, bf16[256,512]{1,0:T(8,128)(2,1)}, u32[]{:S(2)}, u32[]{:S(2)}) collective-permute-start(bf16[256,512]{1,0:T(8,128)(2,1)} %embedding_back.9), channel_id=1, source_target_pairs={{0,16},{8,24},{16,0},{24,8},{1,17},{9,25},{17,1},{25,9},{2,18},{10... | collective-permute-start | bytes 786440 | tf_op jit(solution)/shard_map/embedding_back/ppermute | solution.py:388
  629.3 20.1 %all-to-all-start.1 = ((bf16[32,32,256]{2,1,0:T(8,128)(2,1)}), bf16[32,32,256]{2,1,0:T(8,128)(2,1)}, u32[]{:S(2)}, u32[]{:S(2)}) async-start(bf16[32,32,256]{2,1,0:T(8,128)(2,1)} %embedding_back.8), calls=%async_computation.7 | async-start | bytes 1048576 | tf_op jit(solution)/shard_map/embedding_back/all_to_all | solution.py:1433
  632.7 32.8 %reduce-scatter.20.cloned.1.call-start = ((), (), s32[]{:S(2)}) async-start(), calls=%async_computation.17 | async-start | bytes 1310720 | tf_op jit(solution)/shard_map/embedding_back/reduce_scatter | solution.py:1091
  633.5 4.5 collective-permute-start.66
  634.8 5.2 collective-permute-start.63
  635.0 8.2 %collective-permute-start.64 = (bf16[32,2048]{1,0:T(8,128)(2,1)}, bf16[32,2048]{1,0:T(8,128)(2,1)}, u32[]{:S(2)}, u32[]{:S(2)}) collective-permute-start(bf16[32,2048]{1,0:T(8,128)(2,1)} %dynamic-slice_bitcast_fusion.1), channel_id=1, source_target_pairs={{0,1},{1,0},{2,3},{3,2},{4,5},{5,4},{6,7},{7,6},{8,9},{9,8},{10,11... | collective-permute-start | bytes 393224 | tf_op jit(solution)/shard_map/own_grads/ppermute | solution.py:392
  665.5 5.1 collective-permute-start.61
  673.6 4.8 collective-permute-start.62
  675.8 10.8 %all-to-all-start.2 = ((f32[32,8,128]{2,1,0:T(8,128)}), f32[32,8,128]{2,1,0:T(8,128)S(1)}, u32[]{:S(2)}, u32[]{:S(2)}) async-start(f32[32,8,128]{2,1,0:T(8,128)} %broadcast_in_dim.109), calls=%async_computation.9 | async-start | bytes 262144 | tf_op jit(solution)/shard_map/clip_and_update/all_to_all | solution.py:1487
  (183 other events, 1109.2 us)
Sparse Core Ops, SparseCore 0:
  19.9 190.2 all-gather.5
  213.5 93.2 all-gather.3
  421.9 29.3 reduce-scatter.7
  453.6 29.2 reduce-scatter.9
  492.9 26.5 reduce-scatter.11
  537.0 21.7 reduce-scatter.13
  569.3 27.1 reduce-scatter.15
  599.4 25.7 reduce-scatter.17
  636.5 28.2 reduce-scatter.19

commit v4 on v3

--- a/solution.py
+++ b/solution.py
@@ -960,7 +960,7 @@
     rates, decays = weight_rates(), [DECAY_RATE] * 8 + [0.0]
     count = len(weights)
 
-    steps = 8
+    steps = 4
 
     def split(item):
         return item.shape[-1] % (steps * 128) == 0
@@ -1414,7 +1414,7 @@
         d_joined = piece_dot_back(result[2], *bridge_mat, 128)
         d_joined, d_bridged_low = flow.turn(d_joined, result[2])
         d_joined, g_bridge = flow.add((d_joined,), (joined, d_bridged_low, spot, True))
-        d_joined = d_joined + swap_core(d_joined)
+        d_joined = d_joined + swap_core(d_joined.astype(LOW)).astype(WIDE)
         d_encoded = d_joined[:, :width]
         result, shares_zero, d_gain_one = tp_backward(
             d_encoded, d_encoded.astype(LOW), kept_zero, mats_zero, gain[0], gain[1], *parts

time: 713 us -> 712 us (level)
    ppermute x16, waiting for transfers between devices: 40.3 us -> 48.3 us  [swap_y(): return lax.ppermute(item, 'dp', [(i, i ^ 2) for i in range(4)])]
    unnamed x356 -> x342, local copies, waits for them, and re-layouts: 76.6 us -> 71.1 us
  transfers between devices with their start and end apart: 79 -> 79, of which waited for: 38 -> 38; matrix products, arithmetic and copies ran while one was open for 15% -> 14% of each run, Pallas kernels for 18% -> 19%
where the time goes in v4:
time: 712 us; the launch traced here: 709 us
  waiting for transfers between devices  257 us (36%)
  Pallas kernels  163 us (23%)
  local copies, waits for them, and re-layouts  135 us (19%)
  starting transfers between devices  79.6 us (11%)
  other arithmetic  50.9 us (7%)
  between operations  18.1 us (3%)
    ppermute x12, waiting for transfers between devices, shift_z(): lax.ppermute(item, 'fsdp', [(i, (i + 2 * hops) % 8) for i in range(8)])  111 us
    unnamed x342, local copies, waits for them, and re-layouts  71.1 us
    ppermute x14, waiting for transfers between devices, swap_x(): return lax.ppermute(item, 'dp', [(i, i ^ 1) for i in range(4)])  60.8 us
    ppermute x16, waiting for transfers between devices, swap_y(): return lax.ppermute(item, 'dp', [(i, i ^ 2) for i in range(4)])  48.3 us
    pallas_call x22, Pallas kernels, one_step(): pl.pallas_call(body, grid_spec=pltpu.PrefetchScalarGridSpec(num_scalar_pr...  39.3 us
    ppermute x12, starting transfers between devices, shift_z(): lax.ppermute(item, 'fsdp', [(i, (i + 2 * hops) % 8) for i in range(8)])  27.2 us
    pallas_call x18, Pallas kernels, outer_sum(): pl.pallas_call(body, grid_spec=pltpu.PrefetchScalarGridSpec(num_scalar_pr...  27.1 us
    pallas_call x9, Pallas kernels, piece_dot_back(): pl.pallas_call(body, grid_spec=pltpu.PrefetchScalarGridSpec(num_scalar_pr...  26.8 us
  transfers between devices with their start and end apart: 79, of which 38 were waited for; matrix products, arithmetic and copies ran while one was open for 14% of the time, Pallas kernels for 19%

profile of v4, /device:TPU:0, one launch (start us, length us, event | category | flops | bytes accessed | tf_op | source)
XLA Modules:
  0.0 708.6 jit_solution(6440201155884376242)
XLA Ops:
  11.7 3.3 dynamic-slice_reduce_fusion.1
  21.6 5.0 collective-permute-start.2
  29.4 3.2 collective-permute-done
  35.9 7.3 %collective-permute-done.3 = bf16[4,208,128]{2,1,0:T(8,128)(2,1)S(1)} collective-permute-done((bf16[4,208,128]{2,1,0:T(8,128)(2,1)S(1)}, bf16[4,208,128]{2,1,0:T(8,128)(2,1)S(1)}, u32[]{:S(2)}, u32[]{:S(2)}) %collective-permute-start.3) | collective-permute-done | bytes 213024 | tf_op jit(solution)/shard_map/features/ppermute | solution.py:384
  44.7 4.9 collective-permute-done.5
  56.1 7.6 %collective-permute-done.10 = bf16[256,512]{1,0:T(8,128)(2,1)S(1)} collective-permute-done((bf16[256,512]{1,0:T(8,128)(2,1)S(1)}, bf16[256,512]{1,0:T(8,128)(2,1)S(1)}, u32[]{:S(2)}, u32[]{:S(2)}) %collective-permute-start.10) | collective-permute-done | bytes 262176 | tf_op jit(solution)/shard_map/weights/ppermute | solution.py:396
  63.7 3.4 collective-permute-start.11
  67.9 6.4 copy.175
  74.2 6.5 reshape.312
  84.3 3.1 collective-permute-start.12
  98.7 4.1 concatenate.98
  112.7 10.8 %collective-permute-done.20 = bf16[256,512]{1,0:T(8,128)(2,1)} collective-permute-done((bf16[256,512]{1,0:T(8,128)(2,1)S(1)}, bf16[256,512]{1,0:T(8,128)(2,1)}, u32[]{:S(2)}, u32[]{:S(2)}) %collective-permute-start.20) | collective-permute-done | bytes 262176 | tf_op jit(solution)/shard_map/weights/ppermute | solution.py:396
  129.5 3.3 copy.177
  135.7 6.8 collective-permute-done.21
  142.6 3.3 collective-permute-start.22
  146.8 5.7 all-to-all-start
  153.9 5.5 collective-permute-done.22
  166.4 4.0 collective-permute-start.8
  172.6 2.6 collective-permute-start.26
  175.2 25.5 %collective-permute-done.23 = bf16[1024,512]{1,0:T(8,128)(2,1)} collective-permute-done((bf16[1024,512]{1,0:T(8,128)(2,1)S(1)}, bf16[1024,512]{1,0:T(8,128)(2,1)}, u32[]{:S(2)}, u32[]{:S(2)}) %collective-permute-start.23) | collective-permute-done | bytes 1048608 | tf_op jit(solution)/shard_map/weights/ppermute | solution.py:396
  200.7 6.5 collective-permute-start.24
  208.6 5.8 collective-permute-done.15
  219.1 6.4 forward_layers.17
  228.3 9.9 %collective-permute-done.24 = bf16[1024,512]{1,0:T(8,128)(2,1)S(1)} collective-permute-done((bf16[1024,512]{1,0:T(8,128)(2,1)}, bf16[1024,512]{1,0:T(8,128)(2,1)S(1)}, u32[]{:S(2)}, u32[]{:S(2)}) %collective-permute-start.24) | collective-permute-done | bytes 1048608 | tf_op jit(solution)/shard_map/weights/ppermute | solution.py:396
  241.3 3.5 forward_layers.20
  249.0 4.4 copy-done
  253.4 2.6 forward_layers.21
  259.2 41.8 %collective-permute-done.30 = bf16[1024,512]{1,0:T(8,128)(2,1)} collective-permute-done((bf16[1024,512]{1,0:T(8,128)(2,1)S(1)}, bf16[1024,512]{1,0:T(8,128)(2,1)}, u32[]{:S(2)}, u32[]{:S(2)}) %collective-permute-start.30) | collective-permute-done | bytes 1048608 | tf_op jit(solution)/shard_map/weights/ppermute | solution.py:396
  308.0 6.4 forward_layers.25
  316.2 4.0 copy-done.2
  325.4 3.5 forward_layers.28
  334.4 2.6 forward_layers.29
  348.9 4.2 backward_layers.38.grads_ref.right_ref
  353.3 3.5 backward_layers.39.mine_ref
  359.3 2.7 collective-permute-done.36.other_ref
  365.4 19.5 %collective-permute-done.37.far_left_ref.far_right_ref = bf16[256,2048]{1,0:T(8,128)(2,1)S(1)} collective-permute-done((bf16[256,2048]{1,0:T(8,128)(2,1)S(1)}, bf16[256,2048]{1,0:T(8,128)(2,1)S(1)}, u32[]{:S(2)}, u32[]{:S(2)}) %collective-permute-start.37) | collective-permute-done | bytes 1048608 | tf_op jit(solution)/shard_map/backward_layers/ppermute | solution.py:384
  384.8 4.2 collective-permute-done.38.far_left_ref.far_right_ref
  394.9 8.6 %backward_layers.46.grads_ref.right_ref = bf16[256,1536]{1,0:T(8,128)(2,1)S(1)} custom-call(f32[8]{0:T(128)S(1)} %multiply_power_fusion.slopes_ref, bf16[256,1536]{1,0:T(8,128)(2,1)S(1)} %copy-done.52, f32[256,512]{1,0:T(8,128)S(1)} %get-tuple-element.242.mine_ref, f32[256,512]{1,0:T(8,128)S(1)} %collective-permute-done.39.other_ref, ...), custom_call_target="tpu_custom_call" | custom-call | flops 1000 | bytes 1000 | tf_op jit(solution)/shard_map/backward_layers/pallas_call | solution.py:688
  408.0 3.8 backward_layers.47.mine_ref
  411.7 4.6 collective-permute-done.40
  418.5 3.2 add_convert_fusion.3
  430.3 4.1 backward_layers.52
  434.4 4.1 copy-done.3
  440.3 10.3 %collective-permute-done.44.far_left_ref.far_right_ref = bf16[256,2048]{1,0:T(8,128)(2,1)S(1)} collective-permute-done((bf16[256,2048]{1,0:T(8,128)(2,1)}, bf16[256,2048]{1,0:T(8,128)(2,1)S(1)}, u32[]{:S(2)}, u32[]{:S(2)}) %collective-permute-start.44) | collective-permute-done | bytes 1048608 | tf_op jit(solution)/shard_map/backward_layers/ppermute | solution.py:388
  458.1 4.2 backward_layers.57.grads_ref.right_ref
  466.9 4.5 backward_layers.58.mine_ref
  472.5 8.0 %collective-permute-done.46 = bf16[256,512]{1,0:T(8,128)(2,1)S(1)} collective-permute-done((bf16[256,512]{1,0:T(8,128)(2,1)S(1)}, bf16[256,512]{1,0:T(8,128)(2,1)S(1)}, u32[]{:S(2)}, u32[]{:S(2)}) %collective-permute-start.46) | collective-permute-done | bytes 262176 | tf_op jit(solution)/shard_map/backward_layers/ppermute | solution.py:388
  495.8 3.7 backward_layers.64
  502.4 24.5 %collective-permute-done.50 = bf16[512,512]{1,0:T(8,128)(2,1)S(1)} collective-permute-done((bf16[512,512]{1,0:T(8,128)(2,1)}, bf16[512,512]{1,0:T(8,128)(2,1)S(1)}, u32[]{:S(2)}, u32[]{:S(2)}) %collective-permute-start.50) | collective-permute-done | bytes 524320 | tf_op jit(solution)/shard_map/backward_layers/ppermute | solution.py:384
  527.0 2.9 backward_layers.67
  529.9 2.6 backward_layers.68
  540.6 8.6 %backward_layers.69.grads_ref.right_ref = bf16[256,1536]{1,0:T(8,128)(2,1)S(1)} custom-call(f32[8]{0:T(128)S(1)} %multiply_power_fusion.slopes_ref, bf16[256,1536]{1,0:T(8,128)(2,1)S(1)} %copy-done.54, f32[256,512]{1,0:T(8,128)S(1)} %copy-done.104, f32[256,512]{1,0:T(8,128)S(1)} %copy-done.108, f32[2,1,128]{2,1,0:T(1,128)S(1)} %constant_dynamic-slice_fusion.valid_ref), custom_call_target="tpu_custom_call" | custom-call | flops 1000 | bytes 1000 | tf_op jit(solution)/shard_map/backward_layers/pallas_call | solution.py:688
  557.3 2.8 backward_layers.70.mine_ref
  561.1 3.3 add_convert_fusion.1
  586.3 10.5 %collective-permute-done.58.far_left_ref.far_right_ref = bf16[256,2048]{1,0:T(8,128)(2,1)S(1)} collective-permute-done((bf16[256,2048]{1,0:T(8,128)(2,1)}, bf16[256,2048]{1,0:T(8,128)(2,1)S(1)}, u32[]{:S(2)}, u32[]{:S(2)}) %collective-permute-start.58) | collective-permute-done | bytes 1048608 | tf_op jit(solution)/shard_map/backward_layers/ppermute | solution.py:388
  604.4 3.9 copy.193.strided_ref
  612.9 7.4 %collective-permute-done.60 = bf16[256,1536]{1,0:T(8,128)(2,1)} collective-permute-done((bf16[256,1536]{1,0:T(8,128)(2,1)}, bf16[256,1536]{1,0:T(8,128)(2,1)}, u32[]{:S(2)}, u32[]{:S(2)}) %collective-permute-start.60) | collective-permute-done | bytes 786464 | tf_op jit(solution)/shard_map/embedding_back/ppermute | solution.py:384
  620.3 5.5 reduce-scatter.18.cloned.1.call-done.refs_0_
  629.9 3.4 all-to-all-start.1
  653.1 4.9 embedding_back.13
  659.5 6.6 embedding_back.14.refs_2_.refs_7_
  676.4 2.6 all-to-all-start.2
  681.2 6.0 all-to-all-done.2
  687.8 12.8 %clip_and_update.5 = (f32[8,128]{1,0:T(8,128)}, f32[32,256]{1,0:T(8,128)}, f32[32,256]{1,0:T(8,128)}, f32[32,256]{1,0:T(8,128)}, f32[31,32,64]{2,1,0:T(8,128)}, ...) custom-call(s32[17]{0:T(128)} %copy-done.110, ...), custom_call_target="tpu_custom_call" | custom-call | flops 1000 | bytes 1000 | tf_op jit(solution)/shard_map/clip_and_update/pallas_call | solution.py:1016
  (703 shorter events, 269.7 us)
Async XLA Ops:
  7.2 241.8 %all-gather.6.cloned.1.call-start = ((), (), s32[]{:S(2)}) async-start(), calls=%async_computation.18 | async-start | bytes 11141120 | tf_op jit(solution)/shard_map/weights/all_gather | solution.py:1315
  19.8 312.4 %all-gather.4.cloned.1.call-start = ((), (), s32[]{:S(2)}) async-start(), calls=%async_computation.10 | async-start | bytes 4456448 | tf_op jit(solution)/shard_map/weights/all_gather | solution.py:1315
  21.6 11.0 %collective-permute-start.2 = (bf16[208,128]{1,0:T(8,128)(2,1)S(1)}, bf16[208,128]{1,0:T(8,128)(2,1)S(1)}, u32[]{:S(2)}, u32[]{:S(2)}) collective-permute-start(bf16[208,128]{1,0:T(8,128)(2,1)S(1)} %concatenate.93), channel_id=1, source_target_pairs={{0,6},{1,7},{2,0},{3,1},{4,2},{5,3},{6,4},{7,5},{8,14},{9,15},{10,... | collective-permute-start | bytes 159752 | tf_op jit(solution)/shard_map/features/ppermute | solution.py:396
  26.6 6.0 collective-permute-start.1
  26.6 6.0 collective-permute-start
  27.6 54.6 %collective-permute-start.7 = (bf16[256,32]{0,1:T(8,128)(2,1)S(1)}, bf16[256,32]{0,1:T(8,128)(2,1)S(1)}, u32[]{:S(2)}, u32[]{:S(2)}) collective-permute-start(bf16[256,32]{0,1:T(8,128)(2,1)S(1)} %convert_element_type.216), channel_id=1, source_target_pairs={{0,1},{1,0},{2,3},{3,2},{4,5},{5,4},{6,7},{7,6},{8,9},{9,8},{10,11... | collective-permute-start | bytes 49160 | tf_op jit(solution)/shard_map/embedding/ppermute | solution.py:392
  32.7 12.0 %collective-permute-start.4 = (bf16[4,208,128]{2,1,0:T(8,128)(2,1)S(1)}, bf16[4,208,128]{2,1,0:T(8,128)(2,1)S(1)}, u32[]{:S(2)}, u32[]{:S(2)}) collective-permute-start(bf16[4,208,128]{2,1,0:T(8,128)(2,1)S(1)} %bitcast_dynamic-update-slice_fusion.4), channel_id=1, source_target_pairs={{0,16},{8,24},{16,0},{24,8},{1,17},{9,25},{17,1},{25,9},{2,18},{10... | collective-permute-start | bytes 638984 | tf_op jit(solution)/shard_map/features/ppermute | solution.py:388
  34.2 8.9 %collective-permute-start.3 = (bf16[4,208,128]{2,1,0:T(8,128)(2,1)S(1)}, bf16[4,208,128]{2,1,0:T(8,128)(2,1)S(1)}, u32[]{:S(2)}, u32[]{:S(2)}) collective-permute-start(bf16[4,208,128]{2,1,0:T(8,128)(2,1)S(1)} %bitcast_dynamic-update-slice_fusion.4), channel_id=1, source_target_pairs={{0,8},{8,0},{16,24},{24,16},{1,9},{9,1},{17,25},{25,17},{2,10},{10... | collective-permute-start | bytes 638984 | tf_op jit(solution)/shard_map/features/ppermute | solution.py:384
  43.2 6.5 collective-permute-start.5
  49.7 37.8 %collective-permute-start.6 = (bf16[16,208,128]{2,1,0:T(8,128)(2,1)S(1)}, bf16[16,208,128]{2,1,0:T(8,128)(2,1)}, u32[]{:S(2)}, u32[]{:S(2)}) collective-permute-start(bf16[16,208,128]{2,1,0:T(8,128)(2,1)S(1)} %bitcast.391), channel_id=1, source_target_pairs={{0,1},{1,0},{2,3},{3,2},{4,5},{5,4},{6,7},{7,6},{8,9},{9,8},{10,11... | collective-permute-start | bytes 2555912 | tf_op jit(solution)/shard_map/features/ppermute | solution.py:392
  51.4 12.3 %collective-permute-start.10 = (bf16[256,512]{1,0:T(8,128)(2,1)S(1)}, bf16[256,512]{1,0:T(8,128)(2,1)S(1)}, u32[]{:S(2)}, u32[]{:S(2)}) collective-permute-start(bf16[256,512]{1,0:T(8,128)(2,1)S(1)} %bitcast.411), channel_id=1, source_target_pairs={{0,2},{1,3},{2,4},{3,5},{4,6},{5,7},{6,0},{7,1},{8,10},{9,11},{10,... | collective-permute-start | bytes 786440 | tf_op jit(solution)/shard_map/weights/ppermute | solution.py:396
  55.5 26.9 %collective-permute-start.17 = (bf16[256,512]{1,0:T(8,128)(2,1)}, bf16[256,512]{1,0:T(8,128)(2,1)}, u32[]{:S(2)}, u32[]{:S(2)}) collective-permute-start(bf16[256,512]{1,0:T(8,128)(2,1)} %bitcast.77), channel_id=1, source_target_pairs={{0,8},{8,0},{16,24},{24,16},{1,9},{9,1},{17,25},{25,17},{2,10},{10... | collective-permute-start | bytes 786440 | tf_op jit(solution)/shard_map/weights/ppermute | solution.py:384
  63.7 20.6 %collective-permute-start.11 = (bf16[256,512]{1,0:T(8,128)(2,1)S(1)}, bf16[256,512]{1,0:T(8,128)(2,1)}, u32[]{:S(2)}, u32[]{:S(2)}) collective-permute-start(bf16[256,512]{1,0:T(8,128)(2,1)S(1)} %collective-permute-done.10), channel_id=1, source_target_pairs={{0,2},{1,3},{2,4},{3,5},{4,6},{5,7},{6,0},{7,1},{8,10},{9,11},{10,... | collective-permute-start | bytes 786440 | tf_op jit(solution)/shard_map/weights/ppermute | solution.py:396
  82.2 70.3 %collective-permute-start.18 = (bf16[256,512]{1,0:T(8,128)(2,1)}, bf16[256,512]{1,0:T(8,128)(2,1)}, u32[]{:S(2)}, u32[]{:S(2)}) collective-permute-start(bf16[256,512]{1,0:T(8,128)(2,1)} %bitcast.77), channel_id=1, source_target_pairs={{0,16},{8,24},{16,0},{24,8},{1,17},{9,25},{17,1},{25,9},{2,18},{10... | collective-permute-start | bytes 786440 | tf_op jit(solution)/shard_map/weights/ppermute | solution.py:388
  82.4 70.2 %collective-permute-start.19 = (bf16[256,512]{1,0:T(8,128)(2,1)}, bf16[256,512]{1,0:T(8,128)(2,1)}, u32[]{:S(2)}, u32[]{:S(2)}) collective-permute-start(bf16[256,512]{1,0:T(8,128)(2,1)} %collective-permute-done.17), channel_id=1, source_target_pairs={{0,16},{8,24},{16,0},{24,8},{1,17},{9,25},{17,1},{25,9},{2,18},{10... | collective-permute-start | bytes 786440 | tf_op jit(solution)/shard_map/weights/ppermute | solution.py:388
  84.3 21.9 %collective-permute-start.12 = (bf16[256,512]{1,0:T(8,128)(2,1)}, bf16[256,512]{1,0:T(8,128)(2,1)}, u32[]{:S(2)}, u32[]{:S(2)}) collective-permute-start(bf16[256,512]{1,0:T(8,128)(2,1)} %collective-permute-done.11), channel_id=1, source_target_pairs={{0,2},{1,3},{2,4},{3,5},{4,6},{5,7},{6,0},{7,1},{8,10},{9,11},{10,... | collective-permute-start | bytes 786440 | tf_op jit(solution)/shard_map/weights/ppermute | solution.py:396
  108.3 15.1 %collective-permute-start.20 = (bf16[256,512]{1,0:T(8,128)(2,1)S(1)}, bf16[256,512]{1,0:T(8,128)(2,1)}, u32[]{:S(2)}, u32[]{:S(2)}) collective-permute-start(bf16[256,512]{1,0:T(8,128)(2,1)S(1)} %bitcast.409), channel_id=1, source_target_pairs={{0,2},{1,3},{2,4},{3,5},{4,6},{5,7},{6,0},{7,1},{8,10},{9,11},{10,... | collective-permute-start | bytes 786440 | tf_op jit(solution)/shard_map/weights/ppermute | solution.py:396
  109.1 52.3 %collective-permute-start.14 = (bf16[1024,512]{1,0:T(8,128)(2,1)}, bf16[1024,512]{1,0:T(8,128)(2,1)}, u32[]{:S(2)}, u32[]{:S(2)}) collective-permute-start(bf16[1024,512]{1,0:T(8,128)(2,1)} %pad_maximum_fusion.6), channel_id=1, source_target_pairs={{0,16},{8,24},{16,0},{24,8},{1,17},{9,25},{17,1},{25,9},{2,18},{10... | collective-permute-start | bytes 3145736 | tf_op jit(solution)/shard_map/weights/ppermute | solution.py:388
  110.4 51.0 %collective-permute-start.13 = (bf16[1024,512]{1,0:T(8,128)(2,1)}, bf16[1024,512]{1,0:T(8,128)(2,1)}, u32[]{:S(2)}, u32[]{:S(2)}) collective-permute-start(bf16[1024,512]{1,0:T(8,128)(2,1)} %pad_maximum_fusion.6), channel_id=1, source_target_pairs={{0,8},{8,0},{16,24},{24,16},{1,9},{9,1},{17,25},{25,17},{2,10},{10... | collective-permute-start | bytes 3145736 | tf_op jit(solution)/shard_map/weights/ppermute | solution.py:384
  123.4 19.1 %collective-permute-start.21 = (bf16[256,512]{1,0:T(8,128)(2,1)}, bf16[256,512]{1,0:T(8,128)(2,1)}, u32[]{:S(2)}, u32[]{:S(2)}) collective-permute-start(bf16[256,512]{1,0:T(8,128)(2,1)} %collective-permute-done.20), channel_id=1, source_target_pairs={{0,2},{1,3},{2,4},{3,5},{4,6},{5,7},{6,0},{7,1},{8,10},{9,11},{10,... | collective-permute-start | bytes 786440 | tf_op jit(solution)/shard_map/weights/ppermute | solution.py:396
  142.6 16.8 %collective-permute-start.22 = (bf16[256,512]{1,0:T(8,128)(2,1)}, bf16[256,512]{1,0:T(8,128)(2,1)S(1)}, u32[]{:S(2)}, u32[]{:S(2)}) collective-permute-start(bf16[256,512]{1,0:T(8,128)(2,1)} %collective-permute-done.21), channel_id=1, source_target_pairs={{0,2},{1,3},{2,4},{3,5},{4,6},{5,7},{6,0},{7,1},{8,10},{9,11},{10,... | collective-permute-start | bytes 786440 | tf_op jit(solution)/shard_map/weights/ppermute | solution.py:396
  146.8 18.7 %all-to-all-start = ((bf16[32,16,256]{2,1,0:T(8,128)(2,1)}), bf16[32,16,256]{2,1,0:T(8,128)(2,1)S(1)}, u32[]{:S(2)}, u32[]{:S(2)}) async-start(bf16[32,16,256]{2,1,0:T(8,128)(2,1)} %bitcast.58), calls=%async_computation | async-start | bytes 524288 | tf_op jit(solution)/shard_map/embedding/all_to_all | solution.py:1357
  152.5 329.6 %reduce-scatter.8.cloned.1.call-start = ((), (), s32[]{:S(2)}) async-start(), calls=%async_computation.11 | async-start | bytes 1310720 | tf_op jit(solution)/shard_map/backward_layers/reduce_scatter | solution.py:1091
  161.4 45.8 %collective-permute-start.27 = (bf16[1024,512]{1,0:T(8,128)(2,1)}, bf16[1024,512]{1,0:T(8,128)(2,1)}, u32[]{:S(2)}, u32[]{:S(2)}) collective-permute-start(bf16[1024,512]{1,0:T(8,128)(2,1)} %pad_maximum_fusion.8), channel_id=1, source_target_pairs={{0,16},{8,24},{16,0},{24,8},{1,17},{9,25},{17,1},{25,9},{2,18},{10... | collective-permute-start | bytes 3145736 | tf_op jit(solution)/shard_map/weights/ppermute | solution.py:388
  162.7 38.0 %collective-permute-start.23 = (bf16[1024,512]{1,0:T(8,128)(2,1)S(1)}, bf16[1024,512]{1,0:T(8,128)(2,1)}, u32[]{:S(2)}, u32[]{:S(2)}) collective-permute-start(bf16[1024,512]{1,0:T(8,128)(2,1)S(1)} %pad_maximum_fusion.7), channel_id=1, source_target_pairs={{0,2},{1,3},{2,4},{3,5},{4,6},{5,7},{6,0},{7,1},{8,10},{9,11},{10,... | collective-permute-start | bytes 3145736 | tf_op jit(solution)/shard_map/weights/ppermute | solution.py:396
  162.7 51.6 %collective-permute-start.15 = (bf16[1024,512]{1,0:T(8,128)(2,1)}, bf16[1024,512]{1,0:T(8,128)(2,1)}, u32[]{:S(2)}, u32[]{:S(2)}) collective-permute-start(bf16[1024,512]{1,0:T(8,128)(2,1)} %collective-permute-done.13), channel_id=1, source_target_pairs={{0,16},{8,24},{16,0},{24,8},{1,17},{9,25},{17,1},{25,9},{2,18},{10... | collective-permute-start | bytes 3145736 | tf_op jit(solution)/shard_map/weights/ppermute | solution.py:388
  166.4 5.1 collective-permute-start.8
  172.6 65.6 %collective-permute-start.26 = (bf16[1024,512]{1,0:T(8,128)(2,1)}, bf16[1024,512]{1,0:T(8,128)(2,1)S(1)}, u32[]{:S(2)}, u32[]{:S(2)}) collective-permute-start(bf16[1024,512]{1,0:T(8,128)(2,1)} %pad_maximum_fusion.8), channel_id=1, source_target_pairs={{0,8},{8,0},{16,24},{24,16},{1,9},{9,1},{17,25},{25,17},{2,10},{10... | collective-permute-start | bytes 3145736 | tf_op jit(solution)/shard_map/weights/ppermute | solution.py:384
  200.7 37.4 %collective-permute-start.24 = (bf16[1024,512]{1,0:T(8,128)(2,1)}, bf16[1024,512]{1,0:T(8,128)(2,1)S(1)}, u32[]{:S(2)}, u32[]{:S(2)}) collective-permute-start(bf16[1024,512]{1,0:T(8,128)(2,1)} %collective-permute-done.23), channel_id=1, source_target_pairs={{0,2},{1,3},{2,4},{3,5},{4,6},{5,7},{6,0},{7,1},{8,10},{9,11},{10,... | collective-permute-start | bytes 3145736 | tf_op jit(solution)/shard_map/weights/ppermute | solution.py:396
  207.2 31.0 %collective-permute-start.28 = (bf16[1024,512]{1,0:T(8,128)(2,1)}, bf16[1024,512]{1,0:T(8,128)(2,1)S(1)}, u32[]{:S(2)}, u32[]{:S(2)}) collective-permute-start(bf16[1024,512]{1,0:T(8,128)(2,1)} %collective-permute-done.27), channel_id=1, source_target_pairs={{0,8},{8,0},{16,24},{24,16},{1,9},{9,1},{17,25},{25,17},{2,10},{10... | collective-permute-start | bytes 3145736 | tf_op jit(solution)/shard_map/weights/ppermute | solution.py:384
  256.3 44.8 %collective-permute-start.30 = (bf16[1024,512]{1,0:T(8,128)(2,1)S(1)}, bf16[1024,512]{1,0:T(8,128)(2,1)}, u32[]{:S(2)}, u32[]{:S(2)}) collective-permute-start(bf16[1024,512]{1,0:T(8,128)(2,1)S(1)} %copy-done.135), channel_id=1, source_target_pairs={{0,2},{1,3},{2,4},{3,5},{4,6},{5,7},{6,0},{7,1},{8,10},{9,11},{10,... | collective-permute-start | bytes 3145736 | tf_op jit(solution)/shard_map/weights/ppermute | solution.py:396
  358.1 30.9 %collective-permute-start.38 = (bf16[256,2560]{1,0:T(8,128)(2,1)S(1)}, bf16[256,2560]{1,0:T(8,128)(2,1)S(1)}, u32[]{:S(2)}, u32[]{:S(2)}) collective-permute-start(bf16[256,2560]{1,0:T(8,128)(2,1)S(1)} %backward_layers.41), channel_id=1, source_target_pairs={{0,16},{8,24},{16,0},{24,8},{1,17},{9,25},{17,1},{25,9},{2,18},{10... | collective-permute-start | bytes 3932168 | tf_op jit(solution)/shard_map/backward_layers/ppermute | solution.py:388
  359.3 25.6 %collective-permute-start.37 = (bf16[256,2048]{1,0:T(8,128)(2,1)S(1)}, bf16[256,2048]{1,0:T(8,128)(2,1)S(1)}, u32[]{:S(2)}, u32[]{:S(2)}) collective-permute-start(bf16[256,2048]{1,0:T(8,128)(2,1)S(1)} %backward_layers.40), channel_id=1, source_target_pairs={{0,8},{8,0},{16,24},{24,16},{1,9},{9,1},{17,25},{25,17},{2,10},{10... | collective-permute-start | bytes 3145736 | tf_op jit(solution)/shard_map/backward_layers/ppermute | solution.py:384
  391.8 24.4 %collective-permute-start.40 = (bf16[512,1024]{1,0:T(8,128)(2,1)S(1)}, bf16[512,1024]{1,0:T(8,128)(2,1)S(1)}, u32[]{:S(2)}, u32[]{:S(2)}) collective-permute-start(bf16[512,1024]{1,0:T(8,128)(2,1)S(1)} %backward_layers.44), channel_id=1, source_target_pairs={{0,16},{8,24},{16,0},{24,8},{1,17},{9,25},{17,1},{25,9},{2,18},{10... | collective-permute-start | bytes 3145736 | tf_op jit(solution)/shard_map/backward_layers/ppermute | solution.py:388
  393.0 24.1 %collective-permute-start.41 = (bf16[256,2048]{1,0:T(8,128)(2,1)S(1)}, bf16[256,2048]{1,0:T(8,128)(2,1)S(1)}, u32[]{:S(2)}, u32[]{:S(2)}) collective-permute-start(bf16[256,2048]{1,0:T(8,128)(2,1)S(1)} %backward_layers.45), channel_id=1, source_target_pairs={{0,8},{8,0},{16,24},{24,16},{1,9},{9,1},{17,25},{25,17},{2,10},{10... | collective-permute-start | bytes 3145736 | tf_op jit(solution)/shard_map/backward_layers/ppermute | solution.py:384
  421.8 60.3 %reduce-scatter.10.cloned.1.call-start = ((), (), s32[]{:S(2)}) async-start(), calls=%async_computation.12 | async-start | bytes 1310720 | tf_op jit(solution)/shard_map/backward_layers/reduce_scatter | solution.py:1091
  424.8 25.8 %collective-permute-start.44 = (bf16[256,2048]{1,0:T(8,128)(2,1)}, bf16[256,2048]{1,0:T(8,128)(2,1)S(1)}, u32[]{:S(2)}, u32[]{:S(2)}) collective-permute-start(bf16[256,2048]{1,0:T(8,128)(2,1)} %backward_layers.51), channel_id=1, source_target_pairs={{0,16},{8,24},{16,0},{24,8},{1,17},{9,25},{17,1},{25,9},{2,18},{10... | collective-permute-start | bytes 3145736 | tf_op jit(solution)/shard_map/backward_layers/ppermute | solution.py:388
  425.9 14.4 %collective-permute-start.43 = (bf16[256,1024]{1,0:T(8,128)(2,1)}, bf16[256,1024]{1,0:T(8,128)(2,1)}, u32[]{:S(2)}, u32[]{:S(2)}) collective-permute-start(bf16[256,1024]{1,0:T(8,128)(2,1)} %backward_layers.50), channel_id=1, source_target_pairs={{0,8},{8,0},{16,24},{24,16},{1,9},{9,1},{17,25},{25,17},{2,10},{10... | collective-permute-start | bytes 1572872 | tf_op jit(solution)/shard_map/backward_layers/ppermute | solution.py:384
  425.9 135.2 %reduce-scatter.12.cloned.1.call-start = ((), (), s32[]{:S(2)}) async-start(), calls=%async_computation.13 | async-start | bytes 1310720 | tf_op jit(solution)/shard_map/backward_layers/reduce_scatter | solution.py:1091
  454.9 25.6 %collective-permute-start.48 = (bf16[256,1536]{1,0:T(8,128)(2,1)S(1)}, bf16[256,1536]{1,0:T(8,128)(2,1)S(1)}, u32[]{:S(2)}, u32[]{:S(2)}) collective-permute-start(bf16[256,1536]{1,0:T(8,128)(2,1)S(1)} %backward_layers.56), channel_id=1, source_target_pairs={{0,16},{8,24},{16,0},{24,8},{1,17},{9,25},{17,1},{25,9},{2,18},{10... | collective-permute-start | bytes 2359304 | tf_op jit(solution)/shard_map/backward_layers/ppermute | solution.py:388
  456.0 26.0 %collective-permute-start.47 = (bf16[256,1536]{1,0:T(8,128)(2,1)S(1)}, bf16[256,1536]{1,0:T(8,128)(2,1)}, u32[]{:S(2)}, u32[]{:S(2)}) collective-permute-start(bf16[256,1536]{1,0:T(8,128)(2,1)S(1)} %backward_layers.55), channel_id=1, source_target_pairs={{0,8},{8,0},{16,24},{24,16},{1,9},{9,1},{17,25},{25,17},{2,10},{10... | collective-permute-start | bytes 2359304 | tf_op jit(solution)/shard_map/backward_layers/ppermute | solution.py:384
  456.0 24.4 %collective-permute-start.46 = (bf16[256,512]{1,0:T(8,128)(2,1)S(1)}, bf16[256,512]{1,0:T(8,128)(2,1)S(1)}, u32[]{:S(2)}, u32[]{:S(2)}) collective-permute-start(bf16[256,512]{1,0:T(8,128)(2,1)S(1)} %backward_layers.54), channel_id=1, source_target_pairs={{0,16},{8,24},{16,0},{24,8},{1,17},{9,25},{17,1},{25,9},{2,18},{10... | collective-permute-start | bytes 786440 | tf_op jit(solution)/shard_map/backward_layers/ppermute | solution.py:388
  488.9 38.1 %collective-permute-start.52 = (bf16[256,2560]{1,0:T(8,128)(2,1)}, bf16[256,2560]{1,0:T(8,128)(2,1)S(1)}, u32[]{:S(2)}, u32[]{:S(2)}) collective-permute-start(bf16[256,2560]{1,0:T(8,128)(2,1)} %backward_layers.63), channel_id=1, source_target_pairs={{0,16},{8,24},{16,0},{24,8},{1,17},{9,25},{17,1},{25,9},{2,18},{10... | collective-permute-start | bytes 3932168 | tf_op jit(solution)/shard_map/backward_layers/ppermute | solution.py:388
  490.0 4.7 collective-permute-start.49
  490.0 37.0 %collective-permute-start.51 = (bf16[256,2048]{1,0:T(8,128)(2,1)}, bf16[256,2048]{1,0:T(8,128)(2,1)}, u32[]{:S(2)}, u32[]{:S(2)}) collective-permute-start(bf16[256,2048]{1,0:T(8,128)(2,1)} %backward_layers.62), channel_id=1, source_target_pairs={{0,8},{8,0},{16,24},{24,16},{1,9},{9,1},{17,25},{25,17},{2,10},{10... | collective-permute-start | bytes 3145736 | tf_op jit(solution)/shard_map/backward_layers/ppermute | solution.py:384
  490.0 95.3 %reduce-scatter.14.cloned.1.call-start = ((), (), s32[]{:S(2)}) async-start(), calls=%async_computation.14 | async-start | bytes 655360 | tf_op jit(solution)/shard_map/backward_layers/reduce_scatter | solution.py:1091
  490.1 36.9 %collective-permute-start.50 = (bf16[512,512]{1,0:T(8,128)(2,1)}, bf16[512,512]{1,0:T(8,128)(2,1)S(1)}, u32[]{:S(2)}, u32[]{:S(2)}) collective-permute-start(bf16[512,512]{1,0:T(8,128)(2,1)} %copy-done.102), channel_id=1, source_target_pairs={{0,8},{8,0},{16,24},{24,16},{1,9},{9,1},{17,25},{25,17},{2,10},{10... | collective-permute-start | bytes 1572872 | tf_op jit(solution)/shard_map/backward_layers/ppermute | solution.py:384
  533.5 27.6 %collective-permute-start.54 = (bf16[512,1024]{1,0:T(8,128)(2,1)}, bf16[512,1024]{1,0:T(8,128)(2,1)}, u32[]{:S(2)}, u32[]{:S(2)}) collective-permute-start(bf16[512,1024]{1,0:T(8,128)(2,1)} %backward_layers.67), channel_id=1, source_target_pairs={{0,16},{8,24},{16,0},{24,8},{1,17},{9,25},{17,1},{25,9},{2,18},{10... | collective-permute-start | bytes 3145736 | tf_op jit(solution)/shard_map/backward_layers/ppermute | solution.py:388
  534.4 26.7 %collective-permute-start.55 = (bf16[256,2048]{1,0:T(8,128)(2,1)}, bf16[256,2048]{1,0:T(8,128)(2,1)}, u32[]{:S(2)}, u32[]{:S(2)}) collective-permute-start(bf16[256,2048]{1,0:T(8,128)(2,1)} %backward_layers.68), channel_id=1, source_target_pairs={{0,8},{8,0},{16,24},{24,16},{1,9},{9,1},{17,25},{25,17},{2,10},{10... | collective-permute-start | bytes 3145736 | tf_op jit(solution)/shard_map/backward_layers/ppermute | solution.py:384
  534.8 85.5 %reduce-scatter.16.cloned.1.call-start = ((), (), s32[]{:S(2)}) async-start(), calls=%async_computation.15 | async-start | bytes 1310720 | tf_op jit(solution)/shard_map/backward_layers/reduce_scatter | solution.py:1091
  566.9 58.8 %reduce-scatter.18.cloned.1.call-start = ((), (), s32[]{:S(2)}) async-start(), calls=%async_computation.16 | async-start | bytes 1310720 | tf_op jit(solution)/shard_map/backward_layers/reduce_scatter | solution.py:1091
  571.0 5.2 collective-permute-start.56
  571.2 25.6 %collective-permute-start.58 = (bf16[256,2048]{1,0:T(8,128)(2,1)}, bf16[256,2048]{1,0:T(8,128)(2,1)S(1)}, u32[]{:S(2)}, u32[]{:S(2)}) collective-permute-start(bf16[256,2048]{1,0:T(8,128)(2,1)} %backward_layers.74), channel_id=1, source_target_pairs={{0,16},{8,24},{16,0},{24,8},{1,17},{9,25},{17,1},{25,9},{2,18},{10... | collective-permute-start | bytes 3145736 | tf_op jit(solution)/shard_map/backward_layers/ppermute | solution.py:388
  572.3 14.1 %collective-permute-start.57 = (bf16[256,1024]{1,0:T(8,128)(2,1)}, bf16[256,1024]{1,0:T(8,128)(2,1)S(1)}, u32[]{:S(2)}, u32[]{:S(2)}) collective-permute-start(bf16[256,1024]{1,0:T(8,128)(2,1)} %backward_layers.73), channel_id=1, source_target_pairs={{0,8},{8,0},{16,24},{24,16},{1,9},{9,1},{17,25},{25,17},{2,10},{10... | collective-permute-start | bytes 1572872 | tf_op jit(solution)/shard_map/backward_layers/ppermute | solution.py:384
  601.0 19.3 %collective-permute-start.60 = (bf16[256,1536]{1,0:T(8,128)(2,1)}, bf16[256,1536]{1,0:T(8,128)(2,1)}, u32[]{:S(2)}, u32[]{:S(2)}) collective-permute-start(bf16[256,1536]{1,0:T(8,128)(2,1)} %embedding_back.10), channel_id=1, source_target_pairs={{0,8},{8,0},{16,24},{24,16},{1,9},{9,1},{17,25},{25,17},{2,10},{10... | collective-permute-start | bytes 2359304 | tf_op jit(solution)/shard_map/embedding_back/ppermute | solution.py:384
  602.7 10.2 %collective-permute-start.59 = (bf16[256,512]{1,0:T(8,128)(2,1)}, bf16[256,512]{1,0:T(8,128)(2,1)}, u32[]{:S(2)}, u32[]{:S(2)}) collective-permute-start(bf16[256,512]{1,0:T(8,128)(2,1)} %embedding_back.9), channel_id=1, source_target_pairs={{0,16},{8,24},{16,0},{24,8},{1,17},{9,25},{17,1},{25,9},{2,18},{10... | collective-permute-start | bytes 786440 | tf_op jit(solution)/shard_map/embedding_back/ppermute | solution.py:388
  629.9 20.1 %all-to-all-start.1 = ((bf16[32,32,256]{2,1,0:T(8,128)(2,1)}), bf16[32,32,256]{2,1,0:T(8,128)(2,1)}, u32[]{:S(2)}, u32[]{:S(2)}) async-start(bf16[32,32,256]{2,1,0:T(8,128)(2,1)} %embedding_back.8), calls=%async_computation.7 | async-start | bytes 1048576 | tf_op jit(solution)/shard_map/embedding_back/all_to_all | solution.py:1433
  633.3 32.8 %reduce-scatter.20.cloned.1.call-start = ((), (), s32[]{:S(2)}) async-start(), calls=%async_computation.17 | async-start | bytes 1310720 | tf_op jit(solution)/shard_map/embedding_back/reduce_scatter | solution.py:1091
  634.0 4.5 collective-permute-start.66
  635.4 5.2 collective-permute-start.63
  635.6 8.2 %collective-permute-start.64 = (bf16[32,2048]{1,0:T(8,128)(2,1)}, bf16[32,2048]{1,0:T(8,128)(2,1)}, u32[]{:S(2)}, u32[]{:S(2)}) collective-permute-start(bf16[32,2048]{1,0:T(8,128)(2,1)} %dynamic-slice_bitcast_fusion.1), channel_id=1, source_target_pairs={{0,1},{1,0},{2,3},{3,2},{4,5},{5,4},{6,7},{7,6},{8,9},{9,8},{10,11... | collective-permute-start | bytes 393224 | tf_op jit(solution)/shard_map/own_grads/ppermute | solution.py:392
  666.1 5.1 collective-permute-start.61
  674.2 4.8 collective-permute-start.62
  676.4 10.8 %all-to-all-start.2 = ((f32[32,8,128]{2,1,0:T(8,128)}), f32[32,8,128]{2,1,0:T(8,128)S(1)}, u32[]{:S(2)}, u32[]{:S(2)}) async-start(f32[32,8,128]{2,1,0:T(8,128)} %broadcast_in_dim.109), calls=%async_computation.9 | async-start | bytes 262144 | tf_op jit(solution)/shard_map/clip_and_update/all_to_all | solution.py:1487
  (176 other events, 1098.8 us)
Sparse Core Ops, SparseCore 0:
  19.9 190.2 all-gather.5
  213.5 93.2 all-gather.3
  421.9 29.4 reduce-scatter.7
  453.6 25.7 reduce-scatter.9
  490.1 29.9 reduce-scatter.11
  534.9 24.4 reduce-scatter.13
  567.1 29.9 reduce-scatter.15
  599.9 25.7 reduce-scatter.17
  637.1 28.2 reduce-scatter.19
